TPU v7x, 32 devices: a whole 2x2x4 slice. The times are simulated.
32 devices in a mesh: cuts: 4 (over y, x), layer: 8 (over z, core).
Axes of the slice: x: 2, y: 2, z: 4, core: 2. Of those that a mesh axis runs over, the one named last changes fastest.
Arguments:
- vectors: float32 [4, 64, 16, 1024], P('cuts', None, 'layer'), may hold values from -40 to 40
- diag_blocks: bfloat16 [16, 1024, 1024], P('layer'), may hold values from -1 to 1, as said below
- couplings: bfloat16 [16, 1024, 1024], P('layer'), may hold values from -0.09375 to 0.09375
- bounds: int32 [4, 2], P('cuts'), may hold values from -128 to 160, as said below
Outputs:
- filtered: float32 [4, 64, 16, 1024], P('cuts', None, 'layer')
Inputs may be any that keep to these rules, and one draw needn't show every extreme that they name: `bounds`: column 0 holds each slice's lower end, which is -128 at slice 0 and to at most -81; column 1 holds its upper end, from 128 to 160. `diag_blocks`: each block is symmetric.
All inputs are finite; a program needn't handle non-finite values.
Results may differ from a plain program's by a relative error of at most 0.012.
Values may be sent and summed in bfloat16 or wider, within the bound.
No kernel may reach another device: no remote copies, remote signals or barrier semaphores. Data moves between devices by JAX's collectives and lax.ppermute only.
A program may use at most 64 MiB of HBM per device.

v0:
```python
import functools

import jax
import jax.numpy as jnp
from jax import lax
from jax.experimental import pallas as pl
from jax.experimental.pallas import tpu as pltpu
from jax.sharding import PartitionSpec as P

EDGE = 16
DEG = 4
ROWS = 8
HIGHEST = lax.Precision.HIGHEST
BF16 = jnp.bfloat16
F32 = jnp.float32
VMEM = pl.BlockSpec(memory_space=pltpu.VMEM)
HBM = pl.BlockSpec(memory_space=pltpu.HBM)


def exchanged(block, first):
    count, slices = lax.axis_size("layer"), lax.axis_size("cuts")
    route = []
    for cut in range(slices):
        for i in range(count):
            j = i + 1 if (i - first) % 2 == 0 else i - 1
            to = (cut, j) if 0 <= j < count else (cut ^ 1 if cut ^ 1 < slices else cut, i)
            route.append((cut * count + i, to[0] * count + to[1]))
    return lax.ppermute(block, ("cuts", "layer"), route)


def far_away(block):
    return pltpu.with_memory_space_constraint(block, pltpu.HBM)


def rotated(block, distance):
    size = lax.axis_size("cuts")
    return lax.ppermute(block, "cuts", [(i, (i + distance) % size) for i in range(size)])


def partial_sums(block):
    size = lax.axis_size("layer")
    if size & (size - 1) or size == 1:
        return [lax.psum(block, "layer")]
    block = block + lax.ppermute(block, "layer", [(i, i ^ 1) for i in range(size)])
    reach = 2
    while size // reach > 4:
        block = block + lax.ppermute(block, "layer", [(i, i ^ reach) for i in range(size)])
        reach *= 2
    return [block] + [
        lax.ppermute(block, "layer", [(i, i ^ step) for i in range(size)])
        for step in range(reach, size, reach)
    ]


def product(block, matrix):
    return jnp.dot(block, matrix, preferred_element_type=F32)


def product_t(block, matrix, precision=None):
    return lax.dot_general(
        block, matrix, (((1,), (1,)), ((), ())), precision=precision, preferred_element_type=F32
    )


def exact(first, second):
    return jnp.dot(first, second, precision=HIGHEST, preferred_element_type=F32)


def inverse_factor(gram):
    size = gram.shape[0]
    row = lax.broadcasted_iota(jnp.int32, (size, size), 0)
    column = lax.broadcasted_iota(jnp.int32, (size, size), 1)
    work = jnp.concatenate([jnp.where(row == column, 1.0, 0.0), gram], 1)
    finished = []
    for start in range(0, size, ROWS):
        left = size - start
        at = lax.broadcasted_iota(jnp.int32, (left, 2 * size), 0)
        lines = [
            jnp.broadcast_to(work[:, size + start + c : size + start + c + 1], (left, 2 * size))
            for c in range(ROWS)
        ]
        pivots = jnp.zeros((ROWS, 2 * size), F32)
        for c in range(ROWS):
            pivot = lines[c][c : c + 1]
            factor = jnp.where(at > c, lines[c] * (1.0 / pivot), 0.0)
            pivots = jnp.where(at[:ROWS] == c, pivot, pivots)
            work = work - factor * work[c : c + 1]
            for d in range(c + 1, ROWS):
                lines[d] = lines[d] - factor * lines[d][c : c + 1]
        finished.append(lax.rsqrt(pivots) * work[:ROWS])
        work = work[ROWS:]
    return jnp.concatenate(finished, 0)[:, :size]


def position(axis):
    return lax.axis_index(axis).astype(jnp.int32)


def send_outer(odd, rounded_ref, last_ref, send_ref):
    @pl.when(odd == 0)
    def _():
        send_ref[...] = rounded_ref[...]

    @pl.when(odd == 1)
    def _():
        send_ref[...] = product(rounded_ref[...], last_ref[...]).astype(BF16)


def send_inner(odd, rounded_ref, last_ref, send_ref):
    end = rounded_ref.shape[0] - 1

    @pl.when(odd == 1)
    def _():
        send_ref[...] = rounded_ref[end]

    @pl.when(odd == 0)
    def _():
        send_ref[...] = product(rounded_ref[end], last_ref[...]).astype(BF16)


def enter_kernel(
    far_bounds_ref, vectors_ref, couplings_ref,
    outer_ref, rest_ref, outer16_ref, rest16_ref, inner_send_ref, outer_send_ref, last_ref, mids_ref, rows_ref,
    bounds_ref, block_ref, sems,
):
    layers = vectors_ref.shape[1]
    copies = [
        pltpu.make_async_copy(vectors_ref, block_ref, sems.at[0]),
        pltpu.make_async_copy(couplings_ref.at[layers - 1], last_ref, sems.at[1]),
        pltpu.make_async_copy(couplings_ref.at[pl.ds(0, layers - 1)], mids_ref, sems.at[2]),
        pltpu.make_async_copy(far_bounds_ref, bounds_ref, sems.at[3]),
    ]
    for copy in copies:
        copy.start()
    odd = position("layer") % 2
    copies[0].wait()
    for parity in (0, 1):

        @pl.when(odd == parity)
        def _():
            order = range(layers)[:: -1 if parity else 1]
            outer_ref[...] = block_ref[:, order[0], :]
            for i, l in enumerate(order[1:]):
                rest_ref[i] = block_ref[:, l, :]

    outer16_ref[...] = outer_ref[...].astype(BF16)
    rest16_ref[...] = rest_ref[...].astype(BF16)
    copies[1].wait()
    send_outer(odd, outer16_ref, last_ref, outer_send_ref)
    send_inner(odd, rest16_ref, last_ref, inner_send_ref)
    copies[3].wait()
    width = rows_ref.shape[1]
    low, high = bounds_ref[0, 0].astype(F32), bounds_ref[0, 1].astype(F32)
    half = jnp.full((1, width), (high - low) * (1.0 / 128.0), F32)
    rows_ref[0:1] = jnp.full((1, width), (low + high) * (1.0 / 128.0), F32)
    rows_ref[1:2] = 1.0 / half
    rows_ref[2:3] = 2.0 / half
    copies[2].wait()


def interior_kernel(
    layers, load, first_step, final, rows_ref, outer16_ref, rest16_ref, arrived_ref, diag_ref, last_ref, mids_ref, *refs,
):
    *refs, sum_ref = refs
    if load:
        (outer_ref, rest_ref, outer_before_ref, rest_before_ref, *outs, last_t_ref, mids_t_ref) = refs
        last_t_ref[...] = jnp.transpose(last_ref[...])
        for i in range(layers - 1):
            mids_t_ref[i] = jnp.transpose(mids_ref[i])
    else:
        (last_t_ref, mids_t_ref, outer_ref, rest_ref, outer_before_ref, rest_before_ref, *outs) = refs
    base_ref, next_ref, next16_ref, last_out_ref = outs
    centre, scale = rows_ref[0:1], rows_ref[1:2] if first_step else rows_ref[2:3]
    odd = position("layer") % 2

    def rounded(place):
        return rest16_ref[place - 1] if place else outer16_ref[...]

    def add(block, straight, link):
        @pl.when(odd == straight)
        def _():
            sum_ref[...] += product(block, mids_ref[link])

        @pl.when(odd != straight)
        def _():
            sum_ref[...] += product(block, mids_t_ref[link])

    for place in range(layers)[::-1]:
        sum_ref[...] = product(rounded(place), diag_ref[place + odd * (layers - 1 - 2 * place)])
        if place < layers - 1:
            add(rounded(place + 1), 1, place + odd * (layers - 2 - 2 * place))
        if place > 0:
            add(rounded(place - 1), 0, place - 1 + odd * (layers - 2 * place))
        if place == layers - 1:

            @pl.when(odd == 0)
            def _():
                sum_ref[...] += product(arrived_ref[...], last_t_ref[...])

            @pl.when(odd == 1)
            def _():
                sum_ref[...] += arrived_ref[...].astype(F32)

        if place:
            term = (sum_ref[...] - centre * rest_ref[place - 1]) * scale
            term = term if first_step else term - rest_before_ref[place - 1]
            next_ref[place - 1] = term
            next16_ref[place - 1] = term.astype(BF16)
        else:
            term = (sum_ref[...] - centre * outer_ref[...]) * scale
            base_ref[...] = term if first_step else term - outer_before_ref[...]
    if final:
        last_out_ref[...] = sum(
            product_t(next_ref[i], next_ref[i], HIGHEST) for i in range(layers - 1)
        )
    else:
        send_inner(odd, next16_ref, last_ref, last_out_ref)


def finish(count, first_step, rows_ref, base_ref, arrived_ref, last_t_ref, store):
    scale = rows_ref[1:2] if first_step else rows_ref[2:3]
    at = position("layer")
    odd = at % 2

    @pl.when((odd == 0) & (at > 0))
    def _():
        store(base_ref[...] + arrived_ref[...].astype(F32) * scale)

    @pl.when((odd == 1) & (at < count - 1))
    def _():
        store(base_ref[...] + product(arrived_ref[...], last_t_ref[...]) * scale)

    @pl.when((at == 0) | ((odd == 1) & (at == count - 1)))
    def _():
        store(base_ref[...])


def step_kernel(
    count, first_step, rows_ref, base_ref, arrived_ref, last_ref, last_t_ref, next_ref, next16_ref, send_ref
):
    def store(block):
        next_ref[...] = block
        next16_ref[...] = block.astype(BF16)

    finish(count, first_step, rows_ref, base_ref, arrived_ref, last_t_ref, store)
    send_outer(position("layer") % 2, next16_ref, last_ref, send_ref)


def last_kernel(
    count, rows_ref, base_ref, arrived_ref, last_t_ref, rest16_ref, rest_gram_ref,
    next_ref, next16_ref, low_ref, gram_ref,
):
    def store(block):
        next_ref[...] = block
        next16_ref[...] = block.astype(BF16)

    finish(count, False, rows_ref, base_ref, arrived_ref, last_t_ref, store)
    edge = low_ref.shape[1]
    low_ref[0] = next16_ref[:edge]
    for i in range(low_ref.shape[0] - 1):
        low_ref[i + 1] = rest16_ref[i, :edge]
    gram_ref[...] = rest_gram_ref[...] + product_t(next_ref[...], next_ref[...], HIGHEST)


def normal_kernel(parts, length, *refs):
    grams, (filtered_ref, last_ref, inverse_ref, outer_ref, outer16_ref, send_ref) = refs[:parts], refs[parts:]
    inverse_ref[...] = inverse_factor(sum(ref[...] for ref in grams) * (1.0 / length))
    outer_ref[...] = exact(inverse_ref[...], filtered_ref[...])
    outer16_ref[...] = outer_ref[...].astype(BF16)
    send_outer(position("layer") % 2, outer16_ref, last_ref, send_ref)


def normal_rest_kernel(inverse_ref, filtered_ref, last_ref, rest_ref, rest16_ref, send_ref):
    for i in range(rest_ref.shape[0]):
        rest_ref[i] = exact(inverse_ref[...], filtered_ref[i])
    rest16_ref[...] = rest_ref[...].astype(BF16)
    send_inner(position("layer") % 2, rest16_ref, last_ref, send_ref)


def cross_kernel(gram_ref, outer16_ref, rest16_ref, above_ref, out_ref):
    size, edge = gram_ref.shape[0], above_ref.shape[1]
    rest = range(rest16_ref.shape[0])
    out_ref[:, :size] = gram_ref[...]
    out_ref[:, size : size + edge] = product_t(outer16_ref[...], above_ref[0]) + sum(
        product_t(rest16_ref[i], above_ref[i + 1]) for i in rest
    )
    out_ref[:edge, size + edge :] = sum(
        product_t(above_ref[l], above_ref[l]) for l in range(above_ref.shape[0])
    )
    out_ref[edge:, size + edge :] = jnp.zeros((size - edge, edge), F32)


def factor_kernel(parts, length, slices, *refs):
    grams, (outer_ref, rest_ref, inverse_ref, weights_ref, up_ref) = refs[:parts], refs[parts:]
    size, edge = outer_ref.shape[0], up_ref.shape[1]
    total = sum(ref[...] for ref in grams) * (1.0 / length)
    has_above = (position("cuts") < slices - 1).astype(F32)
    row = lax.broadcasted_iota(jnp.int32, (edge, edge), 0)
    column = lax.broadcasted_iota(jnp.int32, (edge, edge), 1)
    identity = jnp.where(row == column, 1.0, 0.0)
    above_gram = total[:edge, size + edge :] * has_above + identity * (1.0 - has_above)
    own = inverse_factor(total[:, :size])
    above = inverse_factor(above_gram)
    inverse_ref[...] = own
    high = own[size - edge :]
    correlation = product_t(exact(high, total[:, size : size + edge]), above, HIGHEST) * has_above
    weights_ref[...] = exact(correlation, above)
    up = exact(correlation.T, high)
    up_ref[0] = exact(up, outer_ref[...]).astype(BF16)
    for i in range(rest_ref.shape[0]):
        up_ref[i + 1] = exact(up, rest_ref[i]).astype(BF16)


def final_kernel(slices, inverse_ref, weights_ref, outer_ref, rest_ref, above_ref, below_ref, out_ref):
    size, edge = outer_ref.shape[0], above_ref.shape[1]
    layers = above_ref.shape[0]
    has_below = (position("cuts") > 0).astype(F32)
    blocks = []
    for i in range(layers):
        block = exact(inverse_ref[...], rest_ref[i - 1] if i else outer_ref[...])
        high = block[size - edge :] - exact(weights_ref[...], above_ref[i].astype(F32))
        low = block[:edge] - below_ref[i].astype(F32) * has_below
        blocks.append(jnp.concatenate([low, block[edge : size - edge], high], 0))
    for parity in (0, 1):

        @pl.when(position("layer") % 2 == parity)
        def _():
            for i, l in enumerate(range(layers)[:: -1 if parity else 1]):
                out_ref[:, l, :] = blocks[i]


def per_device(vectors, diag_blocks, couplings, bounds):
    vectors = vectors[0]
    count_vec, layers, width = vectors.shape
    count, slices = lax.axis_size("layer"), lax.axis_size("cuts")
    length_all = count * layers * width

    def array(dtype, *shape):
        return jax.ShapeDtypeStruct(shape, dtype)

    outer32, outer16 = array(F32, count_vec, width), array(BF16, count_vec, width)
    rest32, rest16 = array(F32, layers - 1, count_vec, width), array(BF16, layers - 1, count_vec, width)
    square = array(F32, count_vec, count_vec)
    matrix = array(BF16, width, width)
    matrices = array(BF16, layers - 1, width, width)
    edges = array(BF16, layers, EDGE, width)
    one = 2 * count_vec * width * width

    def call(kernel, outs, *operands, far=(), scratch_shapes=(), flops=one):
        moved = sum(x.size * x.dtype.itemsize for x in operands)
        return pl.pallas_call(
            kernel,
            out_shape=outs,
            in_specs=[HBM if i in far else VMEM for i in range(len(operands))],
            out_specs=jax.tree.map(lambda _: VMEM, outs),
            scratch_shapes=list(scratch_shapes),
            compiler_params=pltpu.CompilerParams(vmem_limit_bytes=32 * 2**20),
            cost_estimate=pl.CostEstimate(flops=flops, bytes_accessed=moved, transcendentals=0),
        )(*operands)

    outer, rest, outer_r, rest_r, inner_send, outer_send, last, mids, rows = call(
        enter_kernel,
        (outer32, rest32, outer16, rest16, outer16, outer16, matrix, matrices, array(F32, 8, width)),
        *map(far_away, (bounds, vectors, couplings)), far=(0, 1, 2),
        scratch_shapes=[
            pltpu.SMEM(bounds.shape, jnp.int32),
            pltpu.VMEM(vectors.shape, F32),
            pltpu.SemaphoreType.DMA((4,)),
        ],
    )

    def filter_block(outer, rest, outer_r, rest_r, inner_send, outer_send, turned):
        outer_before, rest_before = outer, rest
        for step in range(DEG):
            final = step == DEG - 1
            outer_in = exchanged(outer_send, 1)
            inner_in = exchanged(inner_send, 0)
            load = not turned
            outs = (outer32, rest32, rest16, square if final else outer16)
            base, rest_next, rest_r, extra, *made = call(
                functools.partial(interior_kernel, layers, load, step == 0, final),
                outs + ((matrix, matrices) if load else ()),
                rows, outer_r, rest_r, inner_in, diag_blocks, last, mids, *turned,
                outer, rest, outer_before, rest_before,
                scratch_shapes=[pltpu.VMEM((count_vec, width), F32)],
                flops=(3 * layers - 1) * one,
            )
            turned = turned or made
            if final:
                outer_next, outer_r, low, gram = call(
                    functools.partial(last_kernel, count),
                    (outer32, outer16, edges, square),
                    rows, base, outer_in, turned[0], rest_r, extra,
                )
                return outer_next, rest_next, outer_r, rest_r, low, gram, turned
            inner_send = extra
            outer_next, outer_r, outer_send = call(
                functools.partial(step_kernel, count, step == 0),
                (outer32, outer16, outer16),
                rows, base, outer_in, last, turned[0],
            )
            outer_before, rest_before, outer, rest = outer, rest, outer_next, rest_next

    outer, rest, _, _, _, gram, turned = filter_block(
        outer, rest, outer_r, rest_r, inner_send, outer_send, []
    )
    grams = partial_sums(gram)
    inverse, outer, outer_r, outer_send = call(
        functools.partial(normal_kernel, len(grams), length_all),
        (square, outer32, outer16, outer16), *grams, outer, last,
    )
    rest, rest_r, inner_send = call(
        normal_rest_kernel, (rest32, rest16, outer16), inverse, rest, last
    )
    outer, rest, outer_r, rest_r, low, gram, _ = filter_block(
        outer, rest, outer_r, rest_r, inner_send, outer_send, turned
    )
    above = rotated(low, -1)
    cross = call(
        cross_kernel, array(F32, count_vec, count_vec + 2 * EDGE), gram, outer_r, rest_r, above
    )
    grams = partial_sums(cross)
    inverse, weights, up = call(
        functools.partial(factor_kernel, len(grams), length_all, slices),
        (square, array(F32, EDGE, EDGE), edges), *grams, outer, rest,
    )
    below = rotated(up, 1)
    result = call(
        functools.partial(final_kernel, slices),
        array(F32, count_vec, layers, width), inverse, weights, outer, rest, above, below,
    )
    return result[None]


def solution(mesh):
    in_specs = (
        P("cuts", None, "layer", None),
        P("layer", None, None),
        P("layer", None, None),
        P("cuts", None),
    )
    out_specs = P("cuts", None, "layer", None)
    return jax.shard_map(
        per_device, mesh=mesh, in_specs=in_specs, out_specs=out_specs, check_vma=False
    )
```

profile of v0, /device:TPU:0, one launch (start us, length us, event | category | flops | bytes accessed | tf_op | source)
XLA Modules:
  0.0 82.7 jit_solution(5117830780256189654)
XLA Ops:
  0.0 2.6 %shard_map.46 = (f32[64,1024]{1,0:T(8,128)S(1)}, f32[1,64,1024]{2,1,0:T(8,128)S(1)}, bf16[64,1024]{1,0:T(8,128)(2,1)S(1)}, bf16[1,64,1024]{2,1,0:T(8,128)(2,1)S(...) custom-call(s32[1,2]{1,0:T(1,128)} %far_bounds_ref.1, ...), custom_call_target="tpu_custom_call" | custom-call | flops 134217728 | bytes 4718600 | tf_op jit(solution)/shard_map/pallas_call | solution.py:351
  2.6 0.5 collective-permute-start
  3.1 2.6 %collective-permute-start.1 = (bf16[64,1024]{1,0:T(8,128)(2,1)S(1)}, bf16[64,1024]{1,0:T(8,128)(2,1)S(1)}, u32[]{:S(2)}, u32[]{:S(2)}) collective-permute-start(bf16[64,1024]{1,0:T(8,128)(2,1)S(1)} %get-tuple-element.91), channel_id=1, source_target_pairs={{0,8},{1,2},{2,1},{3,4},{4,3},{5,6},{6,5},{7,15},{8,0},{9,10},{10,... | collective-permute-start | bytes 393224 | tf_op jit(solution)/shard_map/ppermute | solution.py:28
  5.7 0.0 collective-permute-done.arrived_ref
  5.7 3.7 %shard_map.47 = (f32[64,1024]{1,0:T(8,128)S(1)}, f32[1,64,1024]{2,1,0:T(8,128)S(1)}, bf16[1,64,1024]{2,1,0:T(8,128)(2,1)S(1)}, bf16[64,1024]{1,0:T(8,128)(2,1)S(...) custom-call(f32[8,1024]{1,0:T(8,128)S(1)} %get-tuple-element.82.rows_ref, ...), custom_call_target="tpu_custom_call" | custom-call | flops 671088640 | bytes 9863168 | tf_op jit(solution)/shard_map/pallas_call | solution.py:351
  9.4 0.1 collective-permute-start.2
  9.5 0.1 shard_map.48
  9.6 1.3 %collective-permute-start.3 = (bf16[64,1024]{1,0:T(8,128)(2,1)S(1)}, bf16[64,1024]{1,0:T(8,128)(2,1)S(1)}, u32[]{:S(2)}, u32[]{:S(2)}) collective-permute-start(bf16[64,1024]{1,0:T(8,128)(2,1)S(1)} %get-tuple-element.100), channel_id=1, source_target_pairs={{0,8},{1,2},{2,1},{3,4},{4,3},{5,6},{6,5},{7,15},{8,0},{9,10},{10,... | collective-permute-start | bytes 393224 | tf_op jit(solution)/shard_map/ppermute | solution.py:28
  10.9 2.9 %shard_map.49 = (f32[64,1024]{1,0:T(8,128)S(1)}, f32[1,64,1024]{2,1,0:T(8,128)S(1)}, bf16[1,64,1024]{2,1,0:T(8,128)(2,1)S(1)}, bf16[64,1024]{1,0:T(8,128)(2,1)S(1)}) custom-call(f32[8,1024]{1,0:T(8,128)S(1)} %get-tuple-element.82.rows_ref, bf16[64,1024]{1,0:T(8,128)(2,1)S(1)} %get-tuple-element.93.outer16_ref, ...), custom_call_target="tpu_custom_call" | custom-call | flops 671088640 | bytes 14057472 | tf_op jit(solution)/shard_map/pallas_call | solution.py:351
  13.9 0.1 collective-permute-start.4
  13.9 0.7 collective-permute-done.3.arrived_ref
  14.7 1.3 %collective-permute-start.5 = (bf16[64,1024]{1,0:T(8,128)(2,1)S(1)}, bf16[64,1024]{1,0:T(8,128)(2,1)S(1)}, u32[]{:S(2)}, u32[]{:S(2)}) collective-permute-start(bf16[64,1024]{1,0:T(8,128)(2,1)S(1)} %get-tuple-element.107), channel_id=1, source_target_pairs={{0,8},{1,2},{2,1},{3,4},{4,3},{5,6},{6,5},{7,15},{8,0},{9,10},{10,... | collective-permute-start | bytes 393224 | tf_op jit(solution)/shard_map/ppermute | solution.py:28
  16.0 2.9 %shard_map.51 = (f32[64,1024]{1,0:T(8,128)S(1)}, f32[1,64,1024]{2,1,0:T(8,128)S(1)}, bf16[1,64,1024]{2,1,0:T(8,128)(2,1)S(1)}, bf16[64,1024]{1,0:T(8,128)(2,1)S(1)}) custom-call(f32[8,1024]{1,0:T(8,128)S(1)} %get-tuple-element.82.rows_ref, bf16[64,1024]{1,0:T(8,128)(2,1)S(1)} %get-tuple-element.101.outer16_ref, ...), custom_call_target="tpu_custom_call" | custom-call | flops 671088640 | bytes 14057472 | tf_op jit(solution)/shard_map/pallas_call | solution.py:351
  18.9 0.1 collective-permute-start.6
  19.0 0.7 collective-permute-done.5.arrived_ref
  19.7 1.3 %collective-permute-start.7 = (bf16[64,1024]{1,0:T(8,128)(2,1)S(1)}, bf16[64,1024]{1,0:T(8,128)(2,1)S(1)}, u32[]{:S(2)}, u32[]{:S(2)}) collective-permute-start(bf16[64,1024]{1,0:T(8,128)(2,1)S(1)} %get-tuple-element.114), channel_id=1, source_target_pairs={{0,8},{1,2},{2,1},{3,4},{4,3},{5,6},{6,5},{7,15},{8,0},{9,10},{10,... | collective-permute-start | bytes 393224 | tf_op jit(solution)/shard_map/ppermute | solution.py:28
  21.1 0.0 collective-permute-done.6.arrived_ref
  21.1 3.0 %shard_map.53 = (f32[64,1024]{1,0:T(8,128)S(1)}, f32[1,64,1024]{2,1,0:T(8,128)S(1)}, bf16[1,64,1024]{2,1,0:T(8,128)(2,1)S(1)}, f32[64,64]{1,0:T(8,128)S(1)}) custom-call(f32[8,1024]{1,0:T(8,128)S(1)} %get-tuple-element.82.rows_ref, bf16[64,1024]{1,0:T(8,128)(2,1)S(1)} %get-tuple-element.108.outer16_ref, ...), custom_call_target="tpu_custom_call" | custom-call | flops 671088640 | bytes 14057472 | tf_op jit(solution)/shard_map/pallas_call | solution.py:351
  24.1 0.7 collective-permute-done.7.arrived_ref
  24.8 0.9 %shard_map.54 = (f32[64,1024]{1,0:T(8,128)S(1)}, bf16[64,1024]{1,0:T(8,128)(2,1)}, bf16[2,16,1024]{2,1,0:T(8,128)(2,1)}, f32[64,64]{1,0:T(8,128)S(1)}) custom-call(f32[8,1024]{1,0:T(8,128)S(1)} %get-tuple-element.82.rows_ref, f32[64,1024]{1,0:T(8,128)S(1)} %get-tuple-element.113.base_ref, bf16[64,1024]{1,0:T(8,128)(2,1)S(1)} %collective-permute-done.7.arrived_ref, ...), custom_call_target="tpu_custom_call" | custom-call | flops 134217728 | bytes 2670592 | tf_op jit(solution)/shard_map/pallas_call | solution.py:351
  25.7 2.0 %collective-permute-start.8 = (f32[64,64]{1,0:T(8,128)S(1)}, f32[64,64]{1,0:T(8,128)S(1)}, u32[]{:S(2)}, u32[]{:S(2)}) collective-permute-start(f32[64,64]{1,0:T(8,128)S(1)} %get-tuple-element.117), channel_id=1, source_target_pairs={{0,1},{1,0},{2,3},{3,2},{4,5},{5,4},{6,7},{7,6},{8,9},{9,8},{10,11... | collective-permute-start | bytes 49160 | tf_op jit(solution)/shard_map/ppermute | solution.py:44
  27.7 0.9 %collective-permute-done.8 = f32[64,64]{1,0:T(8,128)S(1)} collective-permute-done((f32[64,64]{1,0:T(8,128)S(1)}, f32[64,64]{1,0:T(8,128)S(1)}, u32[]{:S(2)}, u32[]{:S(2)}) %collective-permute-start.8) | collective-permute-done | bytes 16416 | tf_op jit(solution)/shard_map/ppermute | solution.py:44
  28.6 2.0 %collective-permute-start.11 = (f32[64,64]{1,0:T(8,128)S(1)}, f32[64,64]{1,0:T(8,128)S(1)}, u32[]{:S(2)}, u32[]{:S(2)}) collective-permute-start(f32[64,64]{1,0:T(8,128)S(1)} %add.6.refs_0_), channel_id=1, source_target_pairs={{0,6},{1,7},{2,4},{3,5},{4,2},{5,3},{6,0},{7,1},{8,14},{9,15},{10,... | collective-permute-start | bytes 49160 | tf_op jit(solution)/shard_map/ppermute | solution.py:50
  30.6 0.8 collective-permute-start.10
  31.4 1.6 %collective-permute-start.9 = (f32[64,64]{1,0:T(8,128)S(1)}, f32[64,64]{1,0:T(8,128)S(1)}, u32[]{:S(2)}, u32[]{:S(2)}) collective-permute-start(f32[64,64]{1,0:T(8,128)S(1)} %add.6.refs_0_), channel_id=1, source_target_pairs={{0,2},{1,3},{2,0},{3,1},{4,6},{5,7},{6,4},{7,5},{8,10},{9,11},{10,... | collective-permute-start | bytes 49160 | tf_op jit(solution)/shard_map/ppermute | solution.py:50
  33.0 1.5 %collective-permute-done.11.refs_3_ = f32[64,64]{1,0:T(8,128)S(1)} collective-permute-done((f32[64,64]{1,0:T(8,128)S(1)}, f32[64,64]{1,0:T(8,128)S(1)}, u32[]{:S(2)}, u32[]{:S(2)}) %collective-permute-start.11) | collective-permute-done | bytes 16416 | tf_op jit(solution)/shard_map/ppermute | solution.py:50
  34.4 1.0 %collective-permute-done.10.refs_2_ = f32[64,64]{1,0:T(8,128)S(1)} collective-permute-done((f32[64,64]{1,0:T(8,128)S(1)}, f32[64,64]{1,0:T(8,128)S(1)}, u32[]{:S(2)}, u32[]{:S(2)}) %collective-permute-start.10) | collective-permute-done | bytes 16416 | tf_op jit(solution)/shard_map/ppermute | solution.py:50
  35.4 0.3 collective-permute-done.9.refs_1_
  35.7 2.1 %shard_map.55 = (f32[64,64]{1,0:T(8,128)S(1)}, f32[64,1024]{1,0:T(8,128)S(1)}, bf16[64,1024]{1,0:T(8,128)(2,1)S(1)}, bf16[64,1024]{1,0:T(8,128)(2,1)S(1)}) custom-call(f32[64,64]{1,0:T(8,128)S(1)} %add.6.refs_0_, f32[64,64]{1,0:T(8,128)S(1)} %collective-permute-done.9.refs_1_, f32[64,64]{1,0:T(8,128)S(1)} %collective-permute-done.10.refs_2_, ...), custom_call_target="tpu_custom_call" | custom-call | flops 134217728 | bytes 2424832 | tf_op jit(solution)/shard_map/pallas_call | solution.py:351
  37.8 0.8 %shard_map.56 = (f32[1,64,1024]{2,1,0:T(8,128)S(1)}, bf16[1,64,1024]{2,1,0:T(8,128)(2,1)S(1)}, bf16[64,1024]{1,0:T(8,128)(2,1)S(1)}) custom-call(f32[64,64]{1,0:T(8,128)S(1)} %get-tuple-element.120.inverse_ref, f32[1,64,1024]{2,1,0:T(8,128)S(1)} %get-tuple-element.121.filtered_ref, bf16[1024,1024]{1,0:T(8,128)(2,1)S(1)} %get-tuple-element.86.last_ref.refs_5_), custom_call_target="tpu_custom_call" | custom-call | flops 134217728 | bytes 2375680 | tf_op jit(solution)/shard_map/pallas_call | solution.py:351
  38.7 0.1 collective-permute-start.12
  38.8 1.5 %collective-permute-start.13 = (bf16[64,1024]{1,0:T(8,128)(2,1)S(1)}, bf16[64,1024]{1,0:T(8,128)(2,1)S(1)}, u32[]{:S(2)}, u32[]{:S(2)}) collective-permute-start(bf16[64,1024]{1,0:T(8,128)(2,1)S(1)} %get-tuple-element.127), channel_id=1, source_target_pairs={{0,8},{1,2},{2,1},{3,4},{4,3},{5,6},{6,5},{7,15},{8,0},{9,10},{10,... | collective-permute-start | bytes 393224 | tf_op jit(solution)/shard_map/ppermute | solution.py:28
  40.3 0.0 collective-permute-done.12.arrived_ref
  40.3 2.9 %shard_map.57 = (f32[64,1024]{1,0:T(8,128)S(1)}, f32[1,64,1024]{2,1,0:T(8,128)S(1)}, bf16[1,64,1024]{2,1,0:T(8,128)(2,1)S(1)}, bf16[64,1024]{1,0:T(8,128)(2,1)S(1)}) custom-call(f32[8,1024]{1,0:T(8,128)S(1)} %get-tuple-element.82.rows_ref, bf16[64,1024]{1,0:T(8,128)(2,1)S(1)} %get-tuple-element.119.outer16_ref, ...), custom_call_target="tpu_custom_call" | custom-call | flops 671088640 | bytes 14057472 | tf_op jit(solution)/shard_map/pallas_call | solution.py:351
  43.2 0.1 collective-permute-start.14
  43.3 0.5 collective-permute-done.13.arrived_ref
  43.8 1.5 %collective-permute-start.15 = (bf16[64,1024]{1,0:T(8,128)(2,1)S(1)}, bf16[64,1024]{1,0:T(8,128)(2,1)S(1)}, u32[]{:S(2)}, u32[]{:S(2)}) collective-permute-start(bf16[64,1024]{1,0:T(8,128)(2,1)S(1)} %get-tuple-element.134), channel_id=1, source_target_pairs={{0,8},{1,2},{2,1},{3,4},{4,3},{5,6},{6,5},{7,15},{8,0},{9,10},{10,... | collective-permute-start | bytes 393224 | tf_op jit(solution)/shard_map/ppermute | solution.py:28
  45.4 2.9 %shard_map.59 = (f32[64,1024]{1,0:T(8,128)S(1)}, f32[1,64,1024]{2,1,0:T(8,128)S(1)}, bf16[1,64,1024]{2,1,0:T(8,128)(2,1)S(1)}, bf16[64,1024]{1,0:T(8,128)(2,1)S(1)}) custom-call(f32[8,1024]{1,0:T(8,128)S(1)} %get-tuple-element.82.rows_ref, bf16[64,1024]{1,0:T(8,128)(2,1)S(1)} %get-tuple-element.128.outer16_ref, ...), custom_call_target="tpu_custom_call" | custom-call | flops 671088640 | bytes 14057472 | tf_op jit(solution)/shard_map/pallas_call | solution.py:351
  48.3 0.1 collective-permute-start.16
  48.4 0.5 collective-permute-done.15.arrived_ref
  48.9 1.5 %collective-permute-start.17 = (bf16[64,1024]{1,0:T(8,128)(2,1)S(1)}, bf16[64,1024]{1,0:T(8,128)(2,1)S(1)}, u32[]{:S(2)}, u32[]{:S(2)}) collective-permute-start(bf16[64,1024]{1,0:T(8,128)(2,1)S(1)} %get-tuple-element.141), channel_id=1, source_target_pairs={{0,8},{1,2},{2,1},{3,4},{4,3},{5,6},{6,5},{7,15},{8,0},{9,10},{10,... | collective-permute-start | bytes 393224 | tf_op jit(solution)/shard_map/ppermute | solution.py:28
  50.5 0.0 collective-permute-done.16.arrived_ref
  50.5 3.2 %shard_map.61 = (f32[64,1024]{1,0:T(8,128)S(1)}, f32[1,64,1024]{2,1,0:T(8,128)S(1)}, bf16[1,64,1024]{2,1,0:T(8,128)(2,1)S(1)}, bf16[64,1024]{1,0:T(8,128)(2,1)S(1)}) custom-call(f32[8,1024]{1,0:T(8,128)S(1)} %get-tuple-element.82.rows_ref, bf16[64,1024]{1,0:T(8,128)(2,1)S(1)} %get-tuple-element.135.outer16_ref, ...), custom_call_target="tpu_custom_call" | custom-call | flops 671088640 | bytes 14057472 | tf_op jit(solution)/shard_map/pallas_call | solution.py:351
  53.6 0.1 collective-permute-start.18
  53.7 0.3 collective-permute-done.17.arrived_ref
  54.0 1.5 %collective-permute-start.19 = (bf16[64,1024]{1,0:T(8,128)(2,1)S(1)}, bf16[64,1024]{1,0:T(8,128)(2,1)S(1)}, u32[]{:S(2)}, u32[]{:S(2)}) collective-permute-start(bf16[64,1024]{1,0:T(8,128)(2,1)S(1)} %get-tuple-element.148), channel_id=1, source_target_pairs={{0,8},{1,2},{2,1},{3,4},{4,3},{5,6},{6,5},{7,15},{8,0},{9,10},{10,... | collective-permute-start | bytes 393224 | tf_op jit(solution)/shard_map/ppermute | solution.py:28
  55.5 2.8 %shard_map.63 = (f32[64,1024]{1,0:T(8,128)S(1)}, f32[1,64,1024]{2,1,0:T(8,128)S(1)}, bf16[1,64,1024]{2,1,0:T(8,128)(2,1)S(1)}, f32[64,64]{1,0:T(8,128)S(1)}) custom-call(f32[8,1024]{1,0:T(8,128)S(1)} %get-tuple-element.82.rows_ref, bf16[64,1024]{1,0:T(8,128)(2,1)S(1)} %get-tuple-element.142.outer16_ref, ...), custom_call_target="tpu_custom_call" | custom-call | flops 671088640 | bytes 14057472 | tf_op jit(solution)/shard_map/pallas_call | solution.py:351
  58.4 0.7 collective-permute-done.19.arrived_ref
  59.0 0.4 shard_map.64
  59.4 2.5 %collective-permute-start.20 = (bf16[2,16,1024]{2,1,0:T(8,128)(2,1)S(1)}, bf16[2,16,1024]{2,1,0:T(8,128)(2,1)S(1)}, u32[]{:S(2)}, u32[]{:S(2)}) collective-permute-start(bf16[2,16,1024]{2,1,0:T(8,128)(2,1)S(1)} %get-tuple-element.153), channel_id=1, source_target_pairs={{0,24},{8,0},{16,8},{24,16},{1,25},{9,1},{17,9},{25,17},{2,26},{10... | collective-permute-start | bytes 196616 | tf_op jit(solution)/shard_map/ppermute | solution.py:37
  61.9 1.9 %collective-permute-done.20.above_ref = bf16[2,16,1024]{2,1,0:T(8,128)(2,1)S(1)} collective-permute-done((bf16[2,16,1024]{2,1,0:T(8,128)(2,1)S(1)}, bf16[2,16,1024]{2,1,0:T(8,128)(2,1)S(1)}, u32[]{:S(2)}, u32[]{:S(2)}) %collective-permute-start.20) | collective-permute-done | bytes 65568 | tf_op jit(solution)/shard_map/ppermute | solution.py:37
  63.8 0.3 shard_map.65
  64.1 0.9 %collective-permute-start.21 = (f32[64,96]{1,0:T(8,128)S(1)}, f32[64,96]{1,0:T(8,128)S(1)}, u32[]{:S(2)}, u32[]{:S(2)}) collective-permute-start(f32[64,96]{1,0:T(8,128)S(1)} %shard_map.65), channel_id=1, source_target_pairs={{0,1},{1,0},{2,3},{3,2},{4,5},{5,4},{6,7},{7,6},{8,9},{9,8},{10,11... | collective-permute-start | bytes 73736 | tf_op jit(solution)/shard_map/ppermute | solution.py:44
  65.0 0.9 %collective-permute-done.21 = f32[64,96]{1,0:T(8,128)S(1)} collective-permute-done((f32[64,96]{1,0:T(8,128)S(1)}, f32[64,96]{1,0:T(8,128)S(1)}, u32[]{:S(2)}, u32[]{:S(2)}) %collective-permute-start.21) | collective-permute-done | bytes 24608 | tf_op jit(solution)/shard_map/ppermute | solution.py:44
  65.8 1.8 %collective-permute-start.24 = (f32[64,96]{1,0:T(8,128)S(1)}, f32[64,96]{1,0:T(8,128)S(1)}, u32[]{:S(2)}, u32[]{:S(2)}) collective-permute-start(f32[64,96]{1,0:T(8,128)S(1)} %add.7.refs_0_), channel_id=1, source_target_pairs={{0,6},{1,7},{2,4},{3,5},{4,2},{5,3},{6,0},{7,1},{8,14},{9,15},{10,... | collective-permute-start | bytes 73736 | tf_op jit(solution)/shard_map/ppermute | solution.py:50
  67.6 0.9 %collective-permute-start.23 = (f32[64,96]{1,0:T(8,128)S(1)}, f32[64,96]{1,0:T(8,128)S(1)}, u32[]{:S(2)}, u32[]{:S(2)}) collective-permute-start(f32[64,96]{1,0:T(8,128)S(1)} %add.7.refs_0_), channel_id=1, source_target_pairs={{0,4},{1,5},{2,6},{3,7},{4,0},{5,1},{6,2},{7,3},{8,12},{9,13},{10,... | collective-permute-start | bytes 73736 | tf_op jit(solution)/shard_map/ppermute | solution.py:50
  68.5 1.7 %collective-permute-start.22 = (f32[64,96]{1,0:T(8,128)S(1)}, f32[64,96]{1,0:T(8,128)S(1)}, u32[]{:S(2)}, u32[]{:S(2)}) collective-permute-start(f32[64,96]{1,0:T(8,128)S(1)} %add.7.refs_0_), channel_id=1, source_target_pairs={{0,2},{1,3},{2,0},{3,1},{4,6},{5,7},{6,4},{7,5},{8,10},{9,11},{10,... | collective-permute-start | bytes 73736 | tf_op jit(solution)/shard_map/ppermute | solution.py:50
  70.2 1.6 %collective-permute-done.24.refs_3_ = f32[64,96]{1,0:T(8,128)S(1)} collective-permute-done((f32[64,96]{1,0:T(8,128)S(1)}, f32[64,96]{1,0:T(8,128)S(1)}, u32[]{:S(2)}, u32[]{:S(2)}) %collective-permute-start.24) | collective-permute-done | bytes 24608 | tf_op jit(solution)/shard_map/ppermute | solution.py:50
  71.8 1.0 %collective-permute-done.23.refs_2_ = f32[64,96]{1,0:T(8,128)S(1)} collective-permute-done((f32[64,96]{1,0:T(8,128)S(1)}, f32[64,96]{1,0:T(8,128)S(1)}, u32[]{:S(2)}, u32[]{:S(2)}) %collective-permute-start.23) | collective-permute-done | bytes 24608 | tf_op jit(solution)/shard_map/ppermute | solution.py:50
  72.8 0.1 collective-permute-done.22.refs_1_
  72.9 2.7 %shard_map.66 = (f32[64,64]{1,0:T(8,128)S(1)}, f32[16,16]{1,0:T(8,128)S(1)}, bf16[2,16,1024]{2,1,0:T(8,128)(2,1)S(1)}) custom-call(f32[64,96]{1,0:T(8,128)S(1)} %add.7.refs_0_, f32[64,96]{1,0:T(8,128)S(1)} %collective-permute-done.22.refs_1_, f32[64,96]{1,0:T(8,128)S(1)} %collective-permute-done.23.refs_2_, f32[64,96]{1,0:T(8,128)S(1)} %collective-permute-done.24.refs_3_, ...), custom_call_target="tpu_custom_call" | custom-call | flops 134217728 | bytes 622592 | tf_op jit(solution)/shard_map/pallas_call | solution.py:351
  75.7 2.2 %collective-permute-start.25 = (bf16[2,16,1024]{2,1,0:T(8,128)(2,1)S(1)}, bf16[2,16,1024]{2,1,0:T(8,128)(2,1)S(1)}, u32[]{:S(2)}, u32[]{:S(2)}) collective-permute-start(bf16[2,16,1024]{2,1,0:T(8,128)(2,1)S(1)} %get-tuple-element.158), channel_id=1, source_target_pairs={{0,8},{8,16},{16,24},{24,0},{1,9},{9,17},{17,25},{25,1},{2,10},{10... | collective-permute-start | bytes 196616 | tf_op jit(solution)/shard_map/ppermute | solution.py:37
  77.9 3.2 %collective-permute-done.25.below_ref = bf16[2,16,1024]{2,1,0:T(8,128)(2,1)S(1)} collective-permute-done((bf16[2,16,1024]{2,1,0:T(8,128)(2,1)S(1)}, bf16[2,16,1024]{2,1,0:T(8,128)(2,1)S(1)}, u32[]{:S(2)}, u32[]{:S(2)}) %collective-permute-start.25) | collective-permute-done | bytes 65568 | tf_op jit(solution)/shard_map/ppermute | solution.py:37
  81.1 1.6 %shard_map.67 = f32[64,2,1024]{2,1,0:T(2,128)} custom-call(f32[64,64]{1,0:T(8,128)S(1)} %get-tuple-element.156.inverse_ref, f32[16,16]{1,0:T(8,128)S(1)} %get-tuple-element.157.weights_ref, f32[64,1024]{1,0:T(8,128)S(1)} %get-tuple-element.154.refs_4_.outer_ref, f32[1,64,1024]{2,1,0:T(8,128)S(1)} %get-tuple-element.155.refs_5_.rest_ref, ...), custom_call_target="tpu_custom_call" | custom-call | flops 134217728 | bytes 672768 | tf_op jit(solution)/shard_map/pallas_call | solution.py:351
  (14 shorter events, 0.2 us)
Async XLA Ops:
  0.0 5.7 %copy-start = (bf16[2,1024,1024]{2,1,0:T(8,128)(2,1)S(1)}, bf16[2,1024,1024]{2,1,0:T(8,128)(2,1)}, u32[]{:S(2)}) copy-start(bf16[2,1024,1024]{2,1,0:T(8,128)(2,1)} %diag_ref.15) | copy-start | bytes 12582916
  2.6 3.1 %collective-permute-start = (bf16[64,1024]{1,0:T(8,128)(2,1)S(1)}, bf16[64,1024]{1,0:T(8,128)(2,1)S(1)}, u32[]{:S(2)}, u32[]{:S(2)}) collective-permute-start(bf16[64,1024]{1,0:T(8,128)(2,1)S(1)} %get-tuple-element.85), channel_id=1, source_target_pairs={{0,1},{1,0},{2,3},{3,2},{4,5},{5,4},{6,7},{7,6},{8,9},{9,8},{10,11... | collective-permute-start | bytes 393224 | tf_op jit(solution)/shard_map/ppermute | solution.py:28
  3.1 6.4 %collective-permute-start.1 = (bf16[64,1024]{1,0:T(8,128)(2,1)S(1)}, bf16[64,1024]{1,0:T(8,128)(2,1)S(1)}, u32[]{:S(2)}, u32[]{:S(2)}) collective-permute-start(bf16[64,1024]{1,0:T(8,128)(2,1)S(1)} %get-tuple-element.91), channel_id=1, source_target_pairs={{0,8},{1,2},{2,1},{3,4},{4,3},{5,6},{6,5},{7,15},{8,0},{9,10},{10,... | collective-permute-start | bytes 393224 | tf_op jit(solution)/shard_map/ppermute | solution.py:28
  9.4 1.5 %collective-permute-start.2 = (bf16[64,1024]{1,0:T(8,128)(2,1)S(1)}, bf16[64,1024]{1,0:T(8,128)(2,1)S(1)}, u32[]{:S(2)}, u32[]{:S(2)}) collective-permute-start(bf16[64,1024]{1,0:T(8,128)(2,1)S(1)} %get-tuple-element.95), channel_id=1, source_target_pairs={{0,1},{1,0},{2,3},{3,2},{4,5},{5,4},{6,7},{7,6},{8,9},{9,8},{10,11... | collective-permute-start | bytes 393224 | tf_op jit(solution)/shard_map/ppermute | solution.py:28
  9.6 5.0 %collective-permute-start.3 = (bf16[64,1024]{1,0:T(8,128)(2,1)S(1)}, bf16[64,1024]{1,0:T(8,128)(2,1)S(1)}, u32[]{:S(2)}, u32[]{:S(2)}) collective-permute-start(bf16[64,1024]{1,0:T(8,128)(2,1)S(1)} %get-tuple-element.100), channel_id=1, source_target_pairs={{0,8},{1,2},{2,1},{3,4},{4,3},{5,6},{6,5},{7,15},{8,0},{9,10},{10,... | collective-permute-start | bytes 393224 | tf_op jit(solution)/shard_map/ppermute | solution.py:28
  13.9 2.1 %collective-permute-start.4 = (bf16[64,1024]{1,0:T(8,128)(2,1)S(1)}, bf16[64,1024]{1,0:T(8,128)(2,1)S(1)}, u32[]{:S(2)}, u32[]{:S(2)}) collective-permute-start(bf16[64,1024]{1,0:T(8,128)(2,1)S(1)} %get-tuple-element.103), channel_id=1, source_target_pairs={{0,1},{1,0},{2,3},{3,2},{4,5},{5,4},{6,7},{7,6},{8,9},{9,8},{10,11... | collective-permute-start | bytes 393224 | tf_op jit(solution)/shard_map/ppermute | solution.py:28
  14.7 5.0 %collective-permute-start.5 = (bf16[64,1024]{1,0:T(8,128)(2,1)S(1)}, bf16[64,1024]{1,0:T(8,128)(2,1)S(1)}, u32[]{:S(2)}, u32[]{:S(2)}) collective-permute-start(bf16[64,1024]{1,0:T(8,128)(2,1)S(1)} %get-tuple-element.107), channel_id=1, source_target_pairs={{0,8},{1,2},{2,1},{3,4},{4,3},{5,6},{6,5},{7,15},{8,0},{9,10},{10,... | collective-permute-start | bytes 393224 | tf_op jit(solution)/shard_map/ppermute | solution.py:28
  18.9 2.1 %collective-permute-start.6 = (bf16[64,1024]{1,0:T(8,128)(2,1)S(1)}, bf16[64,1024]{1,0:T(8,128)(2,1)S(1)}, u32[]{:S(2)}, u32[]{:S(2)}) collective-permute-start(bf16[64,1024]{1,0:T(8,128)(2,1)S(1)} %get-tuple-element.110), channel_id=1, source_target_pairs={{0,1},{1,0},{2,3},{3,2},{4,5},{5,4},{6,7},{7,6},{8,9},{9,8},{10,11... | collective-permute-start | bytes 393224 | tf_op jit(solution)/shard_map/ppermute | solution.py:28
  19.7 5.0 %collective-permute-start.7 = (bf16[64,1024]{1,0:T(8,128)(2,1)S(1)}, bf16[64,1024]{1,0:T(8,128)(2,1)S(1)}, u32[]{:S(2)}, u32[]{:S(2)}) collective-permute-start(bf16[64,1024]{1,0:T(8,128)(2,1)S(1)} %get-tuple-element.114), channel_id=1, source_target_pairs={{0,8},{1,2},{2,1},{3,4},{4,3},{5,6},{6,5},{7,15},{8,0},{9,10},{10,... | collective-permute-start | bytes 393224 | tf_op jit(solution)/shard_map/ppermute | solution.py:28
  25.7 2.9 %collective-permute-start.8 = (f32[64,64]{1,0:T(8,128)S(1)}, f32[64,64]{1,0:T(8,128)S(1)}, u32[]{:S(2)}, u32[]{:S(2)}) collective-permute-start(f32[64,64]{1,0:T(8,128)S(1)} %get-tuple-element.117), channel_id=1, source_target_pairs={{0,1},{1,0},{2,3},{3,2},{4,5},{5,4},{6,7},{7,6},{8,9},{9,8},{10,11... | collective-permute-start | bytes 49160 | tf_op jit(solution)/shard_map/ppermute | solution.py:44
  28.6 5.8 %collective-permute-start.11 = (f32[64,64]{1,0:T(8,128)S(1)}, f32[64,64]{1,0:T(8,128)S(1)}, u32[]{:S(2)}, u32[]{:S(2)}) collective-permute-start(f32[64,64]{1,0:T(8,128)S(1)} %add.6.refs_0_), channel_id=1, source_target_pairs={{0,6},{1,7},{2,4},{3,5},{4,2},{5,3},{6,0},{7,1},{8,14},{9,15},{10,... | collective-permute-start | bytes 49160 | tf_op jit(solution)/shard_map/ppermute | solution.py:50
  30.6 4.9 %collective-permute-start.10 = (f32[64,64]{1,0:T(8,128)S(1)}, f32[64,64]{1,0:T(8,128)S(1)}, u32[]{:S(2)}, u32[]{:S(2)}) collective-permute-start(f32[64,64]{1,0:T(8,128)S(1)} %add.6.refs_0_), channel_id=1, source_target_pairs={{0,4},{1,5},{2,6},{3,7},{4,0},{5,1},{6,2},{7,3},{8,12},{9,13},{10,... | collective-permute-start | bytes 49160 | tf_op jit(solution)/shard_map/ppermute | solution.py:50
  31.4 4.3 %collective-permute-start.9 = (f32[64,64]{1,0:T(8,128)S(1)}, f32[64,64]{1,0:T(8,128)S(1)}, u32[]{:S(2)}, u32[]{:S(2)}) collective-permute-start(f32[64,64]{1,0:T(8,128)S(1)} %add.6.refs_0_), channel_id=1, source_target_pairs={{0,2},{1,3},{2,0},{3,1},{4,6},{5,7},{6,4},{7,5},{8,10},{9,11},{10,... | collective-permute-start | bytes 49160 | tf_op jit(solution)/shard_map/ppermute | solution.py:50
  38.7 1.6 %collective-permute-start.12 = (bf16[64,1024]{1,0:T(8,128)(2,1)S(1)}, bf16[64,1024]{1,0:T(8,128)(2,1)S(1)}, u32[]{:S(2)}, u32[]{:S(2)}) collective-permute-start(bf16[64,1024]{1,0:T(8,128)(2,1)S(1)} %get-tuple-element.123), channel_id=1, source_target_pairs={{0,1},{1,0},{2,3},{3,2},{4,5},{5,4},{6,7},{7,6},{8,9},{9,8},{10,11... | collective-permute-start | bytes 393224 | tf_op jit(solution)/shard_map/ppermute | solution.py:28
  38.8 5.0 %collective-permute-start.13 = (bf16[64,1024]{1,0:T(8,128)(2,1)S(1)}, bf16[64,1024]{1,0:T(8,128)(2,1)S(1)}, u32[]{:S(2)}, u32[]{:S(2)}) collective-permute-start(bf16[64,1024]{1,0:T(8,128)(2,1)S(1)} %get-tuple-element.127), channel_id=1, source_target_pairs={{0,8},{1,2},{2,1},{3,4},{4,3},{5,6},{6,5},{7,15},{8,0},{9,10},{10,... | collective-permute-start | bytes 393224 | tf_op jit(solution)/shard_map/ppermute | solution.py:28
  43.2 2.1 %collective-permute-start.14 = (bf16[64,1024]{1,0:T(8,128)(2,1)S(1)}, bf16[64,1024]{1,0:T(8,128)(2,1)S(1)}, u32[]{:S(2)}, u32[]{:S(2)}) collective-permute-start(bf16[64,1024]{1,0:T(8,128)(2,1)S(1)} %get-tuple-element.130), channel_id=1, source_target_pairs={{0,1},{1,0},{2,3},{3,2},{4,5},{5,4},{6,7},{7,6},{8,9},{9,8},{10,11... | collective-permute-start | bytes 393224 | tf_op jit(solution)/shard_map/ppermute | solution.py:28
  43.8 5.0 %collective-permute-start.15 = (bf16[64,1024]{1,0:T(8,128)(2,1)S(1)}, bf16[64,1024]{1,0:T(8,128)(2,1)S(1)}, u32[]{:S(2)}, u32[]{:S(2)}) collective-permute-start(bf16[64,1024]{1,0:T(8,128)(2,1)S(1)} %get-tuple-element.134), channel_id=1, source_target_pairs={{0,8},{1,2},{2,1},{3,4},{4,3},{5,6},{6,5},{7,15},{8,0},{9,10},{10,... | collective-permute-start | bytes 393224 | tf_op jit(solution)/shard_map/ppermute | solution.py:28
  48.3 2.1 %collective-permute-start.16 = (bf16[64,1024]{1,0:T(8,128)(2,1)S(1)}, bf16[64,1024]{1,0:T(8,128)(2,1)S(1)}, u32[]{:S(2)}, u32[]{:S(2)}) collective-permute-start(bf16[64,1024]{1,0:T(8,128)(2,1)S(1)} %get-tuple-element.137), channel_id=1, source_target_pairs={{0,1},{1,0},{2,3},{3,2},{4,5},{5,4},{6,7},{7,6},{8,9},{9,8},{10,11... | collective-permute-start | bytes 393224 | tf_op jit(solution)/shard_map/ppermute | solution.py:28
  48.9 5.0 %collective-permute-start.17 = (bf16[64,1024]{1,0:T(8,128)(2,1)S(1)}, bf16[64,1024]{1,0:T(8,128)(2,1)S(1)}, u32[]{:S(2)}, u32[]{:S(2)}) collective-permute-start(bf16[64,1024]{1,0:T(8,128)(2,1)S(1)} %get-tuple-element.141), channel_id=1, source_target_pairs={{0,8},{1,2},{2,1},{3,4},{4,3},{5,6},{6,5},{7,15},{8,0},{9,10},{10,... | collective-permute-start | bytes 393224 | tf_op jit(solution)/shard_map/ppermute | solution.py:28
  53.6 1.9 %collective-permute-start.18 = (bf16[64,1024]{1,0:T(8,128)(2,1)S(1)}, bf16[64,1024]{1,0:T(8,128)(2,1)S(1)}, u32[]{:S(2)}, u32[]{:S(2)}) collective-permute-start(bf16[64,1024]{1,0:T(8,128)(2,1)S(1)} %get-tuple-element.144), channel_id=1, source_target_pairs={{0,1},{1,0},{2,3},{3,2},{4,5},{5,4},{6,7},{7,6},{8,9},{9,8},{10,11... | collective-permute-start | bytes 393224 | tf_op jit(solution)/shard_map/ppermute | solution.py:28
  54.0 5.0 %collective-permute-start.19 = (bf16[64,1024]{1,0:T(8,128)(2,1)S(1)}, bf16[64,1024]{1,0:T(8,128)(2,1)S(1)}, u32[]{:S(2)}, u32[]{:S(2)}) collective-permute-start(bf16[64,1024]{1,0:T(8,128)(2,1)S(1)} %get-tuple-element.148), channel_id=1, source_target_pairs={{0,8},{1,2},{2,1},{3,4},{4,3},{5,6},{6,5},{7,15},{8,0},{9,10},{10,... | collective-permute-start | bytes 393224 | tf_op jit(solution)/shard_map/ppermute | solution.py:28
  59.4 4.4 %collective-permute-start.20 = (bf16[2,16,1024]{2,1,0:T(8,128)(2,1)S(1)}, bf16[2,16,1024]{2,1,0:T(8,128)(2,1)S(1)}, u32[]{:S(2)}, u32[]{:S(2)}) collective-permute-start(bf16[2,16,1024]{2,1,0:T(8,128)(2,1)S(1)} %get-tuple-element.153), channel_id=1, source_target_pairs={{0,24},{8,0},{16,8},{24,16},{1,25},{9,1},{17,9},{25,17},{2,26},{10... | collective-permute-start | bytes 196616 | tf_op jit(solution)/shard_map/ppermute | solution.py:37
  64.1 1.7 %collective-permute-start.21 = (f32[64,96]{1,0:T(8,128)S(1)}, f32[64,96]{1,0:T(8,128)S(1)}, u32[]{:S(2)}, u32[]{:S(2)}) collective-permute-start(f32[64,96]{1,0:T(8,128)S(1)} %shard_map.65), channel_id=1, source_target_pairs={{0,1},{1,0},{2,3},{3,2},{4,5},{5,4},{6,7},{7,6},{8,9},{9,8},{10,11... | collective-permute-start | bytes 73736 | tf_op jit(solution)/shard_map/ppermute | solution.py:44
  65.8 6.0 %collective-permute-start.24 = (f32[64,96]{1,0:T(8,128)S(1)}, f32[64,96]{1,0:T(8,128)S(1)}, u32[]{:S(2)}, u32[]{:S(2)}) collective-permute-start(f32[64,96]{1,0:T(8,128)S(1)} %add.7.refs_0_), channel_id=1, source_target_pairs={{0,6},{1,7},{2,4},{3,5},{4,2},{5,3},{6,0},{7,1},{8,14},{9,15},{10,... | collective-permute-start | bytes 73736 | tf_op jit(solution)/shard_map/ppermute | solution.py:50
  67.6 5.2 %collective-permute-start.23 = (f32[64,96]{1,0:T(8,128)S(1)}, f32[64,96]{1,0:T(8,128)S(1)}, u32[]{:S(2)}, u32[]{:S(2)}) collective-permute-start(f32[64,96]{1,0:T(8,128)S(1)} %add.7.refs_0_), channel_id=1, source_target_pairs={{0,4},{1,5},{2,6},{3,7},{4,0},{5,1},{6,2},{7,3},{8,12},{9,13},{10,... | collective-permute-start | bytes 73736 | tf_op jit(solution)/shard_map/ppermute | solution.py:50
  68.5 4.4 %collective-permute-start.22 = (f32[64,96]{1,0:T(8,128)S(1)}, f32[64,96]{1,0:T(8,128)S(1)}, u32[]{:S(2)}, u32[]{:S(2)}) collective-permute-start(f32[64,96]{1,0:T(8,128)S(1)} %add.7.refs_0_), channel_id=1, source_target_pairs={{0,2},{1,3},{2,0},{3,1},{4,6},{5,7},{6,4},{7,5},{8,10},{9,11},{10,... | collective-permute-start | bytes 73736 | tf_op jit(solution)/shard_map/ppermute | solution.py:50
  75.7 5.4 %collective-permute-start.25 = (bf16[2,16,1024]{2,1,0:T(8,128)(2,1)S(1)}, bf16[2,16,1024]{2,1,0:T(8,128)(2,1)S(1)}, u32[]{:S(2)}, u32[]{:S(2)}) collective-permute-start(bf16[2,16,1024]{2,1,0:T(8,128)(2,1)S(1)} %get-tuple-element.158), channel_id=1, source_target_pairs={{0,8},{8,16},{16,24},{24,0},{1,9},{9,17},{17,25},{25,1},{2,10},{10... | collective-permute-start | bytes 196616 | tf_op jit(solution)/shard_map/ppermute | solution.py:37
where the time goes:
time: 82.9 us; the launch traced here: 82.7 us
  Pallas kernels  36.3 us (44%)
  starting transfers between devices  30 us (36%)
  waiting for transfers between devices  16.2 us (20%)
    pallas_call x22, Pallas kernels, call(): pl.pallas_call(kernel, out_shape=outs, in_specs=[HBM if i in far else VME...  36.3 us
    ppermute x16, starting transfers between devices, exchanged(): return lax.ppermute(block, ('cuts', 'layer'), route)  13.7 us
    ppermute x6, starting transfers between devices, partial_sums(): lax.ppermute(block, 'layer', [(i, i ^ step) for i in range(size)])  8.77 us
    ppermute x6, waiting for transfers between devices, partial_sums(): lax.ppermute(block, 'layer', [(i, i ^ step) for i in range(size)])  5.45 us
    ppermute x2, waiting for transfers between devices, rotated(): lax.ppermute(block, 'cuts', [(i, (i + distance) % size) for i in range(si...  5.1 us
    ppermute x2, starting transfers between devices, rotated(): lax.ppermute(block, 'cuts', [(i, (i + distance) % size) for i in range(si...  4.69 us
    ppermute x16, waiting for transfers between devices, exchanged(): return lax.ppermute(block, ('cuts', 'layer'), route)  3.93 us
    ppermute x2, starting transfers between devices, partial_sums(): lax.ppermute(block, 'layer', [(i, i ^ 1) for i in range(size)])  2.87 us
  transfers between devices with their start and end apart: 26, of which 17 were waited for; matrix products, arithmetic and copies ran while one was open for 0% of the time, Pallas kernels for 30%

commit v1 on v0

--- a/solution.py
+++ b/solution.py
@@ -9,6 +9,7 @@
 
 EDGE = 16
 DEG = 4
+STEPS = 2
 ROWS = 8
 HIGHEST = lax.Precision.HIGHEST
 BF16 = jnp.bfloat16
@@ -37,19 +38,24 @@
     return lax.ppermute(block, "cuts", [(i, (i + distance) % size) for i in range(size)])
 
 
+def doublings():
+    size = lax.axis_size("layer")
+    return [] if size & (size - 1) else [1 << i for i in range(size.bit_length() - 1)]
+
+
+def swapped(block, reach):
+    return lax.ppermute(block, "layer", [(i, i ^ reach) for i in range(lax.axis_size("layer"))])
+
+
 def partial_sums(block):
     size = lax.axis_size("layer")
-    if size & (size - 1) or size == 1:
+    if not doublings():
         return [lax.psum(block, "layer")]
-    block = block + lax.ppermute(block, "layer", [(i, i ^ 1) for i in range(size)])
-    reach = 2
+    reach = 1
     while size // reach > 4:
-        block = block + lax.ppermute(block, "layer", [(i, i ^ reach) for i in range(size)])
+        block = block + swapped(block, reach)
         reach *= 2
-    return [block] + [
-        lax.ppermute(block, "layer", [(i, i ^ step) for i in range(size)])
-        for step in range(reach, size, reach)
-    ]
+    return [block] + [swapped(block, step) for step in range(reach, size, reach)]
 
 
 def product(block, matrix):
@@ -159,7 +165,7 @@
 
 
 def interior_kernel(
-    layers, load, first_step, final, rows_ref, outer16_ref, rest16_ref, arrived_ref, diag_ref, last_ref, mids_ref, *refs,
+    layers, load, first_step, gram, adds, final, rows_ref, outer16_ref, rest16_ref, arrived_ref, diag_ref, last_ref, mids_ref, *refs,
 ):
     *refs, sum_ref = refs
     if load:
@@ -169,7 +175,10 @@
             mids_t_ref[i] = jnp.transpose(mids_ref[i])
     else:
         (last_t_ref, mids_t_ref, outer_ref, rest_ref, outer_before_ref, rest_before_ref, *outs) = refs
-    base_ref, next_ref, next16_ref, last_out_ref = outs
+    if adds:
+        here_ref, there_ref, *outs, total_ref = outs
+        total_ref[...] = here_ref[...] + there_ref[...]
+    base_ref, next_ref, next16_ref, *outs = outs
     centre, scale = rows_ref[0:1], rows_ref[1:2] if first_step else rows_ref[2:3]
     odd = position("layer") % 2
 
@@ -209,12 +218,12 @@
         else:
             term = (sum_ref[...] - centre * outer_ref[...]) * scale
             base_ref[...] = term if first_step else term - outer_before_ref[...]
-    if final:
-        last_out_ref[...] = sum(
-            product_t(next_ref[i], next_ref[i], HIGHEST) for i in range(layers - 1)
+    if not final:
+        send_inner(odd, next16_ref, last_ref, outs[0])
+    if gram:
+        outs[1][...] = product_t(outer_ref[...], outer_ref[...], HIGHEST) + sum(
+            product_t(rest_ref[i], rest_ref[i], HIGHEST) for i in range(layers - 1)
         )
-    else:
-        send_inner(odd, next16_ref, last_ref, last_out_ref)
 
 
 def finish(count, first_step, rows_ref, base_ref, arrived_ref, last_t_ref, store):
@@ -246,35 +255,31 @@
     send_outer(position("layer") % 2, next16_ref, last_ref, send_ref)
 
 
+def normal_kernel(parts, length, *refs):
+    grams, (rest_ref, inverse_ref, next_ref, next16_ref, gram_ref) = refs[:parts], refs[parts:]
+    inverse_ref[...] = inverse_factor(sum(ref[...] for ref in grams) * (1.0 / length))
+    gram_ref[...] = jnp.zeros(gram_ref.shape, F32)
+    for i in range(rest_ref.shape[0]):
+        block = exact(inverse_ref[...], rest_ref[i])
+        next_ref[i] = block
+        next16_ref[i] = block.astype(BF16)
+        gram_ref[...] += product_t(block, block, HIGHEST)
+
+
 def last_kernel(
-    count, rows_ref, base_ref, arrived_ref, last_t_ref, rest16_ref, rest_gram_ref,
+    count, rows_ref, base_ref, arrived_ref, last_t_ref, inverse_ref, rest16_ref, rest_gram_ref,
     next_ref, next16_ref, low_ref, gram_ref,
 ):
     def store(block):
-        next_ref[...] = block
-        next16_ref[...] = block.astype(BF16)
+        next_ref[...] = exact(inverse_ref[...], block)
 
     finish(count, False, rows_ref, base_ref, arrived_ref, last_t_ref, store)
+    next16_ref[...] = next_ref[...].astype(BF16)
     edge = low_ref.shape[1]
     low_ref[0] = next16_ref[:edge]
     for i in range(low_ref.shape[0] - 1):
         low_ref[i + 1] = rest16_ref[i, :edge]
     gram_ref[...] = rest_gram_ref[...] + product_t(next_ref[...], next_ref[...], HIGHEST)
-
-
-def normal_kernel(parts, length, *refs):
-    grams, (filtered_ref, last_ref, inverse_ref, outer_ref, outer16_ref, send_ref) = refs[:parts], refs[parts:]
-    inverse_ref[...] = inverse_factor(sum(ref[...] for ref in grams) * (1.0 / length))
-    outer_ref[...] = exact(inverse_ref[...], filtered_ref[...])
-    outer16_ref[...] = outer_ref[...].astype(BF16)
-    send_outer(position("layer") % 2, outer16_ref, last_ref, send_ref)
-
-
-def normal_rest_kernel(inverse_ref, filtered_ref, last_ref, rest_ref, rest16_ref, send_ref):
-    for i in range(rest_ref.shape[0]):
-        rest_ref[i] = exact(inverse_ref[...], filtered_ref[i])
-    rest16_ref[...] = rest_ref[...].astype(BF16)
-    send_inner(position("layer") % 2, rest16_ref, last_ref, send_ref)
 
 
 def cross_kernel(gram_ref, outer16_ref, rest16_ref, above_ref, out_ref):
@@ -369,51 +374,53 @@
         ],
     )
 
-    def filter_block(outer, rest, outer_r, rest_r, inner_send, outer_send, turned):
-        outer_before, rest_before = outer, rest
-        for step in range(DEG):
-            final = step == DEG - 1
-            outer_in = exchanged(outer_send, 1)
-            inner_in = exchanged(inner_send, 0)
-            load = not turned
-            outs = (outer32, rest32, rest16, square if final else outer16)
-            base, rest_next, rest_r, extra, *made = call(
-                functools.partial(interior_kernel, layers, load, step == 0, final),
-                outs + ((matrix, matrices) if load else ()),
-                rows, outer_r, rest_r, inner_in, diag_blocks, last, mids, *turned,
-                outer, rest, outer_before, rest_before,
-                scratch_shapes=[pltpu.VMEM((count_vec, width), F32)],
-                flops=(3 * layers - 1) * one,
-            )
-            turned = turned or made
-            if final:
-                outer_next, outer_r, low, gram = call(
-                    functools.partial(last_kernel, count),
-                    (outer32, outer16, edges, square),
-                    rows, base, outer_in, turned[0], rest_r, extra,
-                )
-                return outer_next, rest_next, outer_r, rest_r, low, gram, turned
-            inner_send = extra
-            outer_next, outer_r, outer_send = call(
-                functools.partial(step_kernel, count, step == 0),
-                (outer32, outer16, outer16),
-                rows, base, outer_in, last, turned[0],
-            )
-            outer_before, rest_before, outer, rest = outer, rest, outer_next, rest_next
-
-    outer, rest, _, _, _, gram, turned = filter_block(
-        outer, rest, outer_r, rest_r, inner_send, outer_send, []
-    )
-    grams = partial_sums(gram)
-    inverse, outer, outer_r, outer_send = call(
-        functools.partial(normal_kernel, len(grams), length_all),
-        (square, outer32, outer16, outer16), *grams, outer, last,
-    )
-    rest, rest_r, inner_send = call(
-        normal_rest_kernel, (rest32, rest16, outer16), inverse, rest, last
-    )
-    outer, rest, outer_r, rest_r, low, gram, _ = filter_block(
-        outer, rest, outer_r, rest_r, inner_send, outer_send, turned
+    outer_before, rest_before = outer, rest
+    turned, reaches = [], doublings()
+    applications = STEPS * DEG
+    for step in range(applications):
+        first_step, final, gram = step % DEG == 0, step == applications - 1, step == DEG
+        load = step == 0
+        outer_in = exchanged(outer_send, 1)
+        inner_in = exchanged(inner_send, 0)
+        adds = step > DEG and bool(reaches) and not final
+        base, rest_next, rest_r, *extra = call(
+            functools.partial(interior_kernel, layers, load, first_step, gram, adds, final),
+            (outer32, rest32, rest16)
+            + (() if final else (outer16,))
+            + ((square,) if gram or adds else ())
+            + ((matrix, matrices) if load else ()),
+            rows, outer_r, rest_r, inner_in, diag_blocks, last, mids, *turned,
+            outer, rest, outer_before, rest_before,
+            *((total, swapped(total, reaches.pop(0))) if adds else ()),
+            scratch_shapes=[pltpu.VMEM((count_vec, width), F32)],
+            flops=(3 * layers - 1) * one,
+        )
+        if load:
+            *extra, last_t, mids_t = extra
+            turned = [last_t, mids_t]
+        if gram or adds:
+            total = extra[-1]
+        if gram and not reaches:
+            total = lax.psum(total, "layer")
+        if final:
+            break
+        outer_next, outer_r, outer_send = call(
+            functools.partial(step_kernel, count, first_step),
+            (outer32, outer16, outer16), rows, base, outer_in, last, last_t,
+        )
+        inner_send = extra[0]
+        outer_before, rest_before, outer, rest = outer, rest, outer_next, rest_next
+
+    totals = [total]
+    for reach in reaches:
+        totals = [sum(totals), swapped(sum(totals), reach)]
+    inverse, rest, rest_r, rest_gram = call(
+        functools.partial(normal_kernel, len(totals), length_all),
+        (square, rest32, rest16, square), *totals, rest_next,
+    )
+    outer, outer_r, low, gram = call(
+        functools.partial(last_kernel, count), (outer32, outer16, edges, square),
+        rows, base, outer_in, last_t, inverse, rest_r, rest_gram,
     )
     above = rotated(low, -1)
     cross = call(

time: 82.9 us -> 77 us (0.929)
  waiting for transfers between devices: 16.2 us -> 12.5 us
  starting transfers between devices: 30 us -> 28.1 us
    ppermute x16, waiting for transfers between devices: 3.93 us -> 1.94 us  [exchanged(): return lax.ppermute(block, ('cuts', 'layer'), route)]
    ppermute x8 -> x7, starting transfers between devices: 11.6 us -> 9.68 us  [swapped(): lax.ppermute(block, 'layer', [(i, i ^ reach) for i in range(lax.axis_size...]
    ppermute x8 -> x7, waiting for transfers between devices: 7.17 us -> 5.29 us  [swapped(): lax.ppermute(block, 'layer', [(i, i ^ reach) for i in range(lax.axis_size...]
    pallas_call x22 -> x21, Pallas kernels: 36.3 us -> 36 us  [call(): pl.pallas_call(kernel, out_shape=outs, in_specs=[HBM if i in far else VME...]
  transfers between devices with their start and end apart: 26 -> 25, of which waited for: 17 -> 11; matrix products, arithmetic and copies ran while one was open for 0% -> 0% of each run, Pallas kernels for 30% -> 37%
where the time goes in v1:
time: 77 us; the launch traced here: 76.8 us
  Pallas kernels  36 us (47%)
  starting transfers between devices  28.1 us (36%)
  waiting for transfers between devices  12.5 us (16%)
    pallas_call x21, Pallas kernels, call(): pl.pallas_call(kernel, out_shape=outs, in_specs=[HBM if i in far else VME...  36 us
    ppermute x16, starting transfers between devices, exchanged(): return lax.ppermute(block, ('cuts', 'layer'), route)  14 us
    ppermute x7, starting transfers between devices, swapped(): lax.ppermute(block, 'layer', [(i, i ^ reach) for i in range(lax.axis_size...  9.68 us
    ppermute x7, waiting for transfers between devices, swapped(): lax.ppermute(block, 'layer', [(i, i ^ reach) for i in range(lax.axis_size...  5.29 us
    ppermute x2, waiting for transfers between devices, rotated(): lax.ppermute(block, 'cuts', [(i, (i + distance) % size) for i in range(si...  5.25 us
    ppermute x2, starting transfers between devices, rotated(): lax.ppermute(block, 'cuts', [(i, (i + distance) % size) for i in range(si...  4.44 us
    ppermute x16, waiting for transfers between devices, exchanged(): return lax.ppermute(block, ('cuts', 'layer'), route)  1.94 us
  transfers between devices with their start and end apart: 25, of which 11 were waited for; matrix products, arithmetic and copies ran while one was open for 0% of the time, Pallas kernels for 37%

profile of v1, /device:TPU:0, one launch (start us, length us, event | category | flops | bytes accessed | tf_op | source)
XLA Modules:
  0.0 76.8 jit_solution(12254925800043281394)
XLA Ops:
  0.0 2.6 %shard_map.46 = (f32[64,1024]{1,0:T(8,128)S(1)}, f32[1,64,1024]{2,1,0:T(8,128)S(1)}, bf16[64,1024]{1,0:T(8,128)(2,1)S(1)}, bf16[1,64,1024]{2,1,0:T(8,128)(2,1)S(...) custom-call(s32[1,2]{1,0:T(1,128)} %far_bounds_ref.1, ...), custom_call_target="tpu_custom_call" | custom-call | flops 134217728 | bytes 4718600 | tf_op jit(solution)/shard_map/pallas_call | solution.py:356
  2.6 0.5 collective-permute-start
  3.1 2.6 %collective-permute-start.1 = (bf16[64,1024]{1,0:T(8,128)(2,1)S(1)}, bf16[64,1024]{1,0:T(8,128)(2,1)S(1)}, u32[]{:S(2)}, u32[]{:S(2)}) collective-permute-start(bf16[64,1024]{1,0:T(8,128)(2,1)S(1)} %get-tuple-element.90), channel_id=1, source_target_pairs={{0,8},{1,2},{2,1},{3,4},{4,3},{5,6},{6,5},{7,15},{8,0},{9,10},{10,... | collective-permute-start | bytes 393224 | tf_op jit(solution)/shard_map/ppermute | solution.py:29
  5.7 0.0 collective-permute-done.arrived_ref
  5.7 3.7 %shard_map.47 = (f32[64,1024]{1,0:T(8,128)S(1)}, f32[1,64,1024]{2,1,0:T(8,128)S(1)}, bf16[1,64,1024]{2,1,0:T(8,128)(2,1)S(1)}, bf16[64,1024]{1,0:T(8,128)(2,1)S(...) custom-call(f32[8,1024]{1,0:T(8,128)S(1)} %get-tuple-element.81.rows_ref, ...), custom_call_target="tpu_custom_call" | custom-call | flops 671088640 | bytes 9863168 | tf_op jit(solution)/shard_map/pallas_call | solution.py:356
  9.4 0.1 collective-permute-start.2
  9.5 0.0 collective-permute-done.1.arrived_ref
  9.5 0.1 shard_map.48
  9.6 1.3 %collective-permute-start.3 = (bf16[64,1024]{1,0:T(8,128)(2,1)S(1)}, bf16[64,1024]{1,0:T(8,128)(2,1)S(1)}, u32[]{:S(2)}, u32[]{:S(2)}) collective-permute-start(bf16[64,1024]{1,0:T(8,128)(2,1)S(1)} %get-tuple-element.99), channel_id=1, source_target_pairs={{0,8},{1,2},{2,1},{3,4},{4,3},{5,6},{6,5},{7,15},{8,0},{9,10},{10,... | collective-permute-start | bytes 393224 | tf_op jit(solution)/shard_map/ppermute | solution.py:29
  10.9 0.0 collective-permute-done.2.arrived_ref
  10.9 2.9 %shard_map.49 = (f32[64,1024]{1,0:T(8,128)S(1)}, f32[1,64,1024]{2,1,0:T(8,128)S(1)}, bf16[1,64,1024]{2,1,0:T(8,128)(2,1)S(1)}, bf16[64,1024]{1,0:T(8,128)(2,1)S(1)}) custom-call(f32[8,1024]{1,0:T(8,128)S(1)} %get-tuple-element.81.rows_ref, bf16[64,1024]{1,0:T(8,128)(2,1)S(1)} %get-tuple-element.92.outer16_ref, ...), custom_call_target="tpu_custom_call" | custom-call | flops 671088640 | bytes 14057472 | tf_op jit(solution)/shard_map/pallas_call | solution.py:356
  13.9 0.1 collective-permute-start.4
  13.9 0.7 collective-permute-done.3.arrived_ref
  14.7 1.3 %collective-permute-start.5 = (bf16[64,1024]{1,0:T(8,128)(2,1)S(1)}, bf16[64,1024]{1,0:T(8,128)(2,1)S(1)}, u32[]{:S(2)}, u32[]{:S(2)}) collective-permute-start(bf16[64,1024]{1,0:T(8,128)(2,1)S(1)} %get-tuple-element.106), channel_id=1, source_target_pairs={{0,8},{1,2},{2,1},{3,4},{4,3},{5,6},{6,5},{7,15},{8,0},{9,10},{10,... | collective-permute-start | bytes 393224 | tf_op jit(solution)/shard_map/ppermute | solution.py:29
  16.0 0.0 collective-permute-done.4.arrived_ref
  16.0 2.9 %shard_map.51 = (f32[64,1024]{1,0:T(8,128)S(1)}, f32[1,64,1024]{2,1,0:T(8,128)S(1)}, bf16[1,64,1024]{2,1,0:T(8,128)(2,1)S(1)}, bf16[64,1024]{1,0:T(8,128)(2,1)S(1)}) custom-call(f32[8,1024]{1,0:T(8,128)S(1)} %get-tuple-element.81.rows_ref, bf16[64,1024]{1,0:T(8,128)(2,1)S(1)} %get-tuple-element.100.outer16_ref, ...), custom_call_target="tpu_custom_call" | custom-call | flops 671088640 | bytes 14057472 | tf_op jit(solution)/shard_map/pallas_call | solution.py:356
  18.9 0.1 collective-permute-start.6
  19.0 0.7 collective-permute-done.5.arrived_ref
  19.7 1.3 %collective-permute-start.7 = (bf16[64,1024]{1,0:T(8,128)(2,1)S(1)}, bf16[64,1024]{1,0:T(8,128)(2,1)S(1)}, u32[]{:S(2)}, u32[]{:S(2)}) collective-permute-start(bf16[64,1024]{1,0:T(8,128)(2,1)S(1)} %get-tuple-element.113), channel_id=1, source_target_pairs={{0,8},{1,2},{2,1},{3,4},{4,3},{5,6},{6,5},{7,15},{8,0},{9,10},{10,... | collective-permute-start | bytes 393224 | tf_op jit(solution)/shard_map/ppermute | solution.py:29
  21.1 0.0 collective-permute-done.6.arrived_ref
  21.1 3.1 %shard_map.53 = (f32[64,1024]{1,0:T(8,128)S(1)}, f32[1,64,1024]{2,1,0:T(8,128)S(1)}, bf16[1,64,1024]{2,1,0:T(8,128)(2,1)S(1)}, bf16[64,1024]{1,0:T(8,128)(2,1)S(1)}) custom-call(f32[8,1024]{1,0:T(8,128)S(1)} %get-tuple-element.81.rows_ref, bf16[64,1024]{1,0:T(8,128)(2,1)S(1)} %get-tuple-element.107.outer16_ref, ...), custom_call_target="tpu_custom_call" | custom-call | flops 671088640 | bytes 14057472 | tf_op jit(solution)/shard_map/pallas_call | solution.py:356
  24.2 0.1 collective-permute-start.8
  24.3 0.5 collective-permute-done.7.arrived_ref
  24.8 1.3 %collective-permute-start.9 = (bf16[64,1024]{1,0:T(8,128)(2,1)S(1)}, bf16[64,1024]{1,0:T(8,128)(2,1)S(1)}, u32[]{:S(2)}, u32[]{:S(2)}) collective-permute-start(bf16[64,1024]{1,0:T(8,128)(2,1)S(1)} %get-tuple-element.120), channel_id=1, source_target_pairs={{0,8},{1,2},{2,1},{3,4},{4,3},{5,6},{6,5},{7,15},{8,0},{9,10},{10,... | collective-permute-start | bytes 393224 | tf_op jit(solution)/shard_map/ppermute | solution.py:29
  26.1 0.0 collective-permute-done.8.arrived_ref
  26.2 3.5 %shard_map.55 = (f32[64,1024]{1,0:T(8,128)S(1)}, f32[1,64,1024]{2,1,0:T(8,128)S(1)}, bf16[1,64,1024]{2,1,0:T(8,128)(2,1)S(1)}, bf16[64,1024]{1,0:T(8,128)(2,1)S(1)}, f32[64,64]{1,0:T(8,128)S(1)}) custom-call(f32[8,1024]{1,0:T(8,128)S(1)} %get-tuple-element.81.rows_ref, bf16[64,1024]{1,0:T(8,128)(2,1)S(1)} %get-tuple-element.114.outer16_ref, ...), custom_call_target="tpu_custom_call" | custom-call | flops 671088640 | bytes 14057472 | tf_op jit(solution)/shard_map/pallas_call | solution.py:356
  29.6 0.4 collective-permute-start.10
  30.0 0.2 collective-permute-start.11
  30.2 0.0 collective-permute-done.9.arrived_ref
  30.3 1.2 %collective-permute-start.12 = (bf16[64,1024]{1,0:T(8,128)(2,1)S(1)}, bf16[64,1024]{1,0:T(8,128)(2,1)S(1)}, u32[]{:S(2)}, u32[]{:S(2)}) collective-permute-start(bf16[64,1024]{1,0:T(8,128)(2,1)S(1)} %get-tuple-element.128), channel_id=1, source_target_pairs={{0,8},{1,2},{2,1},{3,4},{4,3},{5,6},{6,5},{7,15},{8,0},{9,10},{10,... | collective-permute-start | bytes 393224 | tf_op jit(solution)/shard_map/ppermute | solution.py:29
  31.5 0.0 collective-permute-done.11.refs_7_
  31.5 0.0 collective-permute-done.10.arrived_ref
  31.5 2.9 %shard_map.57 = (f32[64,1024]{1,0:T(8,128)S(1)}, f32[1,64,1024]{2,1,0:T(8,128)S(1)}, bf16[1,64,1024]{2,1,0:T(8,128)(2,1)S(1)}, bf16[64,1024]{1,0:T(8,128)(2,1)S(1)}, f32[64,64]{1,0:T(8,128)S(1)}) custom-call(f32[8,1024]{1,0:T(8,128)S(1)} %get-tuple-element.81.rows_ref, bf16[64,1024]{1,0:T(8,128)(2,1)S(1)} %get-tuple-element.121.outer16_ref, ...), custom_call_target="tpu_custom_call" | custom-call | flops 671088640 | bytes 14090240 | tf_op jit(solution)/shard_map/pallas_call | solution.py:356
  34.4 1.0 %collective-permute-start.13 = (bf16[64,1024]{1,0:T(8,128)(2,1)S(1)}, bf16[64,1024]{1,0:T(8,128)(2,1)S(1)}, u32[]{:S(2)}, u32[]{:S(2)}) collective-permute-start(bf16[64,1024]{1,0:T(8,128)(2,1)S(1)} %get-tuple-element.131), channel_id=1, source_target_pairs={{0,1},{1,0},{2,3},{3,2},{4,5},{5,4},{6,7},{7,6},{8,9},{9,8},{10,11... | collective-permute-start | bytes 393224 | tf_op jit(solution)/shard_map/ppermute | solution.py:29
  35.4 2.1 %collective-permute-start.14 = (f32[64,64]{1,0:T(8,128)S(1)}, f32[64,64]{1,0:T(8,128)S(1)}, u32[]{:S(2)}, u32[]{:S(2)}) collective-permute-start(f32[64,64]{1,0:T(8,128)S(1)} %get-tuple-element.134.refs_6_), channel_id=1, source_target_pairs={{0,2},{1,3},{2,0},{3,1},{4,6},{5,7},{6,4},{7,5},{8,10},{9,11},{10,... | collective-permute-start | bytes 49160 | tf_op jit(solution)/shard_map/ppermute | solution.py:47
  37.5 0.0 collective-permute-done.12.arrived_ref
  37.6 1.3 %collective-permute-start.15 = (bf16[64,1024]{1,0:T(8,128)(2,1)S(1)}, bf16[64,1024]{1,0:T(8,128)(2,1)S(1)}, u32[]{:S(2)}, u32[]{:S(2)}) collective-permute-start(bf16[64,1024]{1,0:T(8,128)(2,1)S(1)} %get-tuple-element.136), channel_id=1, source_target_pairs={{0,8},{1,2},{2,1},{3,4},{4,3},{5,6},{6,5},{7,15},{8,0},{9,10},{10,... | collective-permute-start | bytes 393224 | tf_op jit(solution)/shard_map/ppermute | solution.py:29
  38.9 0.6 collective-permute-done.14.refs_7_
  39.5 2.9 %shard_map.59 = (f32[64,1024]{1,0:T(8,128)S(1)}, f32[1,64,1024]{2,1,0:T(8,128)S(1)}, bf16[1,64,1024]{2,1,0:T(8,128)(2,1)S(1)}, bf16[64,1024]{1,0:T(8,128)(2,1)S(1)}, f32[64,64]{1,0:T(8,128)S(1)}) custom-call(f32[8,1024]{1,0:T(8,128)S(1)} %get-tuple-element.81.rows_ref, bf16[64,1024]{1,0:T(8,128)(2,1)S(1)} %get-tuple-element.129.outer16_ref, ...), custom_call_target="tpu_custom_call" | custom-call | flops 671088640 | bytes 14090240 | tf_op jit(solution)/shard_map/pallas_call | solution.py:356
  42.5 0.1 collective-permute-start.16
  42.5 0.1 collective-permute-done.15.arrived_ref
  42.6 0.2 shard_map.60
  42.9 1.3 %collective-permute-start.17 = (bf16[64,1024]{1,0:T(8,128)(2,1)S(1)}, bf16[64,1024]{1,0:T(8,128)(2,1)S(1)}, u32[]{:S(2)}, u32[]{:S(2)}) collective-permute-start(bf16[64,1024]{1,0:T(8,128)(2,1)S(1)} %get-tuple-element.143), channel_id=1, source_target_pairs={{0,8},{1,2},{2,1},{3,4},{4,3},{5,6},{6,5},{7,15},{8,0},{9,10},{10,... | collective-permute-start | bytes 393224 | tf_op jit(solution)/shard_map/ppermute | solution.py:29
  44.2 2.9 %collective-permute-start.18 = (f32[64,64]{1,0:T(8,128)S(1)}, f32[64,64]{1,0:T(8,128)S(1)}, u32[]{:S(2)}, u32[]{:S(2)}) collective-permute-start(f32[64,64]{1,0:T(8,128)S(1)} %get-tuple-element.144.refs_0_), channel_id=1, source_target_pairs={{0,4},{1,5},{2,6},{3,7},{4,0},{5,1},{6,2},{7,3},{8,12},{9,13},{10,... | collective-permute-start | bytes 49160 | tf_op jit(solution)/shard_map/ppermute | solution.py:47
  47.1 0.0 collective-permute-done.16.arrived_ref
  47.1 3.1 %shard_map.61 = (f32[64,1024]{1,0:T(8,128)S(1)}, f32[1,64,1024]{2,1,0:T(8,128)S(1)}, bf16[1,64,1024]{2,1,0:T(8,128)(2,1)}) custom-call(f32[8,1024]{1,0:T(8,128)S(1)} %get-tuple-element.81.rows_ref, bf16[64,1024]{1,0:T(8,128)(2,1)S(1)} %get-tuple-element.137.outer16_ref, bf16[1,64,1024]{2,1,0:T(8,128)(2,1)S(1)} %get-tuple-element.138.rest16_ref, ...), custom_call_target="tpu_custom_call" | custom-call | flops 671088640 | bytes 14057472 | tf_op jit(solution)/shard_map/pallas_call | solution.py:356
  50.2 0.8 collective-permute-done.18.refs_1_
  50.9 2.4 %shard_map.62 = (f32[64,64]{1,0:T(8,128)S(1)}, f32[1,64,1024]{2,1,0:T(8,128)S(1)}, bf16[1,64,1024]{2,1,0:T(8,128)(2,1)S(1)}, f32[64,64]{1,0:T(8,128)S(1)}) custom-call(f32[64,64]{1,0:T(8,128)S(1)} %get-tuple-element.144.refs_0_, f32[64,64]{1,0:T(8,128)S(1)} %collective-permute-done.18.refs_1_, f32[1,64,1024]{2,1,0:T(8,128)S(1)} %get-tuple-element.145.refs_2_), custom_call_target="tpu_custom_call" | custom-call | flops 134217728 | bytes 294912 | tf_op jit(solution)/shard_map/pallas_call | solution.py:356
  53.3 0.8 shard_map.63
  54.1 2.3 %collective-permute-start.19 = (bf16[2,16,1024]{2,1,0:T(8,128)(2,1)S(1)}, bf16[2,16,1024]{2,1,0:T(8,128)(2,1)S(1)}, u32[]{:S(2)}, u32[]{:S(2)}) collective-permute-start(bf16[2,16,1024]{2,1,0:T(8,128)(2,1)S(1)} %get-tuple-element.151), channel_id=1, source_target_pairs={{0,24},{8,0},{16,8},{24,16},{1,25},{9,1},{17,9},{25,17},{2,26},{10... | collective-permute-start | bytes 196616 | tf_op jit(solution)/shard_map/ppermute | solution.py:38
  56.4 2.0 %collective-permute-done.19.above_ref = bf16[2,16,1024]{2,1,0:T(8,128)(2,1)S(1)} collective-permute-done((bf16[2,16,1024]{2,1,0:T(8,128)(2,1)S(1)}, bf16[2,16,1024]{2,1,0:T(8,128)(2,1)S(1)}, u32[]{:S(2)}, u32[]{:S(2)}) %collective-permute-start.19) | collective-permute-done | bytes 65568 | tf_op jit(solution)/shard_map/ppermute | solution.py:38
  58.4 0.3 shard_map.64
  58.7 0.1 collective-permute-start.20
  58.8 1.2 %collective-permute-done.20 = f32[64,96]{1,0:T(8,128)S(1)} collective-permute-done((f32[64,96]{1,0:T(8,128)S(1)}, f32[64,96]{1,0:T(8,128)S(1)}, u32[]{:S(2)}, u32[]{:S(2)}) %collective-permute-start.20) | collective-permute-done | bytes 24608 | tf_op jit(solution)/shard_map/ppermute | solution.py:47
  60.0 2.2 %collective-permute-start.23 = (f32[64,96]{1,0:T(8,128)S(1)}, f32[64,96]{1,0:T(8,128)S(1)}, u32[]{:S(2)}, u32[]{:S(2)}) collective-permute-start(f32[64,96]{1,0:T(8,128)S(1)} %add.3.refs_0_), channel_id=1, source_target_pairs={{0,6},{1,7},{2,4},{3,5},{4,2},{5,3},{6,0},{7,1},{8,14},{9,15},{10,... | collective-permute-start | bytes 73736 | tf_op jit(solution)/shard_map/ppermute | solution.py:47
  62.2 0.4 collective-permute-start.22
  62.6 1.8 %collective-permute-start.21 = (f32[64,96]{1,0:T(8,128)S(1)}, f32[64,96]{1,0:T(8,128)S(1)}, u32[]{:S(2)}, u32[]{:S(2)}) collective-permute-start(f32[64,96]{1,0:T(8,128)S(1)} %add.3.refs_0_), channel_id=1, source_target_pairs={{0,2},{1,3},{2,0},{3,1},{4,6},{5,7},{6,4},{7,5},{8,10},{9,11},{10,... | collective-permute-start | bytes 73736 | tf_op jit(solution)/shard_map/ppermute | solution.py:47
  64.4 1.3 %collective-permute-done.23.refs_3_ = f32[64,96]{1,0:T(8,128)S(1)} collective-permute-done((f32[64,96]{1,0:T(8,128)S(1)}, f32[64,96]{1,0:T(8,128)S(1)}, u32[]{:S(2)}, u32[]{:S(2)}) %collective-permute-start.23) | collective-permute-done | bytes 24608 | tf_op jit(solution)/shard_map/ppermute | solution.py:47
  65.7 1.4 %collective-permute-done.22.refs_2_ = f32[64,96]{1,0:T(8,128)S(1)} collective-permute-done((f32[64,96]{1,0:T(8,128)S(1)}, f32[64,96]{1,0:T(8,128)S(1)}, u32[]{:S(2)}, u32[]{:S(2)}) %collective-permute-start.22) | collective-permute-done | bytes 24608 | tf_op jit(solution)/shard_map/ppermute | solution.py:47
  67.1 0.0 collective-permute-done.21.refs_1_
  67.1 2.7 %shard_map.65 = (f32[64,64]{1,0:T(8,128)S(1)}, f32[16,16]{1,0:T(8,128)S(1)}, bf16[2,16,1024]{2,1,0:T(8,128)(2,1)S(1)}) custom-call(f32[64,96]{1,0:T(8,128)S(1)} %add.3.refs_0_, f32[64,96]{1,0:T(8,128)S(1)} %collective-permute-done.21.refs_1_, f32[64,96]{1,0:T(8,128)S(1)} %collective-permute-done.22.refs_2_, f32[64,96]{1,0:T(8,128)S(1)} %collective-permute-done.23.refs_3_, ...), custom_call_target="tpu_custom_call" | custom-call | flops 134217728 | bytes 622592 | tf_op jit(solution)/shard_map/pallas_call | solution.py:356
  69.8 2.2 %collective-permute-start.24 = (bf16[2,16,1024]{2,1,0:T(8,128)(2,1)S(1)}, bf16[2,16,1024]{2,1,0:T(8,128)(2,1)S(1)}, u32[]{:S(2)}, u32[]{:S(2)}) collective-permute-start(bf16[2,16,1024]{2,1,0:T(8,128)(2,1)S(1)} %get-tuple-element.156), channel_id=1, source_target_pairs={{0,8},{8,16},{16,24},{24,0},{1,9},{9,17},{17,25},{25,1},{2,10},{10... | collective-permute-start | bytes 196616 | tf_op jit(solution)/shard_map/ppermute | solution.py:38
  72.0 3.2 %collective-permute-done.24.below_ref = bf16[2,16,1024]{2,1,0:T(8,128)(2,1)S(1)} collective-permute-done((bf16[2,16,1024]{2,1,0:T(8,128)(2,1)S(1)}, bf16[2,16,1024]{2,1,0:T(8,128)(2,1)S(1)}, u32[]{:S(2)}, u32[]{:S(2)}) %collective-permute-start.24) | collective-permute-done | bytes 65568 | tf_op jit(solution)/shard_map/ppermute | solution.py:38
  75.2 1.6 %shard_map.66 = f32[64,2,1024]{2,1,0:T(2,128)} custom-call(f32[64,64]{1,0:T(8,128)S(1)} %get-tuple-element.154.inverse_ref, f32[16,16]{1,0:T(8,128)S(1)} %get-tuple-element.155.weights_ref, f32[64,1024]{1,0:T(8,128)S(1)} %get-tuple-element.152.refs_4_.outer_ref, f32[1,64,1024]{2,1,0:T(8,128)S(1)} %get-tuple-element.153.refs_5_.rest_ref, ...), custom_call_target="tpu_custom_call" | custom-call | flops 134217728 | bytes 672768 | tf_op jit(solution)/shard_map/pallas_call | solution.py:356
  (10 shorter events, 0.2 us)
Async XLA Ops:
  0.0 5.7 %copy-start = (bf16[2,1024,1024]{2,1,0:T(8,128)(2,1)S(1)}, bf16[2,1024,1024]{2,1,0:T(8,128)(2,1)}, u32[]{:S(2)}) copy-start(bf16[2,1024,1024]{2,1,0:T(8,128)(2,1)} %diag_ref.15) | copy-start | bytes 12582916
  2.6 3.1 %collective-permute-start = (bf16[64,1024]{1,0:T(8,128)(2,1)S(1)}, bf16[64,1024]{1,0:T(8,128)(2,1)S(1)}, u32[]{:S(2)}, u32[]{:S(2)}) collective-permute-start(bf16[64,1024]{1,0:T(8,128)(2,1)S(1)} %get-tuple-element.84), channel_id=1, source_target_pairs={{0,1},{1,0},{2,3},{3,2},{4,5},{5,4},{6,7},{7,6},{8,9},{9,8},{10,11... | collective-permute-start | bytes 393224 | tf_op jit(solution)/shard_map/ppermute | solution.py:29
  3.1 6.4 %collective-permute-start.1 = (bf16[64,1024]{1,0:T(8,128)(2,1)S(1)}, bf16[64,1024]{1,0:T(8,128)(2,1)S(1)}, u32[]{:S(2)}, u32[]{:S(2)}) collective-permute-start(bf16[64,1024]{1,0:T(8,128)(2,1)S(1)} %get-tuple-element.90), channel_id=1, source_target_pairs={{0,8},{1,2},{2,1},{3,4},{4,3},{5,6},{6,5},{7,15},{8,0},{9,10},{10,... | collective-permute-start | bytes 393224 | tf_op jit(solution)/shard_map/ppermute | solution.py:29
  9.4 1.5 %collective-permute-start.2 = (bf16[64,1024]{1,0:T(8,128)(2,1)S(1)}, bf16[64,1024]{1,0:T(8,128)(2,1)S(1)}, u32[]{:S(2)}, u32[]{:S(2)}) collective-permute-start(bf16[64,1024]{1,0:T(8,128)(2,1)S(1)} %get-tuple-element.94), channel_id=1, source_target_pairs={{0,1},{1,0},{2,3},{3,2},{4,5},{5,4},{6,7},{7,6},{8,9},{9,8},{10,11... | collective-permute-start | bytes 393224 | tf_op jit(solution)/shard_map/ppermute | solution.py:29
  9.6 5.0 %collective-permute-start.3 = (bf16[64,1024]{1,0:T(8,128)(2,1)S(1)}, bf16[64,1024]{1,0:T(8,128)(2,1)S(1)}, u32[]{:S(2)}, u32[]{:S(2)}) collective-permute-start(bf16[64,1024]{1,0:T(8,128)(2,1)S(1)} %get-tuple-element.99), channel_id=1, source_target_pairs={{0,8},{1,2},{2,1},{3,4},{4,3},{5,6},{6,5},{7,15},{8,0},{9,10},{10,... | collective-permute-start | bytes 393224 | tf_op jit(solution)/shard_map/ppermute | solution.py:29
  13.9 2.1 %collective-permute-start.4 = (bf16[64,1024]{1,0:T(8,128)(2,1)S(1)}, bf16[64,1024]{1,0:T(8,128)(2,1)S(1)}, u32[]{:S(2)}, u32[]{:S(2)}) collective-permute-start(bf16[64,1024]{1,0:T(8,128)(2,1)S(1)} %get-tuple-element.102), channel_id=1, source_target_pairs={{0,1},{1,0},{2,3},{3,2},{4,5},{5,4},{6,7},{7,6},{8,9},{9,8},{10,11... | collective-permute-start | bytes 393224 | tf_op jit(solution)/shard_map/ppermute | solution.py:29
  14.7 5.0 %collective-permute-start.5 = (bf16[64,1024]{1,0:T(8,128)(2,1)S(1)}, bf16[64,1024]{1,0:T(8,128)(2,1)S(1)}, u32[]{:S(2)}, u32[]{:S(2)}) collective-permute-start(bf16[64,1024]{1,0:T(8,128)(2,1)S(1)} %get-tuple-element.106), channel_id=1, source_target_pairs={{0,8},{1,2},{2,1},{3,4},{4,3},{5,6},{6,5},{7,15},{8,0},{9,10},{10,... | collective-permute-start | bytes 393224 | tf_op jit(solution)/shard_map/ppermute | solution.py:29
  18.9 2.1 %collective-permute-start.6 = (bf16[64,1024]{1,0:T(8,128)(2,1)S(1)}, bf16[64,1024]{1,0:T(8,128)(2,1)S(1)}, u32[]{:S(2)}, u32[]{:S(2)}) collective-permute-start(bf16[64,1024]{1,0:T(8,128)(2,1)S(1)} %get-tuple-element.109), channel_id=1, source_target_pairs={{0,1},{1,0},{2,3},{3,2},{4,5},{5,4},{6,7},{7,6},{8,9},{9,8},{10,11... | collective-permute-start | bytes 393224 | tf_op jit(solution)/shard_map/ppermute | solution.py:29
  19.7 5.0 %collective-permute-start.7 = (bf16[64,1024]{1,0:T(8,128)(2,1)S(1)}, bf16[64,1024]{1,0:T(8,128)(2,1)S(1)}, u32[]{:S(2)}, u32[]{:S(2)}) collective-permute-start(bf16[64,1024]{1,0:T(8,128)(2,1)S(1)} %get-tuple-element.113), channel_id=1, source_target_pairs={{0,8},{1,2},{2,1},{3,4},{4,3},{5,6},{6,5},{7,15},{8,0},{9,10},{10,... | collective-permute-start | bytes 393224 | tf_op jit(solution)/shard_map/ppermute | solution.py:29
  24.2 2.0 %collective-permute-start.8 = (bf16[64,1024]{1,0:T(8,128)(2,1)S(1)}, bf16[64,1024]{1,0:T(8,128)(2,1)S(1)}, u32[]{:S(2)}, u32[]{:S(2)}) collective-permute-start(bf16[64,1024]{1,0:T(8,128)(2,1)S(1)} %get-tuple-element.116), channel_id=1, source_target_pairs={{0,1},{1,0},{2,3},{3,2},{4,5},{5,4},{6,7},{7,6},{8,9},{9,8},{10,11... | collective-permute-start | bytes 393224 | tf_op jit(solution)/shard_map/ppermute | solution.py:29
  24.8 5.4 %collective-permute-start.9 = (bf16[64,1024]{1,0:T(8,128)(2,1)S(1)}, bf16[64,1024]{1,0:T(8,128)(2,1)S(1)}, u32[]{:S(2)}, u32[]{:S(2)}) collective-permute-start(bf16[64,1024]{1,0:T(8,128)(2,1)S(1)} %get-tuple-element.120), channel_id=1, source_target_pairs={{0,8},{1,2},{2,1},{3,4},{4,3},{5,6},{6,5},{7,15},{8,0},{9,10},{10,... | collective-permute-start | bytes 393224 | tf_op jit(solution)/shard_map/ppermute | solution.py:29
  29.6 1.8 %collective-permute-start.10 = (bf16[64,1024]{1,0:T(8,128)(2,1)S(1)}, bf16[64,1024]{1,0:T(8,128)(2,1)S(1)}, u32[]{:S(2)}, u32[]{:S(2)}) collective-permute-start(bf16[64,1024]{1,0:T(8,128)(2,1)S(1)} %get-tuple-element.123), channel_id=1, source_target_pairs={{0,1},{1,0},{2,3},{3,2},{4,5},{5,4},{6,7},{7,6},{8,9},{9,8},{10,11... | collective-permute-start | bytes 393224 | tf_op jit(solution)/shard_map/ppermute | solution.py:29
  30.0 1.5 %collective-permute-start.11 = (f32[64,64]{1,0:T(8,128)S(1)}, f32[64,64]{1,0:T(8,128)S(1)}, u32[]{:S(2)}, u32[]{:S(2)}) collective-permute-start(f32[64,64]{1,0:T(8,128)S(1)} %get-tuple-element.126.refs_6_), channel_id=1, source_target_pairs={{0,1},{1,0},{2,3},{3,2},{4,5},{5,4},{6,7},{7,6},{8,9},{9,8},{10,11... | collective-permute-start | bytes 49160 | tf_op jit(solution)/shard_map/ppermute | solution.py:47
  30.3 7.3 %collective-permute-start.12 = (bf16[64,1024]{1,0:T(8,128)(2,1)S(1)}, bf16[64,1024]{1,0:T(8,128)(2,1)S(1)}, u32[]{:S(2)}, u32[]{:S(2)}) collective-permute-start(bf16[64,1024]{1,0:T(8,128)(2,1)S(1)} %get-tuple-element.128), channel_id=1, source_target_pairs={{0,8},{1,2},{2,1},{3,4},{4,3},{5,6},{6,5},{7,15},{8,0},{9,10},{10,... | collective-permute-start | bytes 393224 | tf_op jit(solution)/shard_map/ppermute | solution.py:29
  34.4 5.1 %collective-permute-start.13 = (bf16[64,1024]{1,0:T(8,128)(2,1)S(1)}, bf16[64,1024]{1,0:T(8,128)(2,1)S(1)}, u32[]{:S(2)}, u32[]{:S(2)}) collective-permute-start(bf16[64,1024]{1,0:T(8,128)(2,1)S(1)} %get-tuple-element.131), channel_id=1, source_target_pairs={{0,1},{1,0},{2,3},{3,2},{4,5},{5,4},{6,7},{7,6},{8,9},{9,8},{10,11... | collective-permute-start | bytes 393224 | tf_op jit(solution)/shard_map/ppermute | solution.py:29
  35.4 4.1 %collective-permute-start.14 = (f32[64,64]{1,0:T(8,128)S(1)}, f32[64,64]{1,0:T(8,128)S(1)}, u32[]{:S(2)}, u32[]{:S(2)}) collective-permute-start(f32[64,64]{1,0:T(8,128)S(1)} %get-tuple-element.134.refs_6_), channel_id=1, source_target_pairs={{0,2},{1,3},{2,0},{3,1},{4,6},{5,7},{6,4},{7,5},{8,10},{9,11},{10,... | collective-permute-start | bytes 49160 | tf_op jit(solution)/shard_map/ppermute | solution.py:47
  37.6 5.0 %collective-permute-start.15 = (bf16[64,1024]{1,0:T(8,128)(2,1)S(1)}, bf16[64,1024]{1,0:T(8,128)(2,1)S(1)}, u32[]{:S(2)}, u32[]{:S(2)}) collective-permute-start(bf16[64,1024]{1,0:T(8,128)(2,1)S(1)} %get-tuple-element.136), channel_id=1, source_target_pairs={{0,8},{1,2},{2,1},{3,4},{4,3},{5,6},{6,5},{7,15},{8,0},{9,10},{10,... | collective-permute-start | bytes 393224 | tf_op jit(solution)/shard_map/ppermute | solution.py:29
  42.5 4.6 %collective-permute-start.16 = (bf16[64,1024]{1,0:T(8,128)(2,1)S(1)}, bf16[64,1024]{1,0:T(8,128)(2,1)S(1)}, u32[]{:S(2)}, u32[]{:S(2)}) collective-permute-start(bf16[64,1024]{1,0:T(8,128)(2,1)S(1)} %get-tuple-element.139), channel_id=1, source_target_pairs={{0,1},{1,0},{2,3},{3,2},{4,5},{5,4},{6,7},{7,6},{8,9},{9,8},{10,11... | collective-permute-start | bytes 393224 | tf_op jit(solution)/shard_map/ppermute | solution.py:29
  42.9 10.5 %collective-permute-start.17 = (bf16[64,1024]{1,0:T(8,128)(2,1)S(1)}, bf16[64,1024]{1,0:T(8,128)(2,1)S(1)}, u32[]{:S(2)}, u32[]{:S(2)}) collective-permute-start(bf16[64,1024]{1,0:T(8,128)(2,1)S(1)} %get-tuple-element.143), channel_id=1, source_target_pairs={{0,8},{1,2},{2,1},{3,4},{4,3},{5,6},{6,5},{7,15},{8,0},{9,10},{10,... | collective-permute-start | bytes 393224 | tf_op jit(solution)/shard_map/ppermute | solution.py:29
  44.2 6.7 %collective-permute-start.18 = (f32[64,64]{1,0:T(8,128)S(1)}, f32[64,64]{1,0:T(8,128)S(1)}, u32[]{:S(2)}, u32[]{:S(2)}) collective-permute-start(f32[64,64]{1,0:T(8,128)S(1)} %get-tuple-element.144.refs_0_), channel_id=1, source_target_pairs={{0,4},{1,5},{2,6},{3,7},{4,0},{5,1},{6,2},{7,3},{8,12},{9,13},{10,... | collective-permute-start | bytes 49160 | tf_op jit(solution)/shard_map/ppermute | solution.py:47
  54.1 4.3 %collective-permute-start.19 = (bf16[2,16,1024]{2,1,0:T(8,128)(2,1)S(1)}, bf16[2,16,1024]{2,1,0:T(8,128)(2,1)S(1)}, u32[]{:S(2)}, u32[]{:S(2)}) collective-permute-start(bf16[2,16,1024]{2,1,0:T(8,128)(2,1)S(1)} %get-tuple-element.151), channel_id=1, source_target_pairs={{0,24},{8,0},{16,8},{24,16},{1,25},{9,1},{17,9},{25,17},{2,26},{10... | collective-permute-start | bytes 196616 | tf_op jit(solution)/shard_map/ppermute | solution.py:38
  58.7 1.3 %collective-permute-start.20 = (f32[64,96]{1,0:T(8,128)S(1)}, f32[64,96]{1,0:T(8,128)S(1)}, u32[]{:S(2)}, u32[]{:S(2)}) collective-permute-start(f32[64,96]{1,0:T(8,128)S(1)} %shard_map.64), channel_id=1, source_target_pairs={{0,1},{1,0},{2,3},{3,2},{4,5},{5,4},{6,7},{7,6},{8,9},{9,8},{10,11... | collective-permute-start | bytes 73736 | tf_op jit(solution)/shard_map/ppermute | solution.py:47
  60.0 5.7 %collective-permute-start.23 = (f32[64,96]{1,0:T(8,128)S(1)}, f32[64,96]{1,0:T(8,128)S(1)}, u32[]{:S(2)}, u32[]{:S(2)}) collective-permute-start(f32[64,96]{1,0:T(8,128)S(1)} %add.3.refs_0_), channel_id=1, source_target_pairs={{0,6},{1,7},{2,4},{3,5},{4,2},{5,3},{6,0},{7,1},{8,14},{9,15},{10,... | collective-permute-start | bytes 73736 | tf_op jit(solution)/shard_map/ppermute | solution.py:47
  62.2 4.9 %collective-permute-start.22 = (f32[64,96]{1,0:T(8,128)S(1)}, f32[64,96]{1,0:T(8,128)S(1)}, u32[]{:S(2)}, u32[]{:S(2)}) collective-permute-start(f32[64,96]{1,0:T(8,128)S(1)} %add.3.refs_0_), channel_id=1, source_target_pairs={{0,4},{1,5},{2,6},{3,7},{4,0},{5,1},{6,2},{7,3},{8,12},{9,13},{10,... | collective-permute-start | bytes 73736 | tf_op jit(solution)/shard_map/ppermute | solution.py:47
  62.6 4.5 %collective-permute-start.21 = (f32[64,96]{1,0:T(8,128)S(1)}, f32[64,96]{1,0:T(8,128)S(1)}, u32[]{:S(2)}, u32[]{:S(2)}) collective-permute-start(f32[64,96]{1,0:T(8,128)S(1)} %add.3.refs_0_), channel_id=1, source_target_pairs={{0,2},{1,3},{2,0},{3,1},{4,6},{5,7},{6,4},{7,5},{8,10},{9,11},{10,... | collective-permute-start | bytes 73736 | tf_op jit(solution)/shard_map/ppermute | solution.py:47
  69.8 5.4 %collective-permute-start.24 = (bf16[2,16,1024]{2,1,0:T(8,128)(2,1)S(1)}, bf16[2,16,1024]{2,1,0:T(8,128)(2,1)S(1)}, u32[]{:S(2)}, u32[]{:S(2)}) collective-permute-start(bf16[2,16,1024]{2,1,0:T(8,128)(2,1)S(1)} %get-tuple-element.156), channel_id=1, source_target_pairs={{0,8},{8,16},{16,24},{24,0},{1,9},{9,17},{17,25},{25,1},{2,10},{10... | collective-permute-start | bytes 196616 | tf_op jit(solution)/shard_map/ppermute | solution.py:38

commit v2 on v1

--- a/solution.py
+++ b/solution.py
@@ -44,7 +44,8 @@
 
 
 def swapped(block, reach):
-    return lax.ppermute(block, "layer", [(i, i ^ reach) for i in range(lax.axis_size("layer"))])
+    far = reach | 1
+    return lax.ppermute(block, "layer", [(i, i ^ far) for i in range(lax.axis_size("layer"))])
 
 
 def partial_sums(block):
@@ -255,23 +256,34 @@
     send_outer(position("layer") % 2, next16_ref, last_ref, send_ref)
 
 
-def normal_kernel(parts, length, *refs):
-    grams, (rest_ref, inverse_ref, next_ref, next16_ref, gram_ref) = refs[:parts], refs[parts:]
-    inverse_ref[...] = inverse_factor(sum(ref[...] for ref in grams) * (1.0 / length))
+def identity(size):
+    row = lax.broadcasted_iota(jnp.int32, (size, size), 0)
+    column = lax.broadcasted_iota(jnp.int32, (size, size), 1)
+    return jnp.where(row == column, 1.0, 0.0)
+
+
+def row_scales(gram):
+    return lax.rsqrt(jnp.sum(gram * identity(gram.shape[0]), axis=1, keepdims=True))
+
+
+def scale_kernel(parts, length, *refs):
+    grams, (rest_ref, next_ref, next16_ref, gram_ref, scales_ref) = refs[:parts], refs[parts:]
+    scales = row_scales(sum(ref[...] for ref in grams) * (1.0 / length))
+    scales_ref[...] = jnp.broadcast_to(scales, scales_ref.shape)
     gram_ref[...] = jnp.zeros(gram_ref.shape, F32)
     for i in range(rest_ref.shape[0]):
-        block = exact(inverse_ref[...], rest_ref[i])
+        block = rest_ref[i] * scales
         next_ref[i] = block
         next16_ref[i] = block.astype(BF16)
         gram_ref[...] += product_t(block, block, HIGHEST)
 
 
 def last_kernel(
-    count, rows_ref, base_ref, arrived_ref, last_t_ref, inverse_ref, rest16_ref, rest_gram_ref,
+    count, rows_ref, base_ref, arrived_ref, last_t_ref, scales_ref, rest16_ref, rest_gram_ref,
     next_ref, next16_ref, low_ref, gram_ref,
 ):
     def store(block):
-        next_ref[...] = exact(inverse_ref[...], block)
+        next_ref[...] = block * scales_ref[:, :1]
 
     finish(count, False, rows_ref, base_ref, arrived_ref, last_t_ref, store)
     next16_ref[...] = next_ref[...].astype(BF16)
@@ -282,8 +294,16 @@
     gram_ref[...] = rest_gram_ref[...] + product_t(next_ref[...], next_ref[...], HIGHEST)
 
 
+def first_factor_kernel(parts, length, *refs):
+    grams, (_, inverse_ref) = refs[:parts], refs[parts:]
+    gram = sum(ref[...] for ref in grams) * (1.0 / length)
+    scales = row_scales(gram)
+    across = jnp.sum(identity(gram.shape[0]) * scales, axis=0, keepdims=True)
+    inverse_ref[...] = inverse_factor(gram * scales * across)
+
+
 def cross_kernel(gram_ref, outer16_ref, rest16_ref, above_ref, out_ref):
-    size, edge = gram_ref.shape[0], above_ref.shape[1]
+    size, edge = outer16_ref.shape[0], above_ref.shape[1]
     rest = range(rest16_ref.shape[0])
     out_ref[:, :size] = gram_ref[...]
     out_ref[:, size : size + edge] = product_t(outer16_ref[...], above_ref[0]) + sum(
@@ -296,42 +316,47 @@
 
 
 def factor_kernel(parts, length, slices, *refs):
-    grams, (outer_ref, rest_ref, inverse_ref, weights_ref, up_ref) = refs[:parts], refs[parts:]
+    grams, (first_ref, outer_ref, rest_ref, inverse_ref, weights_ref, up_ref) = refs[:parts], refs[parts:]
     size, edge = outer_ref.shape[0], up_ref.shape[1]
+    first = first_ref[...]
     total = sum(ref[...] for ref in grams) * (1.0 / length)
     has_above = (position("cuts") < slices - 1).astype(F32)
-    row = lax.broadcasted_iota(jnp.int32, (edge, edge), 0)
-    column = lax.broadcasted_iota(jnp.int32, (edge, edge), 1)
-    identity = jnp.where(row == column, 1.0, 0.0)
-    above_gram = total[:edge, size + edge :] * has_above + identity * (1.0 - has_above)
-    own = inverse_factor(total[:, :size])
-    above = inverse_factor(above_gram)
+    above = total[:edge, size + edge :] * has_above + identity(edge) * (1.0 - has_above)
+    above = inverse_factor(above)
+    own = product_t(exact(first, total[:, :size]), first, HIGHEST)
+    own = exact(inverse_factor(own), first)
     inverse_ref[...] = own
     high = own[size - edge :]
     correlation = product_t(exact(high, total[:, size : size + edge]), above, HIGHEST) * has_above
-    weights_ref[...] = exact(correlation, above)
     up = exact(correlation.T, high)
     up_ref[0] = exact(up, outer_ref[...]).astype(BF16)
     for i in range(rest_ref.shape[0]):
         up_ref[i + 1] = exact(up, rest_ref[i]).astype(BF16)
-
-
-def final_kernel(slices, inverse_ref, weights_ref, outer_ref, rest_ref, above_ref, below_ref, out_ref):
-    size, edge = outer_ref.shape[0], above_ref.shape[1]
-    layers = above_ref.shape[0]
-    has_below = (position("cuts") > 0).astype(F32)
-    blocks = []
+    weights_ref[...] = exact(correlation, above)
+
+
+def vectors_kernel(inverse_ref, weights_ref, outer_ref, rest_ref, above_ref, all_ref):
+    layers, size, _ = all_ref.shape
+    edge = above_ref.shape[1]
     for i in range(layers):
         block = exact(inverse_ref[...], rest_ref[i - 1] if i else outer_ref[...])
-        high = block[size - edge :] - exact(weights_ref[...], above_ref[i].astype(F32))
-        low = block[:edge] - below_ref[i].astype(F32) * has_below
-        blocks.append(jnp.concatenate([low, block[edge : size - edge], high], 0))
+        all_ref[i] = block
+        all_ref[i, size - edge :] = block[size - edge :] - exact(
+            weights_ref[...], above_ref[i].astype(F32)
+        )
+
+
+def final_kernel(all_ref, below_ref, out_ref):
+    layers, size, _ = all_ref.shape
+    edge = below_ref.shape[1]
+    has_below = (position("cuts") > 0).astype(F32)
     for parity in (0, 1):
 
         @pl.when(position("layer") % 2 == parity)
         def _():
             for i, l in enumerate(range(layers)[:: -1 if parity else 1]):
-                out_ref[:, l, :] = blocks[i]
+                out_ref[:edge, l, :] = all_ref[i, :edge] - below_ref[i].astype(F32) * has_below
+                out_ref[edge:, l, :] = all_ref[i, edge:]
 
 
 def per_device(vectors, diag_blocks, couplings, bounds):
@@ -414,28 +439,31 @@
     totals = [total]
     for reach in reaches:
         totals = [sum(totals), swapped(sum(totals), reach)]
-    inverse, rest, rest_r, rest_gram = call(
-        functools.partial(normal_kernel, len(totals), length_all),
-        (square, rest32, rest16, square), *totals, rest_next,
+    rest, rest_r, rest_gram, scales = call(
+        functools.partial(scale_kernel, len(totals), length_all),
+        (rest32, rest16, square, array(F32, count_vec, 128)), *totals, rest_next,
     )
     outer, outer_r, low, gram = call(
         functools.partial(last_kernel, count), (outer32, outer16, edges, square),
-        rows, base, outer_in, last_t, inverse, rest_r, rest_gram,
+        rows, base, outer_in, last_t, scales, rest_r, rest_gram,
     )
     above = rotated(low, -1)
+    first = call(
+        functools.partial(first_factor_kernel, len(totals), length_all), square, *totals, gram
+    )
     cross = call(
         cross_kernel, array(F32, count_vec, count_vec + 2 * EDGE), gram, outer_r, rest_r, above
     )
     grams = partial_sums(cross)
     inverse, weights, up = call(
         functools.partial(factor_kernel, len(grams), length_all, slices),
-        (square, array(F32, EDGE, EDGE), edges), *grams, outer, rest,
+        (square, array(F32, EDGE, EDGE), edges), *grams, first, outer, rest,
     )
     below = rotated(up, 1)
-    result = call(
-        functools.partial(final_kernel, slices),
-        array(F32, count_vec, layers, width), inverse, weights, outer, rest, above, below,
-    )
+    vectors_all = call(
+        vectors_kernel, array(F32, layers, count_vec, width), inverse, weights, outer, rest, above
+    )
+    result = call(final_kernel, array(F32, count_vec, layers, width), vectors_all, below)
     return result[None]
 
 

time: 77 us -> 73.5 us (0.955)
  waiting for transfers between devices: 12.5 us -> 9.71 us
    ppermute x7, waiting for transfers between devices: 5.29 us -> 2.39 us  [swapped(): lax.ppermute(block, 'layer', [(i, i ^ far) for i in range(lax.axis_size('...]
    ppermute x7, starting transfers between devices: 9.68 us -> 8.71 us  [swapped(): lax.ppermute(block, 'layer', [(i, i ^ far) for i in range(lax.axis_size('...]
    pallas_call x21 -> x23, Pallas kernels: 36 us -> 35.9 us  [call(): pl.pallas_call(kernel, out_shape=outs, in_specs=[HBM if i in far else VME...]
  transfers between devices with their start and end apart: 25 -> 25, of which waited for: 11 -> 9; matrix products, arithmetic and copies ran while one was open for 0% -> 0% of each run, Pallas kernels for 37% -> 39%
where the time goes in v2:
time: 73.5 us; the launch traced here: 73.3 us
  Pallas kernels  35.9 us (49%)
  starting transfers between devices  27.5 us (37%)
  waiting for transfers between devices  9.71 us (13%)
    pallas_call x23, Pallas kernels, call(): pl.pallas_call(kernel, out_shape=outs, in_specs=[HBM if i in far else VME...  35.9 us
    ppermute x16, starting transfers between devices, exchanged(): return lax.ppermute(block, ('cuts', 'layer'), route)  14 us
    ppermute x7, starting transfers between devices, swapped(): lax.ppermute(block, 'layer', [(i, i ^ far) for i in range(lax.axis_size('...  8.71 us
    ppermute x2, waiting for transfers between devices, rotated(): lax.ppermute(block, 'cuts', [(i, (i + distance) % size) for i in range(si...  5.07 us
    ppermute x2, starting transfers between devices, rotated(): lax.ppermute(block, 'cuts', [(i, (i + distance) % size) for i in range(si...  4.78 us
    ppermute x7, waiting for transfers between devices, swapped(): lax.ppermute(block, 'layer', [(i, i ^ far) for i in range(lax.axis_size('...  2.39 us
    ppermute x16, waiting for transfers between devices, exchanged(): return lax.ppermute(block, ('cuts', 'layer'), route)  2.25 us
  transfers between devices with their start and end apart: 25, of which 9 were waited for; matrix products, arithmetic and copies ran while one was open for 0% of the time, Pallas kernels for 39%

profile of v2, /device:TPU:0, one launch (start us, length us, event | category | flops | bytes accessed | tf_op | source)
XLA Modules:
  0.0 73.3 jit_solution(7691134676744637893)
XLA Ops:
  0.0 2.6 %shard_map.46 = (f32[64,1024]{1,0:T(8,128)S(1)}, f32[1,64,1024]{2,1,0:T(8,128)S(1)}, bf16[64,1024]{1,0:T(8,128)(2,1)S(1)}, bf16[1,64,1024]{2,1,0:T(8,128)(2,1)S(...) custom-call(s32[1,2]{1,0:T(1,128)} %far_bounds_ref.1, ...), custom_call_target="tpu_custom_call" | custom-call | flops 134217728 | bytes 4718600 | tf_op jit(solution)/shard_map/pallas_call | solution.py:381
  2.6 0.5 collective-permute-start
  3.1 2.6 %collective-permute-start.1 = (bf16[64,1024]{1,0:T(8,128)(2,1)S(1)}, bf16[64,1024]{1,0:T(8,128)(2,1)S(1)}, u32[]{:S(2)}, u32[]{:S(2)}) collective-permute-start(bf16[64,1024]{1,0:T(8,128)(2,1)S(1)} %get-tuple-element.90), channel_id=1, source_target_pairs={{0,8},{1,2},{2,1},{3,4},{4,3},{5,6},{6,5},{7,15},{8,0},{9,10},{10,... | collective-permute-start | bytes 393224 | tf_op jit(solution)/shard_map/ppermute | solution.py:29
  5.7 0.0 collective-permute-done.arrived_ref
  5.7 3.7 %shard_map.47 = (f32[64,1024]{1,0:T(8,128)S(1)}, f32[1,64,1024]{2,1,0:T(8,128)S(1)}, bf16[1,64,1024]{2,1,0:T(8,128)(2,1)S(1)}, bf16[64,1024]{1,0:T(8,128)(2,1)S(...) custom-call(f32[8,1024]{1,0:T(8,128)S(1)} %get-tuple-element.81.rows_ref, ...), custom_call_target="tpu_custom_call" | custom-call | flops 671088640 | bytes 9863168 | tf_op jit(solution)/shard_map/pallas_call | solution.py:381
  9.4 0.1 collective-permute-start.2
  9.5 0.0 collective-permute-done.1.arrived_ref
  9.5 0.1 shard_map.48
  9.6 1.3 %collective-permute-start.3 = (bf16[64,1024]{1,0:T(8,128)(2,1)S(1)}, bf16[64,1024]{1,0:T(8,128)(2,1)S(1)}, u32[]{:S(2)}, u32[]{:S(2)}) collective-permute-start(bf16[64,1024]{1,0:T(8,128)(2,1)S(1)} %get-tuple-element.99), channel_id=1, source_target_pairs={{0,8},{1,2},{2,1},{3,4},{4,3},{5,6},{6,5},{7,15},{8,0},{9,10},{10,... | collective-permute-start | bytes 393224 | tf_op jit(solution)/shard_map/ppermute | solution.py:29
  10.9 0.0 collective-permute-done.2.arrived_ref
  10.9 2.9 %shard_map.49 = (f32[64,1024]{1,0:T(8,128)S(1)}, f32[1,64,1024]{2,1,0:T(8,128)S(1)}, bf16[1,64,1024]{2,1,0:T(8,128)(2,1)S(1)}, bf16[64,1024]{1,0:T(8,128)(2,1)S(1)}) custom-call(f32[8,1024]{1,0:T(8,128)S(1)} %get-tuple-element.81.rows_ref, bf16[64,1024]{1,0:T(8,128)(2,1)S(1)} %get-tuple-element.92.outer16_ref, ...), custom_call_target="tpu_custom_call" | custom-call | flops 671088640 | bytes 14057472 | tf_op jit(solution)/shard_map/pallas_call | solution.py:381
  13.9 0.1 collective-permute-start.4
  13.9 0.7 collective-permute-done.3.arrived_ref
  14.7 1.3 %collective-permute-start.5 = (bf16[64,1024]{1,0:T(8,128)(2,1)S(1)}, bf16[64,1024]{1,0:T(8,128)(2,1)S(1)}, u32[]{:S(2)}, u32[]{:S(2)}) collective-permute-start(bf16[64,1024]{1,0:T(8,128)(2,1)S(1)} %get-tuple-element.106), channel_id=1, source_target_pairs={{0,8},{1,2},{2,1},{3,4},{4,3},{5,6},{6,5},{7,15},{8,0},{9,10},{10,... | collective-permute-start | bytes 393224 | tf_op jit(solution)/shard_map/ppermute | solution.py:29
  16.0 0.0 collective-permute-done.4.arrived_ref
  16.0 2.9 %shard_map.51 = (f32[64,1024]{1,0:T(8,128)S(1)}, f32[1,64,1024]{2,1,0:T(8,128)S(1)}, bf16[1,64,1024]{2,1,0:T(8,128)(2,1)S(1)}, bf16[64,1024]{1,0:T(8,128)(2,1)S(1)}) custom-call(f32[8,1024]{1,0:T(8,128)S(1)} %get-tuple-element.81.rows_ref, bf16[64,1024]{1,0:T(8,128)(2,1)S(1)} %get-tuple-element.100.outer16_ref, ...), custom_call_target="tpu_custom_call" | custom-call | flops 671088640 | bytes 14057472 | tf_op jit(solution)/shard_map/pallas_call | solution.py:381
  18.9 0.1 collective-permute-start.6
  19.0 0.7 collective-permute-done.5.arrived_ref
  19.7 1.3 %collective-permute-start.7 = (bf16[64,1024]{1,0:T(8,128)(2,1)S(1)}, bf16[64,1024]{1,0:T(8,128)(2,1)S(1)}, u32[]{:S(2)}, u32[]{:S(2)}) collective-permute-start(bf16[64,1024]{1,0:T(8,128)(2,1)S(1)} %get-tuple-element.113), channel_id=1, source_target_pairs={{0,8},{1,2},{2,1},{3,4},{4,3},{5,6},{6,5},{7,15},{8,0},{9,10},{10,... | collective-permute-start | bytes 393224 | tf_op jit(solution)/shard_map/ppermute | solution.py:29
  21.1 0.0 collective-permute-done.6.arrived_ref
  21.1 3.1 %shard_map.53 = (f32[64,1024]{1,0:T(8,128)S(1)}, f32[1,64,1024]{2,1,0:T(8,128)S(1)}, bf16[1,64,1024]{2,1,0:T(8,128)(2,1)S(1)}, bf16[64,1024]{1,0:T(8,128)(2,1)S(1)}) custom-call(f32[8,1024]{1,0:T(8,128)S(1)} %get-tuple-element.81.rows_ref, bf16[64,1024]{1,0:T(8,128)(2,1)S(1)} %get-tuple-element.107.outer16_ref, ...), custom_call_target="tpu_custom_call" | custom-call | flops 671088640 | bytes 14057472 | tf_op jit(solution)/shard_map/pallas_call | solution.py:381
  24.2 0.1 collective-permute-start.8
  24.3 0.5 collective-permute-done.7.arrived_ref
  24.8 1.3 %collective-permute-start.9 = (bf16[64,1024]{1,0:T(8,128)(2,1)S(1)}, bf16[64,1024]{1,0:T(8,128)(2,1)S(1)}, u32[]{:S(2)}, u32[]{:S(2)}) collective-permute-start(bf16[64,1024]{1,0:T(8,128)(2,1)S(1)} %get-tuple-element.120), channel_id=1, source_target_pairs={{0,8},{1,2},{2,1},{3,4},{4,3},{5,6},{6,5},{7,15},{8,0},{9,10},{10,... | collective-permute-start | bytes 393224 | tf_op jit(solution)/shard_map/ppermute | solution.py:29
  26.1 0.0 collective-permute-done.8.arrived_ref
  26.2 3.5 %shard_map.55 = (f32[64,1024]{1,0:T(8,128)S(1)}, f32[1,64,1024]{2,1,0:T(8,128)S(1)}, bf16[1,64,1024]{2,1,0:T(8,128)(2,1)S(1)}, bf16[64,1024]{1,0:T(8,128)(2,1)S(1)}, f32[64,64]{1,0:T(8,128)S(1)}) custom-call(f32[8,1024]{1,0:T(8,128)S(1)} %get-tuple-element.81.rows_ref, bf16[64,1024]{1,0:T(8,128)(2,1)S(1)} %get-tuple-element.114.outer16_ref, ...), custom_call_target="tpu_custom_call" | custom-call | flops 671088640 | bytes 14057472 | tf_op jit(solution)/shard_map/pallas_call | solution.py:381
  29.6 0.4 collective-permute-start.10
  30.0 0.2 collective-permute-start.11
  30.2 0.0 collective-permute-done.9.arrived_ref
  30.3 1.2 %collective-permute-start.12 = (bf16[64,1024]{1,0:T(8,128)(2,1)S(1)}, bf16[64,1024]{1,0:T(8,128)(2,1)S(1)}, u32[]{:S(2)}, u32[]{:S(2)}) collective-permute-start(bf16[64,1024]{1,0:T(8,128)(2,1)S(1)} %get-tuple-element.128), channel_id=1, source_target_pairs={{0,8},{1,2},{2,1},{3,4},{4,3},{5,6},{6,5},{7,15},{8,0},{9,10},{10,... | collective-permute-start | bytes 393224 | tf_op jit(solution)/shard_map/ppermute | solution.py:29
  31.5 0.0 collective-permute-done.11.refs_7_
  31.5 0.0 collective-permute-done.10.arrived_ref
  31.5 2.9 %shard_map.57 = (f32[64,1024]{1,0:T(8,128)S(1)}, f32[1,64,1024]{2,1,0:T(8,128)S(1)}, bf16[1,64,1024]{2,1,0:T(8,128)(2,1)S(1)}, bf16[64,1024]{1,0:T(8,128)(2,1)S(1)}, f32[64,64]{1,0:T(8,128)S(1)}) custom-call(f32[8,1024]{1,0:T(8,128)S(1)} %get-tuple-element.81.rows_ref, bf16[64,1024]{1,0:T(8,128)(2,1)S(1)} %get-tuple-element.121.outer16_ref, ...), custom_call_target="tpu_custom_call" | custom-call | flops 671088640 | bytes 14090240 | tf_op jit(solution)/shard_map/pallas_call | solution.py:381
  34.4 1.0 %collective-permute-start.13 = (bf16[64,1024]{1,0:T(8,128)(2,1)S(1)}, bf16[64,1024]{1,0:T(8,128)(2,1)S(1)}, u32[]{:S(2)}, u32[]{:S(2)}) collective-permute-start(bf16[64,1024]{1,0:T(8,128)(2,1)S(1)} %get-tuple-element.131), channel_id=1, source_target_pairs={{0,1},{1,0},{2,3},{3,2},{4,5},{5,4},{6,7},{7,6},{8,9},{9,8},{10,11... | collective-permute-start | bytes 393224 | tf_op jit(solution)/shard_map/ppermute | solution.py:29
  35.4 2.2 %collective-permute-start.14 = (f32[64,64]{1,0:T(8,128)S(1)}, f32[64,64]{1,0:T(8,128)S(1)}, u32[]{:S(2)}, u32[]{:S(2)}) collective-permute-start(f32[64,64]{1,0:T(8,128)S(1)} %get-tuple-element.134.refs_6_), channel_id=1, source_target_pairs={{0,3},{1,2},{2,1},{3,0},{4,7},{5,6},{6,5},{7,4},{8,11},{9,10},{10,... | collective-permute-start | bytes 49160 | tf_op jit(solution)/shard_map/ppermute | solution.py:48
  37.6 0.0 collective-permute-done.12.arrived_ref
  37.6 1.3 %collective-permute-start.15 = (bf16[64,1024]{1,0:T(8,128)(2,1)S(1)}, bf16[64,1024]{1,0:T(8,128)(2,1)S(1)}, u32[]{:S(2)}, u32[]{:S(2)}) collective-permute-start(bf16[64,1024]{1,0:T(8,128)(2,1)S(1)} %get-tuple-element.136), channel_id=1, source_target_pairs={{0,8},{1,2},{2,1},{3,4},{4,3},{5,6},{6,5},{7,15},{8,0},{9,10},{10,... | collective-permute-start | bytes 393224 | tf_op jit(solution)/shard_map/ppermute | solution.py:29
  39.0 0.3 collective-permute-done.14.refs_7_
  39.3 0.0 collective-permute-done.13.arrived_ref
  39.3 2.9 %shard_map.59 = (f32[64,1024]{1,0:T(8,128)S(1)}, f32[1,64,1024]{2,1,0:T(8,128)S(1)}, bf16[1,64,1024]{2,1,0:T(8,128)(2,1)S(1)}, bf16[64,1024]{1,0:T(8,128)(2,1)S(1)}, f32[64,64]{1,0:T(8,128)S(1)}) custom-call(f32[8,1024]{1,0:T(8,128)S(1)} %get-tuple-element.81.rows_ref, bf16[64,1024]{1,0:T(8,128)(2,1)S(1)} %get-tuple-element.129.outer16_ref, ...), custom_call_target="tpu_custom_call" | custom-call | flops 671088640 | bytes 14090240 | tf_op jit(solution)/shard_map/pallas_call | solution.py:381
  42.2 0.1 collective-permute-start.16
  42.3 0.4 collective-permute-done.15.arrived_ref
  42.7 1.3 %collective-permute-start.17 = (bf16[64,1024]{1,0:T(8,128)(2,1)S(1)}, bf16[64,1024]{1,0:T(8,128)(2,1)S(1)}, u32[]{:S(2)}, u32[]{:S(2)}) collective-permute-start(bf16[64,1024]{1,0:T(8,128)(2,1)S(1)} %get-tuple-element.143), channel_id=1, source_target_pairs={{0,8},{1,2},{2,1},{3,4},{4,3},{5,6},{6,5},{7,15},{8,0},{9,10},{10,... | collective-permute-start | bytes 393224 | tf_op jit(solution)/shard_map/ppermute | solution.py:29
  44.0 2.3 %collective-permute-start.18 = (f32[64,64]{1,0:T(8,128)S(1)}, f32[64,64]{1,0:T(8,128)S(1)}, u32[]{:S(2)}, u32[]{:S(2)}) collective-permute-start(f32[64,64]{1,0:T(8,128)S(1)} %get-tuple-element.144.refs_0_), channel_id=1, source_target_pairs={{0,5},{1,4},{2,7},{3,6},{4,1},{5,0},{6,3},{7,2},{8,13},{9,12},{10,... | collective-permute-start | bytes 49160 | tf_op jit(solution)/shard_map/ppermute | solution.py:48
  46.4 0.0 collective-permute-done.16.arrived_ref
  46.4 3.1 %shard_map.61 = (f32[64,1024]{1,0:T(8,128)S(1)}, f32[1,64,1024]{2,1,0:T(8,128)S(1)}, bf16[1,64,1024]{2,1,0:T(8,128)(2,1)}) custom-call(f32[8,1024]{1,0:T(8,128)S(1)} %get-tuple-element.81.rows_ref, bf16[64,1024]{1,0:T(8,128)(2,1)S(1)} %get-tuple-element.137.outer16_ref, bf16[1,64,1024]{2,1,0:T(8,128)(2,1)S(1)} %get-tuple-element.138.rest16_ref, ...), custom_call_target="tpu_custom_call" | custom-call | flops 671088640 | bytes 14057472 | tf_op jit(solution)/shard_map/pallas_call | solution.py:381
  49.5 0.4 shard_map.62
  49.9 0.5 shard_map.63
  50.4 2.5 %collective-permute-start.19 = (bf16[2,16,1024]{2,1,0:T(8,128)(2,1)S(1)}, bf16[2,16,1024]{2,1,0:T(8,128)(2,1)S(1)}, u32[]{:S(2)}, u32[]{:S(2)}) collective-permute-start(bf16[2,16,1024]{2,1,0:T(8,128)(2,1)S(1)} %get-tuple-element.151), channel_id=1, source_target_pairs={{0,24},{8,0},{16,8},{24,16},{1,25},{9,1},{17,9},{25,17},{2,26},{10... | collective-permute-start | bytes 196616 | tf_op jit(solution)/shard_map/ppermute | solution.py:38
  52.9 2.4 %collective-permute-done.19.above_ref = bf16[2,16,1024]{2,1,0:T(8,128)(2,1)S(1)} collective-permute-done((bf16[2,16,1024]{2,1,0:T(8,128)(2,1)S(1)}, bf16[2,16,1024]{2,1,0:T(8,128)(2,1)S(1)}, u32[]{:S(2)}, u32[]{:S(2)}) %collective-permute-start.19) | collective-permute-done | bytes 65568 | tf_op jit(solution)/shard_map/ppermute | solution.py:38
  55.3 0.3 shard_map.64
  55.6 0.1 collective-permute-start.20
  55.7 1.1 %collective-permute-done.20 = f32[64,96]{1,0:T(8,128)S(1)} collective-permute-done((f32[64,96]{1,0:T(8,128)S(1)}, f32[64,96]{1,0:T(8,128)S(1)}, u32[]{:S(2)}, u32[]{:S(2)}) %collective-permute-start.20) | collective-permute-done | bytes 24608 | tf_op jit(solution)/shard_map/ppermute | solution.py:48
  56.8 2.4 %collective-permute-start.23 = (f32[64,96]{1,0:T(8,128)S(1)}, f32[64,96]{1,0:T(8,128)S(1)}, u32[]{:S(2)}, u32[]{:S(2)}) collective-permute-start(f32[64,96]{1,0:T(8,128)S(1)} %add.3.refs_0_), channel_id=1, source_target_pairs={{0,7},{1,6},{2,5},{3,4},{4,3},{5,2},{6,1},{7,0},{8,15},{9,14},{10,... | collective-permute-start | bytes 73736 | tf_op jit(solution)/shard_map/ppermute | solution.py:48
  59.2 0.5 collective-permute-start.22
  59.7 1.0 %collective-permute-start.21 = (f32[64,96]{1,0:T(8,128)S(1)}, f32[64,96]{1,0:T(8,128)S(1)}, u32[]{:S(2)}, u32[]{:S(2)}) collective-permute-start(f32[64,96]{1,0:T(8,128)S(1)} %add.3.refs_0_), channel_id=1, source_target_pairs={{0,3},{1,2},{2,1},{3,0},{4,7},{5,6},{6,5},{7,4},{8,11},{9,10},{10,... | collective-permute-start | bytes 73736 | tf_op jit(solution)/shard_map/ppermute | solution.py:48
  60.7 1.9 %shard_map.65.refs_4_ = f32[64,64]{1,0:T(8,128)S(1)} custom-call(f32[64,64]{1,0:T(8,128)S(1)} %get-tuple-element.144.refs_0_, f32[64,64]{1,0:T(8,128)S(1)} %collective-permute-done.18.refs_1_, f32[64,64]{1,0:T(8,128)S(1)} %get-tuple-element.149.gram_ref.refs_2_), custom_call_target="tpu_custom_call" | custom-call | flops 134217728 | bytes 49152 | tf_op jit(solution)/shard_map/pallas_call | solution.py:381
  62.6 1.0 %collective-permute-done.22.refs_2_ = f32[64,96]{1,0:T(8,128)S(1)} collective-permute-done((f32[64,96]{1,0:T(8,128)S(1)}, f32[64,96]{1,0:T(8,128)S(1)}, u32[]{:S(2)}, u32[]{:S(2)}) %collective-permute-start.22) | collective-permute-done | bytes 24608 | tf_op jit(solution)/shard_map/ppermute | solution.py:48
  63.6 0.0 collective-permute-done.21.refs_1_
  63.6 3.2 %shard_map.66 = (f32[64,64]{1,0:T(8,128)S(1)}, f32[16,16]{1,0:T(8,128)S(1)}, bf16[2,16,1024]{2,1,0:T(8,128)(2,1)S(1)}) custom-call(f32[64,96]{1,0:T(8,128)S(1)} %add.3.refs_0_, f32[64,96]{1,0:T(8,128)S(1)} %collective-permute-done.21.refs_1_, f32[64,96]{1,0:T(8,128)S(1)} %collective-permute-done.22.refs_2_, f32[64,96]{1,0:T(8,128)S(1)} %collective-permute-done.23.refs_3_, ...), custom_call_target="tpu_custom_call" | custom-call | flops 134217728 | bytes 638976 | tf_op jit(solution)/shard_map/pallas_call | solution.py:381
  66.7 2.3 %collective-permute-start.24 = (bf16[2,16,1024]{2,1,0:T(8,128)(2,1)S(1)}, bf16[2,16,1024]{2,1,0:T(8,128)(2,1)S(1)}, u32[]{:S(2)}, u32[]{:S(2)}) collective-permute-start(bf16[2,16,1024]{2,1,0:T(8,128)(2,1)S(1)} %get-tuple-element.156), channel_id=1, source_target_pairs={{0,8},{8,16},{16,24},{24,0},{1,9},{9,17},{17,25},{25,1},{2,10},{10... | collective-permute-start | bytes 196616 | tf_op jit(solution)/shard_map/ppermute | solution.py:38
  69.0 0.7 shard_map.67.all_ref
  69.7 2.7 %collective-permute-done.24.below_ref = bf16[2,16,1024]{2,1,0:T(8,128)(2,1)S(1)} collective-permute-done((bf16[2,16,1024]{2,1,0:T(8,128)(2,1)S(1)}, bf16[2,16,1024]{2,1,0:T(8,128)(2,1)S(1)}, u32[]{:S(2)}, u32[]{:S(2)}) %collective-permute-start.24) | collective-permute-done | bytes 65568 | tf_op jit(solution)/shard_map/ppermute | solution.py:38
  72.5 0.9 %shard_map.68 = f32[64,2,1024]{2,1,0:T(2,128)} custom-call(f32[2,64,1024]{2,1,0:T(8,128)S(1)} %shard_map.67.all_ref, bf16[2,16,1024]{2,1,0:T(8,128)(2,1)S(1)} %collective-permute-done.24.below_ref), custom_call_target="tpu_custom_call" | custom-call | flops 134217728 | bytes 589824 | tf_op jit(solution)/shard_map/pallas_call | solution.py:381
  (12 shorter events, 0.3 us)
Async XLA Ops:
  0.0 5.7 %copy-start = (bf16[2,1024,1024]{2,1,0:T(8,128)(2,1)S(1)}, bf16[2,1024,1024]{2,1,0:T(8,128)(2,1)}, u32[]{:S(2)}) copy-start(bf16[2,1024,1024]{2,1,0:T(8,128)(2,1)} %diag_ref.15) | copy-start | bytes 12582916
  2.6 3.1 %collective-permute-start = (bf16[64,1024]{1,0:T(8,128)(2,1)S(1)}, bf16[64,1024]{1,0:T(8,128)(2,1)S(1)}, u32[]{:S(2)}, u32[]{:S(2)}) collective-permute-start(bf16[64,1024]{1,0:T(8,128)(2,1)S(1)} %get-tuple-element.84), channel_id=1, source_target_pairs={{0,1},{1,0},{2,3},{3,2},{4,5},{5,4},{6,7},{7,6},{8,9},{9,8},{10,11... | collective-permute-start | bytes 393224 | tf_op jit(solution)/shard_map/ppermute | solution.py:29
  3.1 6.4 %collective-permute-start.1 = (bf16[64,1024]{1,0:T(8,128)(2,1)S(1)}, bf16[64,1024]{1,0:T(8,128)(2,1)S(1)}, u32[]{:S(2)}, u32[]{:S(2)}) collective-permute-start(bf16[64,1024]{1,0:T(8,128)(2,1)S(1)} %get-tuple-element.90), channel_id=1, source_target_pairs={{0,8},{1,2},{2,1},{3,4},{4,3},{5,6},{6,5},{7,15},{8,0},{9,10},{10,... | collective-permute-start | bytes 393224 | tf_op jit(solution)/shard_map/ppermute | solution.py:29
  9.4 1.5 %collective-permute-start.2 = (bf16[64,1024]{1,0:T(8,128)(2,1)S(1)}, bf16[64,1024]{1,0:T(8,128)(2,1)S(1)}, u32[]{:S(2)}, u32[]{:S(2)}) collective-permute-start(bf16[64,1024]{1,0:T(8,128)(2,1)S(1)} %get-tuple-element.94), channel_id=1, source_target_pairs={{0,1},{1,0},{2,3},{3,2},{4,5},{5,4},{6,7},{7,6},{8,9},{9,8},{10,11... | collective-permute-start | bytes 393224 | tf_op jit(solution)/shard_map/ppermute | solution.py:29
  9.6 5.0 %collective-permute-start.3 = (bf16[64,1024]{1,0:T(8,128)(2,1)S(1)}, bf16[64,1024]{1,0:T(8,128)(2,1)S(1)}, u32[]{:S(2)}, u32[]{:S(2)}) collective-permute-start(bf16[64,1024]{1,0:T(8,128)(2,1)S(1)} %get-tuple-element.99), channel_id=1, source_target_pairs={{0,8},{1,2},{2,1},{3,4},{4,3},{5,6},{6,5},{7,15},{8,0},{9,10},{10,... | collective-permute-start | bytes 393224 | tf_op jit(solution)/shard_map/ppermute | solution.py:29
  13.9 2.1 %collective-permute-start.4 = (bf16[64,1024]{1,0:T(8,128)(2,1)S(1)}, bf16[64,1024]{1,0:T(8,128)(2,1)S(1)}, u32[]{:S(2)}, u32[]{:S(2)}) collective-permute-start(bf16[64,1024]{1,0:T(8,128)(2,1)S(1)} %get-tuple-element.102), channel_id=1, source_target_pairs={{0,1},{1,0},{2,3},{3,2},{4,5},{5,4},{6,7},{7,6},{8,9},{9,8},{10,11... | collective-permute-start | bytes 393224 | tf_op jit(solution)/shard_map/ppermute | solution.py:29
  14.7 5.0 %collective-permute-start.5 = (bf16[64,1024]{1,0:T(8,128)(2,1)S(1)}, bf16[64,1024]{1,0:T(8,128)(2,1)S(1)}, u32[]{:S(2)}, u32[]{:S(2)}) collective-permute-start(bf16[64,1024]{1,0:T(8,128)(2,1)S(1)} %get-tuple-element.106), channel_id=1, source_target_pairs={{0,8},{1,2},{2,1},{3,4},{4,3},{5,6},{6,5},{7,15},{8,0},{9,10},{10,... | collective-permute-start | bytes 393224 | tf_op jit(solution)/shard_map/ppermute | solution.py:29
  18.9 2.1 %collective-permute-start.6 = (bf16[64,1024]{1,0:T(8,128)(2,1)S(1)}, bf16[64,1024]{1,0:T(8,128)(2,1)S(1)}, u32[]{:S(2)}, u32[]{:S(2)}) collective-permute-start(bf16[64,1024]{1,0:T(8,128)(2,1)S(1)} %get-tuple-element.109), channel_id=1, source_target_pairs={{0,1},{1,0},{2,3},{3,2},{4,5},{5,4},{6,7},{7,6},{8,9},{9,8},{10,11... | collective-permute-start | bytes 393224 | tf_op jit(solution)/shard_map/ppermute | solution.py:29
  19.7 5.0 %collective-permute-start.7 = (bf16[64,1024]{1,0:T(8,128)(2,1)S(1)}, bf16[64,1024]{1,0:T(8,128)(2,1)S(1)}, u32[]{:S(2)}, u32[]{:S(2)}) collective-permute-start(bf16[64,1024]{1,0:T(8,128)(2,1)S(1)} %get-tuple-element.113), channel_id=1, source_target_pairs={{0,8},{1,2},{2,1},{3,4},{4,3},{5,6},{6,5},{7,15},{8,0},{9,10},{10,... | collective-permute-start | bytes 393224 | tf_op jit(solution)/shard_map/ppermute | solution.py:29
  24.2 2.0 %collective-permute-start.8 = (bf16[64,1024]{1,0:T(8,128)(2,1)S(1)}, bf16[64,1024]{1,0:T(8,128)(2,1)S(1)}, u32[]{:S(2)}, u32[]{:S(2)}) collective-permute-start(bf16[64,1024]{1,0:T(8,128)(2,1)S(1)} %get-tuple-element.116), channel_id=1, source_target_pairs={{0,1},{1,0},{2,3},{3,2},{4,5},{5,4},{6,7},{7,6},{8,9},{9,8},{10,11... | collective-permute-start | bytes 393224 | tf_op jit(solution)/shard_map/ppermute | solution.py:29
  24.8 5.4 %collective-permute-start.9 = (bf16[64,1024]{1,0:T(8,128)(2,1)S(1)}, bf16[64,1024]{1,0:T(8,128)(2,1)S(1)}, u32[]{:S(2)}, u32[]{:S(2)}) collective-permute-start(bf16[64,1024]{1,0:T(8,128)(2,1)S(1)} %get-tuple-element.120), channel_id=1, source_target_pairs={{0,8},{1,2},{2,1},{3,4},{4,3},{5,6},{6,5},{7,15},{8,0},{9,10},{10,... | collective-permute-start | bytes 393224 | tf_op jit(solution)/shard_map/ppermute | solution.py:29
  29.6 1.8 %collective-permute-start.10 = (bf16[64,1024]{1,0:T(8,128)(2,1)S(1)}, bf16[64,1024]{1,0:T(8,128)(2,1)S(1)}, u32[]{:S(2)}, u32[]{:S(2)}) collective-permute-start(bf16[64,1024]{1,0:T(8,128)(2,1)S(1)} %get-tuple-element.123), channel_id=1, source_target_pairs={{0,1},{1,0},{2,3},{3,2},{4,5},{5,4},{6,7},{7,6},{8,9},{9,8},{10,11... | collective-permute-start | bytes 393224 | tf_op jit(solution)/shard_map/ppermute | solution.py:29
  30.0 1.5 %collective-permute-start.11 = (f32[64,64]{1,0:T(8,128)S(1)}, f32[64,64]{1,0:T(8,128)S(1)}, u32[]{:S(2)}, u32[]{:S(2)}) collective-permute-start(f32[64,64]{1,0:T(8,128)S(1)} %get-tuple-element.126.refs_6_), channel_id=1, source_target_pairs={{0,1},{1,0},{2,3},{3,2},{4,5},{5,4},{6,7},{7,6},{8,9},{9,8},{10,11... | collective-permute-start | bytes 49160 | tf_op jit(solution)/shard_map/ppermute | solution.py:48
  30.3 7.3 %collective-permute-start.12 = (bf16[64,1024]{1,0:T(8,128)(2,1)S(1)}, bf16[64,1024]{1,0:T(8,128)(2,1)S(1)}, u32[]{:S(2)}, u32[]{:S(2)}) collective-permute-start(bf16[64,1024]{1,0:T(8,128)(2,1)S(1)} %get-tuple-element.128), channel_id=1, source_target_pairs={{0,8},{1,2},{2,1},{3,4},{4,3},{5,6},{6,5},{7,15},{8,0},{9,10},{10,... | collective-permute-start | bytes 393224 | tf_op jit(solution)/shard_map/ppermute | solution.py:29
  34.4 4.8 %collective-permute-start.13 = (bf16[64,1024]{1,0:T(8,128)(2,1)S(1)}, bf16[64,1024]{1,0:T(8,128)(2,1)S(1)}, u32[]{:S(2)}, u32[]{:S(2)}) collective-permute-start(bf16[64,1024]{1,0:T(8,128)(2,1)S(1)} %get-tuple-element.131), channel_id=1, source_target_pairs={{0,1},{1,0},{2,3},{3,2},{4,5},{5,4},{6,7},{7,6},{8,9},{9,8},{10,11... | collective-permute-start | bytes 393224 | tf_op jit(solution)/shard_map/ppermute | solution.py:29
  35.4 3.8 %collective-permute-start.14 = (f32[64,64]{1,0:T(8,128)S(1)}, f32[64,64]{1,0:T(8,128)S(1)}, u32[]{:S(2)}, u32[]{:S(2)}) collective-permute-start(f32[64,64]{1,0:T(8,128)S(1)} %get-tuple-element.134.refs_6_), channel_id=1, source_target_pairs={{0,3},{1,2},{2,1},{3,0},{4,7},{5,6},{6,5},{7,4},{8,11},{9,10},{10,... | collective-permute-start | bytes 49160 | tf_op jit(solution)/shard_map/ppermute | solution.py:48
  37.6 5.0 %collective-permute-start.15 = (bf16[64,1024]{1,0:T(8,128)(2,1)S(1)}, bf16[64,1024]{1,0:T(8,128)(2,1)S(1)}, u32[]{:S(2)}, u32[]{:S(2)}) collective-permute-start(bf16[64,1024]{1,0:T(8,128)(2,1)S(1)} %get-tuple-element.136), channel_id=1, source_target_pairs={{0,8},{1,2},{2,1},{3,4},{4,3},{5,6},{6,5},{7,15},{8,0},{9,10},{10,... | collective-permute-start | bytes 393224 | tf_op jit(solution)/shard_map/ppermute | solution.py:29
  42.2 4.2 %collective-permute-start.16 = (bf16[64,1024]{1,0:T(8,128)(2,1)S(1)}, bf16[64,1024]{1,0:T(8,128)(2,1)S(1)}, u32[]{:S(2)}, u32[]{:S(2)}) collective-permute-start(bf16[64,1024]{1,0:T(8,128)(2,1)S(1)} %get-tuple-element.139), channel_id=1, source_target_pairs={{0,1},{1,0},{2,3},{3,2},{4,5},{5,4},{6,7},{7,6},{8,9},{9,8},{10,11... | collective-permute-start | bytes 393224 | tf_op jit(solution)/shard_map/ppermute | solution.py:29
  42.7 7.2 %collective-permute-start.17 = (bf16[64,1024]{1,0:T(8,128)(2,1)S(1)}, bf16[64,1024]{1,0:T(8,128)(2,1)S(1)}, u32[]{:S(2)}, u32[]{:S(2)}) collective-permute-start(bf16[64,1024]{1,0:T(8,128)(2,1)S(1)} %get-tuple-element.143), channel_id=1, source_target_pairs={{0,8},{1,2},{2,1},{3,4},{4,3},{5,6},{6,5},{7,15},{8,0},{9,10},{10,... | collective-permute-start | bytes 393224 | tf_op jit(solution)/shard_map/ppermute | solution.py:29
  44.0 5.4 %collective-permute-start.18 = (f32[64,64]{1,0:T(8,128)S(1)}, f32[64,64]{1,0:T(8,128)S(1)}, u32[]{:S(2)}, u32[]{:S(2)}) collective-permute-start(f32[64,64]{1,0:T(8,128)S(1)} %get-tuple-element.144.refs_0_), channel_id=1, source_target_pairs={{0,5},{1,4},{2,7},{3,6},{4,1},{5,0},{6,3},{7,2},{8,13},{9,12},{10,... | collective-permute-start | bytes 49160 | tf_op jit(solution)/shard_map/ppermute | solution.py:48
  50.4 4.9 %collective-permute-start.19 = (bf16[2,16,1024]{2,1,0:T(8,128)(2,1)S(1)}, bf16[2,16,1024]{2,1,0:T(8,128)(2,1)S(1)}, u32[]{:S(2)}, u32[]{:S(2)}) collective-permute-start(bf16[2,16,1024]{2,1,0:T(8,128)(2,1)S(1)} %get-tuple-element.151), channel_id=1, source_target_pairs={{0,24},{8,0},{16,8},{24,16},{1,25},{9,1},{17,9},{25,17},{2,26},{10... | collective-permute-start | bytes 196616 | tf_op jit(solution)/shard_map/ppermute | solution.py:38
  55.6 1.3 %collective-permute-start.20 = (f32[64,96]{1,0:T(8,128)S(1)}, f32[64,96]{1,0:T(8,128)S(1)}, u32[]{:S(2)}, u32[]{:S(2)}) collective-permute-start(f32[64,96]{1,0:T(8,128)S(1)} %shard_map.64), channel_id=1, source_target_pairs={{0,1},{1,0},{2,3},{3,2},{4,5},{5,4},{6,7},{7,6},{8,9},{9,8},{10,11... | collective-permute-start | bytes 73736 | tf_op jit(solution)/shard_map/ppermute | solution.py:48
  56.8 5.8 %collective-permute-start.23 = (f32[64,96]{1,0:T(8,128)S(1)}, f32[64,96]{1,0:T(8,128)S(1)}, u32[]{:S(2)}, u32[]{:S(2)}) collective-permute-start(f32[64,96]{1,0:T(8,128)S(1)} %add.3.refs_0_), channel_id=1, source_target_pairs={{0,7},{1,6},{2,5},{3,4},{4,3},{5,2},{6,1},{7,0},{8,15},{9,14},{10,... | collective-permute-start | bytes 73736 | tf_op jit(solution)/shard_map/ppermute | solution.py:48
  59.2 4.3 %collective-permute-start.22 = (f32[64,96]{1,0:T(8,128)S(1)}, f32[64,96]{1,0:T(8,128)S(1)}, u32[]{:S(2)}, u32[]{:S(2)}) collective-permute-start(f32[64,96]{1,0:T(8,128)S(1)} %add.3.refs_0_), channel_id=1, source_target_pairs={{0,5},{1,4},{2,7},{3,6},{4,1},{5,0},{6,3},{7,2},{8,13},{9,12},{10,... | collective-permute-start | bytes 73736 | tf_op jit(solution)/shard_map/ppermute | solution.py:48
  59.7 3.8 %collective-permute-start.21 = (f32[64,96]{1,0:T(8,128)S(1)}, f32[64,96]{1,0:T(8,128)S(1)}, u32[]{:S(2)}, u32[]{:S(2)}) collective-permute-start(f32[64,96]{1,0:T(8,128)S(1)} %add.3.refs_0_), channel_id=1, source_target_pairs={{0,3},{1,2},{2,1},{3,0},{4,7},{5,6},{6,5},{7,4},{8,11},{9,10},{10,... | collective-permute-start | bytes 73736 | tf_op jit(solution)/shard_map/ppermute | solution.py:48
  66.7 5.7 %collective-permute-start.24 = (bf16[2,16,1024]{2,1,0:T(8,128)(2,1)S(1)}, bf16[2,16,1024]{2,1,0:T(8,128)(2,1)S(1)}, u32[]{:S(2)}, u32[]{:S(2)}) collective-permute-start(bf16[2,16,1024]{2,1,0:T(8,128)(2,1)S(1)} %get-tuple-element.156), channel_id=1, source_target_pairs={{0,8},{8,16},{16,24},{24,0},{1,9},{9,17},{17,25},{25,1},{2,10},{10... | collective-permute-start | bytes 196616 | tf_op jit(solution)/shard_map/ppermute | solution.py:38

commit v3 on v2

v3 whole, which is shorter than its diff:
```python
import functools

import jax
import jax.numpy as jnp
from jax import lax
from jax.experimental import pallas as pl
from jax.experimental.pallas import tpu as pltpu
from jax.sharding import PartitionSpec as P

EDGE = 16
DEG = 4
STEPS = 2
ROWS = 16
ROWS_FULL = 128
HIGHEST = lax.Precision.HIGHEST
BF16 = jnp.bfloat16
F32 = jnp.float32
VMEM = pl.BlockSpec(memory_space=pltpu.VMEM)
HBM = pl.BlockSpec(memory_space=pltpu.HBM)


def exchanged(block, first):
    count, slices = lax.axis_size("layer"), lax.axis_size("cuts")
    route = []
    for cut in range(slices):
        for i in range(count):
            j = i + 1 if (i - first) % 2 == 0 else i - 1
            to = (cut, j) if 0 <= j < count else (cut ^ 1 if cut ^ 1 < slices else cut, i)
            route.append((cut * count + i, to[0] * count + to[1]))
    return lax.ppermute(block, ("cuts", "layer"), route)


def far_away(block):
    return pltpu.with_memory_space_constraint(block, pltpu.HBM)


def rotated(block, distance):
    size = lax.axis_size("cuts")
    return lax.ppermute(block, "cuts", [(i, (i + distance) % size) for i in range(size)])


def doublings():
    size = lax.axis_size("layer")
    return [] if size & (size - 1) else [1 << i for i in range(size.bit_length() - 1)]


def swapped(block, reach):
    far = reach | 1
    return lax.ppermute(block, "layer", [(i, i ^ far) for i in range(lax.axis_size("layer"))])


def partial_sums(block):
    size = lax.axis_size("layer")
    if not doublings():
        return [lax.psum(block, "layer")]
    reach = 1
    while size // reach > 4:
        block = block + swapped(block, reach)
        reach *= 2
    return [block] + [swapped(block, step) for step in range(reach, size, reach)]


def product(block, matrix):
    size = block.shape[0]
    block = jnp.concatenate([block] * max(1, ROWS_FULL // size), 0)
    return jnp.dot(block, matrix, preferred_element_type=F32)[:size]


def product_t(block, matrix, precision=None):
    return lax.dot_general(
        block, matrix, (((1,), (1,)), ((), ())), precision=precision, preferred_element_type=F32
    )


def exact(first, second):
    return jnp.dot(first, second, precision=HIGHEST, preferred_element_type=F32)


def identity(size):
    row = lax.broadcasted_iota(jnp.int32, (size, size), 0)
    column = lax.broadcasted_iota(jnp.int32, (size, size), 1)
    return jnp.where(row == column, 1.0, 0.0)


def inverse_factors(*grams):
    sizes = [gram.shape[0] for gram in grams]
    works = [jnp.concatenate([identity(gram.shape[0]), gram], 1) for gram in grams]
    finished = [[] for _ in grams]
    for start in range(0, max(sizes), ROWS):
        live = [i for i, size in enumerate(sizes) if start < size]
        shapes = {i: (sizes[i] - start, 2 * sizes[i]) for i in live}
        at = {i: lax.broadcasted_iota(jnp.int32, shapes[i], 0) for i in live}
        lines, pivots = {}, {}
        for i in live:
            first = sizes[i] + start
            lines[i] = [
                jnp.broadcast_to(works[i][:, first + c : first + c + 1], shapes[i])
                for c in range(ROWS)
            ]
            pivots[i] = jnp.zeros((ROWS, shapes[i][1]), F32)
        for c in range(ROWS):
            for i in live:
                pivot = lines[i][c][c : c + 1]
                factor = jnp.where(at[i] > c, lines[i][c] * (1.0 / pivot), 0.0)
                for d in range(c + 1, ROWS):
                    lines[i][d] = lines[i][d] - factor * lines[i][d][c : c + 1]
                pivots[i] = jnp.where(at[i][:ROWS] == c, pivot, pivots[i])
                works[i] = works[i] - factor * works[i][c : c + 1]
        for i in live:
            finished[i].append(lax.rsqrt(pivots[i]) * works[i][:ROWS])
            works[i] = works[i][ROWS:]
    return [jnp.concatenate(rows, 0)[:, :size] for rows, size in zip(finished, sizes)]


def position(axis):
    return lax.axis_index(axis).astype(jnp.int32)


def send_outer(odd, rounded_ref, last_ref, send_ref):
    @pl.when(odd == 0)
    def _():
        send_ref[...] = rounded_ref[...]

    @pl.when(odd == 1)
    def _():
        send_ref[...] = product(rounded_ref[...], last_ref[...]).astype(BF16)


def send_inner(odd, rounded_ref, last_ref, send_ref):
    end = rounded_ref.shape[0] - 1

    @pl.when(odd == 1)
    def _():
        send_ref[...] = rounded_ref[end]

    @pl.when(odd == 0)
    def _():
        send_ref[...] = product(rounded_ref[end], last_ref[...]).astype(BF16)


def enter_kernel(
    far_bounds_ref, vectors_ref, couplings_ref,
    outer_ref, rest_ref, outer16_ref, rest16_ref, inner_send_ref, outer_send_ref, last_ref, mids_ref, rows_ref,
    bounds_ref, block_ref, sems,
):
    layers = vectors_ref.shape[1]
    copies = [
        pltpu.make_async_copy(vectors_ref, block_ref, sems.at[0]),
        pltpu.make_async_copy(couplings_ref.at[layers - 1], last_ref, sems.at[1]),
        pltpu.make_async_copy(couplings_ref.at[pl.ds(0, layers - 1)], mids_ref.at[0], sems.at[2]),
        pltpu.make_async_copy(far_bounds_ref, bounds_ref, sems.at[3]),
    ]
    for copy in copies:
        copy.start()
    odd = position("layer") % 2
    copies[0].wait()
    for parity in (0, 1):

        @pl.when(odd == parity)
        def _():
            order = range(layers)[:: -1 if parity else 1]
            outer_ref[...] = block_ref[:, order[0], :]
            for i, l in enumerate(order[1:]):
                rest_ref[i] = block_ref[:, l, :]

    outer16_ref[...] = outer_ref[...].astype(BF16)
    rest16_ref[...] = rest_ref[...].astype(BF16)
    copies[1].wait()
    send_outer(odd, outer16_ref, last_ref, outer_send_ref)
    send_inner(odd, rest16_ref, last_ref, inner_send_ref)
    copies[3].wait()
    width = rows_ref.shape[1]
    low, high = bounds_ref[0, 0].astype(F32), bounds_ref[0, 1].astype(F32)
    half = jnp.full((1, width), (high - low) * (1.0 / 128.0), F32)
    rows_ref[0:1] = jnp.full((1, width), (low + high) * (1.0 / 128.0), F32)
    rows_ref[1:2] = 1.0 / half
    rows_ref[2:3] = 2.0 / half
    copies[2].wait()


def turn(matrix_ref, turned_ref):
    size = matrix_ref.shape[0]
    block = 2 * ROWS_FULL if size % (2 * ROWS_FULL) == 0 else size
    for i in range(0, size, block):
        for j in range(0, size, block):
            turned_ref[pl.ds(i, block), pl.ds(j, block)] = jnp.transpose(
                matrix_ref[pl.ds(j, block), pl.ds(i, block)]
            )


def turn_kernel(last_ref, mids_in_ref, last_t_ref, mids_ref):
    turn(last_ref, last_t_ref)
    for i in range(mids_ref.shape[1]):
        turn(mids_in_ref.at[0, i], mids_ref.at[1, i])


def add_arrived(count, scale, base_ref, arrived_ref, last_t_ref, store):
    at = position("layer")
    odd = at % 2

    @pl.when((odd == 0) & (at > 0))
    def _():
        store(base_ref[...] + arrived_ref[...].astype(F32) * scale)

    @pl.when((odd == 1) & (at < count - 1))
    def _():
        store(base_ref[...] + product(arrived_ref[...], last_t_ref[...]) * scale)

    @pl.when((at == 0) | ((odd == 1) & (at == count - 1)))
    def _():
        store(base_ref[...])


def interior_kernel(
    count, layers, step, ahead, gram, adds, final, rows_ref, outer_a_ref, outer_b_ref, rest16_ref, arrived_ref,
    diag_ref, last_ref, last_t_ref, mids_ref, rest_ref, outer_before_ref, rest_before_ref, *refs,
):
    *refs, sum_ref = refs
    outs = list(refs)
    if adds:
        here_ref, there_ref = outs.pop(0), outs.pop(0)
    base_ref, next_ref = outs.pop(0), outs.pop(0)
    first_step = step % DEG == 0
    centre, scale = rows_ref[0:1], rows_ref[1:2] if first_step else rows_ref[2:3]
    odd = position("layer") % 2
    if step:
        outer_ref = outs.pop(0)

        def store(block):
            outer_ref[...] = block

        before = rows_ref[1:2] if (step - 1) % DEG == 0 else rows_ref[2:3]
        add_arrived(count, before, outer_a_ref, outer_b_ref, last_t_ref, store)
        outer16 = outer_ref[...].astype(BF16)
    else:
        outer_ref, outer16 = outer_a_ref, outer_b_ref[...]

    def rounded(place):
        return rest16_ref[place - 1] if place else outer16

    for place in range(layers)[::-1]:
        term = product(rounded(place), diag_ref[place + odd * (layers - 1 - 2 * place)])
        if place < layers - 1:
            link = place + odd * (layers - 2 - 2 * place)
            term = term + product(rounded(place + 1), mids_ref[1 - odd, link])
        if place > 0:
            link = place - 1 + odd * (layers - 2 * place)
            term = term + product(rounded(place - 1), mids_ref[odd, link])
        if place == layers - 1:
            sum_ref[...] = term

            @pl.when(odd == 0)
            def _():
                sum_ref[...] += product(arrived_ref[...], last_t_ref[...])

            @pl.when(odd == 1)
            def _():
                sum_ref[...] += arrived_ref[...].astype(F32)

            term = sum_ref[...]
        if place:
            term = (term - centre * rest_ref[place - 1]) * scale
            next_ref[place - 1] = term if first_step else term - rest_before_ref[place - 1]
        else:
            term = (term - centre * outer_ref[...]) * scale
            base_ref[...] = term if first_step else term - outer_before_ref[...]
    if not final:
        next16_ref, send_ref = outs.pop(0), outs.pop(0)
        next16_ref[...] = next_ref[...].astype(BF16)
        send_inner(odd, next16_ref, last_ref, send_ref)
    if ahead:
        ahead_ref = outs.pop(0)

        @pl.when(odd == 1)
        def _():
            ahead_ref[...] = product(base_ref[...].astype(BF16), last_ref[...])

    if gram:
        outs.pop(0)[...] = product_t(outer_ref[...], outer_ref[...], HIGHEST) + sum(
            product_t(rest_ref[i], rest_ref[i], HIGHEST) for i in range(layers - 1)
        )
    if adds:
        outs.pop(0)[...] = here_ref[...] + there_ref[...]


def square_kernel(part, last_ref, last_t_ref, square_ref):
    size = square_ref.shape[0]

    @pl.when(position("layer") % 2 == 1)
    def _():
        def chunk(i, carry):
            place = pl.multiple_of(i * 2 * ROWS_FULL, 2 * ROWS_FULL)
            rows = last_t_ref[pl.ds(part * size + place, 2 * ROWS_FULL)]
            square_ref[pl.ds(place, 2 * ROWS_FULL)] = product(rows, last_ref[...]).astype(BF16)
            return carry

        lax.fori_loop(0, size // (2 * ROWS_FULL), chunk, 0)


def plain_step_kernel(first_step, rows_ref, base_ref, arrived_ref, last_ref, last_t_ref, *refs):
    send_ref = refs[-1]
    scale = rows_ref[1:2] if first_step else rows_ref[2:3]
    odd = position("layer") % 2

    @pl.when(odd == 0)
    def _():
        has_before = (position("layer") > 0).astype(F32)
        term = arrived_ref[...].astype(F32) * (scale * has_before)
        send_ref[...] = (base_ref[...] + term).astype(BF16)

    @pl.when(odd == 1)
    def _():
        block = base_ref[...] + product(arrived_ref[...], last_t_ref[...]) * scale
        send_ref[...] = product(block.astype(BF16), last_ref[...]).astype(BF16)


def step_kernel(first_step, rows_ref, base_ref, arrived_ref, ahead_ref, square_a_ref, square_b_ref, send_ref):
    scale = rows_ref[1:2] if first_step else rows_ref[2:3]
    odd = position("layer") % 2

    @pl.when(odd == 0)
    def _():
        has_before = (position("layer") > 0).astype(F32)
        term = arrived_ref[...].astype(F32) * (scale * has_before)
        send_ref[...] = (base_ref[...] + term).astype(BF16)

    @pl.when(odd == 1)
    def _():
        half = square_a_ref.shape[0]
        term = product(arrived_ref[:, :half], square_a_ref[...])
        term = term + product(arrived_ref[:, half:], square_b_ref[...])
        block = ahead_ref[...] + term * scale
        send_ref[...] = block.astype(BF16)


def row_scales(gram):
    return lax.rsqrt(jnp.sum(gram * identity(gram.shape[0]), axis=1, keepdims=True))


def scale_kernel(parts, length, *refs):
    grams, (rest_ref, next_ref, next16_ref, gram_ref, scales_ref) = refs[:parts], refs[parts:]
    scales = row_scales(sum(ref[...] for ref in grams) * (1.0 / length))
    scales_ref[...] = jnp.broadcast_to(scales, scales_ref.shape)
    gram_ref[...] = jnp.zeros(gram_ref.shape, F32)
    for i in range(rest_ref.shape[0]):
        block = rest_ref[i] * scales
        next_ref[i] = block
        next16_ref[i] = block.astype(BF16)
        gram_ref[...] += product_t(block, block, HIGHEST)


def last_kernel(
    count, rows_ref, base_ref, arrived_ref, last_t_ref, scales_ref, rest16_ref, rest_gram_ref,
    next_ref, next16_ref, low_ref, gram_ref,
):
    def store(block):
        next_ref[...] = block * scales_ref[:, :1]

    add_arrived(count, rows_ref[2:3], base_ref, arrived_ref, last_t_ref, store)
    next16_ref[...] = next_ref[...].astype(BF16)
    edge = low_ref.shape[1]
    low_ref[0] = next16_ref[:edge]
    for i in range(low_ref.shape[0] - 1):
        low_ref[i + 1] = rest16_ref[i, :edge]
    gram_ref[...] = rest_gram_ref[...] + product_t(next_ref[...], next_ref[...], HIGHEST)


def first_factor_kernel(parts, length, *refs):
    grams, (outer_ref, rest_ref, inverse_ref, all_ref) = refs[:parts], refs[parts:]
    gram = sum(ref[...] for ref in grams) * (1.0 / length)
    scales = row_scales(gram)
    across = jnp.sum(identity(gram.shape[0]) * scales, axis=0, keepdims=True)
    inverse_ref[...] = inverse_factors(gram * scales * across)[0]
    all_ref[0] = exact(inverse_ref[...], outer_ref[...])
    for i in range(rest_ref.shape[0]):
        all_ref[i + 1] = exact(inverse_ref[...], rest_ref[i])


def cross_kernel(gram_ref, outer16_ref, rest16_ref, above_ref, out_ref):
    size, edge = outer16_ref.shape[0], above_ref.shape[1]
    rest = range(rest16_ref.shape[0])
    out_ref[:, :size] = gram_ref[...]
    out_ref[:, size : size + edge] = product_t(outer16_ref[...], above_ref[0]) + sum(
        product_t(rest16_ref[i], above_ref[i + 1]) for i in rest
    )
    out_ref[:edge, size + edge :] = sum(
        product_t(above_ref[l], above_ref[l]) for l in range(above_ref.shape[0])
    )
    out_ref[edge:, size + edge :] = jnp.zeros((size - edge, edge), F32)


def factor_kernel(parts, length, slices, *refs):
    grams, (first_ref, all_ref, inverse_ref, weights_ref, up_ref) = refs[:parts], refs[parts:]
    size, edge = all_ref.shape[1], up_ref.shape[1]
    first = first_ref[...]
    total = sum(ref[...] for ref in grams) * (1.0 / length)
    has_above = (position("cuts") < slices - 1).astype(F32)
    above = total[:edge, size + edge :] * has_above + identity(edge) * (1.0 - has_above)
    cross = exact(first, total[:, size : size + edge]) * has_above
    own = product_t(exact(first, total[:, :size]), first, HIGHEST)
    inverse, above = inverse_factors(own, above)
    inverse_ref[...] = inverse
    high = inverse[size - edge :]
    correlation = product_t(exact(high, cross), above, HIGHEST)
    up = exact(correlation.T, high)
    for i in range(all_ref.shape[0]):
        up_ref[i] = exact(up, all_ref[i]).astype(BF16)
    weights_ref[...] = exact(correlation, above)


def vectors_kernel(inverse_ref, weights_ref, first_ref, above_ref, all_ref):
    layers, size, _ = all_ref.shape
    edge = above_ref.shape[1]
    for i in range(layers):
        block = exact(inverse_ref[...], first_ref[i])
        all_ref[i] = block
        all_ref[i, size - edge :] = block[size - edge :] - exact(
            weights_ref[...], above_ref[i].astype(F32)
        )


def final_kernel(all_ref, below_ref, out_ref):
    layers, size, _ = all_ref.shape
    edge = below_ref.shape[1]
    has_below = (position("cuts") > 0).astype(F32)
    for parity in (0, 1):

        @pl.when(position("layer") % 2 == parity)
        def _():
            for i, l in enumerate(range(layers)[:: -1 if parity else 1]):
                out_ref[:edge, l, :] = all_ref[i, :edge] - below_ref[i].astype(F32) * has_below
                out_ref[edge:, l, :] = all_ref[i, edge:]


def per_device(vectors, diag_blocks, couplings, bounds):
    vectors = vectors[0]
    count_vec, layers, width = vectors.shape
    count, slices = lax.axis_size("layer"), lax.axis_size("cuts")
    length_all = count * layers * width

    def array(dtype, *shape):
        return jax.ShapeDtypeStruct(shape, dtype)

    outer32, outer16 = array(F32, count_vec, width), array(BF16, count_vec, width)
    rest32, rest16 = array(F32, layers - 1, count_vec, width), array(BF16, layers - 1, count_vec, width)
    square = array(F32, count_vec, count_vec)
    matrix = array(BF16, width, width)
    matrices = array(BF16, 2, layers - 1, width, width)
    edges = array(BF16, layers, EDGE, width)
    one = 2 * count_vec * width * width

    def call(kernel, outs, *operands, far=(), scratch_shapes=(), flops=one, aliases=()):
        moved = sum(x.size * x.dtype.itemsize for x in operands)
        return pl.pallas_call(
            kernel,
            out_shape=outs,
            in_specs=[HBM if i in far else VMEM for i in range(len(operands))],
            out_specs=jax.tree.map(lambda _: VMEM, outs),
            scratch_shapes=list(scratch_shapes),
            input_output_aliases=dict(aliases),
            compiler_params=pltpu.CompilerParams(vmem_limit_bytes=32 * 2**20),
            cost_estimate=pl.CostEstimate(flops=flops, bytes_accessed=moved, transcendentals=0),
        )(*operands)

    outer, rest, outer_r, rest_r, inner_send, outer_send, last, mids, rows = call(
        enter_kernel,
        (outer32, rest32, outer16, rest16, outer16, outer16, matrix, matrices, array(F32, 8, width)),
        *map(far_away, (bounds, vectors, couplings)), far=(0, 1, 2),
        scratch_shapes=[
            pltpu.SMEM(bounds.shape, jnp.int32),
            pltpu.VMEM(vectors.shape, F32),
            pltpu.SemaphoreType.DMA((4,)),
        ],
    )

    last_t, mids = call(turn_kernel, (matrix, matrices), last, mids, aliases={1: 1})
    half = array(BF16, width // 2, width)
    squares = [call(functools.partial(square_kernel, i), half, last, last_t) for i in range(2)]
    outer_a, outer_b = outer, outer_r
    outer_now, rest_before = outer, rest
    reaches = doublings()
    applications = STEPS * DEG
    for step in range(applications):
        final, gram = step == applications - 1, step == DEG
        ahead = 1 < step < applications - 1
        adds = step > DEG and bool(reaches) and not final
        outer_in = exchanged(outer_send, 1)
        inner_in = exchanged(inner_send, 0)
        base, rest_next, *extra = call(
            functools.partial(interior_kernel, count, layers, step, ahead, gram, adds, final),
            (outer32, rest32)
            + ((outer32,) if step else ())
            + (() if final else (rest16, outer16))
            + ((outer32,) if ahead else ())
            + ((square,) if gram or adds else ()),
            rows, outer_a, outer_b, rest_r, inner_in, diag_blocks, last, last_t, mids,
            rest, outer_now, rest_before,
            *((total, swapped(total, reaches.pop(0))) if adds else ()),
            scratch_shapes=[pltpu.VMEM((count_vec, width), F32)],
            flops=(3 * layers - 1) * one,
        )
        if step:
            outer_now = extra.pop(0)
        if gram or adds:
            total = extra[-1]
        if gram and not reaches:
            total = lax.psum(total, "layer")
        if final:
            break
        rest_r, inner_send = extra[:2]
        if ahead:
            outer_send = call(
                functools.partial(step_kernel, step % DEG == 0),
                outer16, rows, base, outer_in, extra[2], *squares,
            )
        else:
            outer_send = call(
                functools.partial(plain_step_kernel, step % DEG == 0),
                outer16, rows, base, outer_in, last, last_t, *squares[:step],
            )
        outer_a, outer_b = base, outer_in
        rest_before, rest = rest, rest_next

    totals = [total]
    for reach in reaches:
        totals = [sum(totals), swapped(sum(totals), reach)]
    rest, rest_r, rest_gram, scales = call(
        functools.partial(scale_kernel, len(totals), length_all),
        (rest32, rest16, square, array(F32, count_vec, 128)), *totals, rest_next,
    )
    outer, outer_r, low, gram = call(
        functools.partial(last_kernel, count), (outer32, outer16, edges, square),
        rows, base, outer_in, last_t, scales, rest_r, rest_gram,
    )
    above = rotated(low, -1)
    field32 = array(F32, layers, count_vec, width)
    cross = call(
        cross_kernel, array(F32, count_vec, count_vec + 2 * EDGE), gram, outer_r, rest_r, above
    )
    first, first_all = call(
        functools.partial(first_factor_kernel, len(totals), length_all),
        (square, field32), *totals, outer, rest,
    )
    grams = partial_sums(cross)
    inverse, weights, up = call(
        functools.partial(factor_kernel, len(grams), length_all, slices),
        (square, array(F32, EDGE, EDGE), edges), *grams, first, first_all,
    )
    below = rotated(up, 1)
    vectors_all = call(vectors_kernel, field32, inverse, weights, first_all, above)
    result = call(final_kernel, array(F32, count_vec, layers, width), vectors_all, below)
    return result[None]


def solution(mesh):
    in_specs = (
        P("cuts", None, "layer", None),
        P("layer", None, None),
        P("layer", None, None),
        P("cuts", None),
    )
    out_specs = P("cuts", None, "layer", None)
    return jax.shard_map(
        per_device, mesh=mesh, in_specs=in_specs, out_specs=out_specs, check_vma=False
    )
```

time: 73.5 us -> 70 us (0.952)
  Pallas kernels: 35.9 us -> 32.2 us
  waiting for transfers between devices: 9.71 us -> 12.7 us
  starting transfers between devices: 27.5 us -> 24.6 us
    pallas_call x23 -> x26, Pallas kernels: 35.9 us -> 32.2 us  [call(): pl.pallas_call(kernel, out_shape=outs, in_specs=[HBM if i in far else VME...]
    ppermute x16, waiting for transfers between devices: 2.25 us -> 4.45 us  [exchanged(): return lax.ppermute(block, ('cuts', 'layer'), route)]
    ppermute x16, starting transfers between devices: 14 us -> 12.1 us  [exchanged(): return lax.ppermute(block, ('cuts', 'layer'), route)]
    ppermute x2, starting transfers between devices: 4.78 us -> 3.34 us  [rotated(): lax.ppermute(block, 'cuts', [(i, (i + distance) % size) for i in range(si...]
    ppermute x2, waiting for transfers between devices: 5.07 us -> 5.92 us  [rotated(): lax.ppermute(block, 'cuts', [(i, (i + distance) % size) for i in range(si...]
  transfers between devices with their start and end apart: 25 -> 25, of which waited for: 9 -> 11; matrix products, arithmetic and copies ran while one was open for 0% -> 0% of each run, Pallas kernels for 39% -> 36%
where the time goes in v3:
time: 70 us; the launch traced here: 69.8 us
  Pallas kernels  32.2 us (46%)
  starting transfers between devices  24.6 us (35%)
  waiting for transfers between devices  12.7 us (18%)
    pallas_call x26, Pallas kernels, call(): pl.pallas_call(kernel, out_shape=outs, in_specs=[HBM if i in far else VME...  32.2 us
    ppermute x16, starting transfers between devices, exchanged(): return lax.ppermute(block, ('cuts', 'layer'), route)  12.1 us
    ppermute x7, starting transfers between devices, swapped(): lax.ppermute(block, 'layer', [(i, i ^ far) for i in range(lax.axis_size('...  9.17 us
    ppermute x2, waiting for transfers between devices, rotated(): lax.ppermute(block, 'cuts', [(i, (i + distance) % size) for i in range(si...  5.92 us
    ppermute x16, waiting for transfers between devices, exchanged(): return lax.ppermute(block, ('cuts', 'layer'), route)  4.45 us
    ppermute x2, starting transfers between devices, rotated(): lax.ppermute(block, 'cuts', [(i, (i + distance) % size) for i in range(si...  3.34 us
    ppermute x7, waiting for transfers between devices, swapped(): lax.ppermute(block, 'layer', [(i, i ^ far) for i in range(lax.axis_size('...  2.37 us
  transfers between devices with their start and end apart: 25, of which 11 were waited for; matrix products, arithmetic and copies ran while one was open for 0% of the time, Pallas kernels for 36%

profile of v3, /device:TPU:0, one launch (start us, length us, event | category | flops | bytes accessed | tf_op | source)
XLA Modules:
  0.0 69.8 jit_solution(12529106361844031458)
XLA Ops:
  0.0 2.4 %shard_map.46 = (f32[64,1024]{1,0:T(8,128)S(1)}, f32[1,64,1024]{2,1,0:T(8,128)S(1)}, bf16[64,1024]{1,0:T(8,128)(2,1)S(1)}, bf16[1,64,1024]{2,1,0:T(8,128)(2,1)S(...) custom-call(s32[1,2]{1,0:T(1,128)} %far_bounds_ref.1, ...), custom_call_target="tpu_custom_call" | custom-call | flops 134217728 | bytes 4718600 | tf_op jit(solution)/shard_map/pallas_call | solution.py:454
  2.4 0.0 copy-start
  2.5 0.5 collective-permute-start
  3.0 2.6 %collective-permute-start.1 = (bf16[64,1024]{1,0:T(8,128)(2,1)S(1)}, bf16[64,1024]{1,0:T(8,128)(2,1)S(1)}, u32[]{:S(2)}, u32[]{:S(2)}) collective-permute-start(bf16[64,1024]{1,0:T(8,128)(2,1)S(1)} %get-tuple-element.84), channel_id=1, source_target_pairs={{0,8},{1,2},{2,1},{3,4},{4,3},{5,6},{6,5},{7,15},{8,0},{9,10},{10,... | collective-permute-start | bytes 393224 | tf_op jit(solution)/shard_map/ppermute | solution.py:30
  5.5 1.4 %shard_map.47 = (bf16[1024,1024]{1,0:T(8,128)(2,1)S(1)}, bf16[2,1,1024,1024]{3,2,1,0:T(8,128)(2,1)S(1)}) custom-call(bf16[1024,1024]{1,0:T(8,128)(2,1)S(1)} %get-tuple-element.78.last_ref, bf16[2,1,1024,1024]{3,2,1,0:T(8,128)(2,1)S(1)} %get-tuple-element.79.mids_in_ref), custom_call_target="tpu_custom_call", output_to_operand_aliasing={{1}: (1, {})} | custom-call | flops 134217728 | bytes 6291456 | tf_op jit(solution)/shard_map/pallas_call | solution.py:454
  6.9 0.0 collective-permute-done.arrived_ref
  7.0 2.4 %shard_map.48 = (f32[64,1024]{1,0:T(8,128)S(1)}, f32[1,64,1024]{2,1,0:T(8,128)S(1)}, bf16[1,64,1024]{2,1,0:T(8,128)(2,1)S(1)}, bf16[64,1024]{1,0:T(8,128)(2,1)S(1)}) custom-call(f32[8,1024]{1,0:T(8,128)S(1)} %get-tuple-element.73.rows_ref, f32[64,1024]{1,0:T(8,128)S(1)} %get-tuple-element.74.outer_a_ref.outer_before_ref, ...), custom_call_target="tpu_custom_call" | custom-call | flops 671088640 | bytes 14057472 | tf_op jit(solution)/shard_map/pallas_call | solution.py:454
  9.3 0.1 collective-permute-start.2
  9.4 0.1 shard_map.50
  9.5 1.1 %collective-permute-start.3 = (bf16[64,1024]{1,0:T(8,128)(2,1)S(1)}, bf16[64,1024]{1,0:T(8,128)(2,1)S(1)}, u32[]{:S(2)}, u32[]{:S(2)}) collective-permute-start(bf16[64,1024]{1,0:T(8,128)(2,1)S(1)} %shard_map.50), channel_id=1, source_target_pairs={{0,8},{1,2},{2,1},{3,4},{4,3},{5,6},{6,5},{7,15},{8,0},{9,10},{10,... | collective-permute-start | bytes 393224 | tf_op jit(solution)/shard_map/ppermute | solution.py:30
  10.6 0.1 collective-permute-done.2.arrived_ref
  10.7 2.4 %shard_map.49 = (f32[64,1024]{1,0:T(8,128)S(1)}, f32[1,64,1024]{2,1,0:T(8,128)S(1)}, f32[64,1024]{1,0:T(8,128)S(1)}, bf16[1,64,1024]{2,1,0:T(8,128)(2,1)S(1)}, bf16[64,1024]{1,0:T(8,128)(2,1)S(1)}) custom-call(f32[8,1024]{1,0:T(8,128)S(1)} %get-tuple-element.73.rows_ref, f32[64,1024]{1,0:T(8,128)S(1)} %get-tuple-element.83.outer_a_ref.base_ref, ...), custom_call_target="tpu_custom_call" | custom-call | flops 671088640 | bytes 14057472 | tf_op jit(solution)/shard_map/pallas_call | solution.py:454
  13.1 0.1 collective-permute-start.4
  13.2 1.3 %collective-permute-done.3.outer_b_ref.arrived_ref = bf16[64,1024]{1,0:T(8,128)(2,1)S(1)} collective-permute-done((bf16[64,1024]{1,0:T(8,128)(2,1)S(1)}, bf16[64,1024]{1,0:T(8,128)(2,1)S(1)}, u32[]{:S(2)}, u32[]{:S(2)}) %collective-permute-start.3) | collective-permute-done | bytes 131104 | tf_op jit(solution)/shard_map/ppermute | solution.py:30
  14.6 1.1 %collective-permute-start.5 = (bf16[64,1024]{1,0:T(8,128)(2,1)S(1)}, bf16[64,1024]{1,0:T(8,128)(2,1)S(1)}, u32[]{:S(2)}, u32[]{:S(2)}) collective-permute-start(bf16[64,1024]{1,0:T(8,128)(2,1)S(1)} %shard_map.53), channel_id=1, source_target_pairs={{0,8},{1,2},{2,1},{3,4},{4,3},{5,6},{6,5},{7,15},{8,0},{9,10},{10,... | collective-permute-start | bytes 393224 | tf_op jit(solution)/shard_map/ppermute | solution.py:30
  15.7 0.0 collective-permute-done.4.arrived_ref
  15.7 2.4 %shard_map.51 = (f32[64,1024]{1,0:T(8,128)S(1)}, f32[1,64,1024]{2,1,0:T(8,128)S(1)}, f32[64,1024]{1,0:T(8,128)S(1)}, bf16[1,64,1024]{2,1,0:T(8,128)(2,1)S(1)}, b...) custom-call(f32[8,1024]{1,0:T(8,128)S(1)} %get-tuple-element.73.rows_ref, ...), custom_call_target="tpu_custom_call" | custom-call | flops 671088640 | bytes 14057472 | tf_op jit(solution)/shard_map/pallas_call | solution.py:454
  18.1 0.4 collective-permute-start.6
  18.5 1.1 %collective-permute-done.5.outer_b_ref.arrived_ref = bf16[64,1024]{1,0:T(8,128)(2,1)S(1)} collective-permute-done((bf16[64,1024]{1,0:T(8,128)(2,1)S(1)}, bf16[64,1024]{1,0:T(8,128)(2,1)S(1)}, u32[]{:S(2)}, u32[]{:S(2)}) %collective-permute-start.5) | collective-permute-done | bytes 131104 | tf_op jit(solution)/shard_map/ppermute | solution.py:30
  19.6 1.1 %collective-permute-start.7 = (bf16[64,1024]{1,0:T(8,128)(2,1)S(1)}, bf16[64,1024]{1,0:T(8,128)(2,1)S(1)}, u32[]{:S(2)}, u32[]{:S(2)}) collective-permute-start(bf16[64,1024]{1,0:T(8,128)(2,1)S(1)} %shard_map.56), channel_id=1, source_target_pairs={{0,8},{1,2},{2,1},{3,4},{4,3},{5,6},{6,5},{7,15},{8,0},{9,10},{10,... | collective-permute-start | bytes 393224 | tf_op jit(solution)/shard_map/ppermute | solution.py:30
  20.8 0.0 collective-permute-done.6.arrived_ref
  20.8 2.4 %shard_map.54 = (f32[64,1024]{1,0:T(8,128)S(1)}, f32[1,64,1024]{2,1,0:T(8,128)S(1)}, f32[64,1024]{1,0:T(8,128)S(1)}, bf16[1,64,1024]{2,1,0:T(8,128)(2,1)S(1)}, b...) custom-call(f32[8,1024]{1,0:T(8,128)S(1)} %get-tuple-element.73.rows_ref, ...), custom_call_target="tpu_custom_call" | custom-call | flops 671088640 | bytes 14057472 | tf_op jit(solution)/shard_map/pallas_call | solution.py:454
  23.2 0.2 collective-permute-start.8
  23.4 1.2 %collective-permute-done.7.outer_b_ref.arrived_ref = bf16[64,1024]{1,0:T(8,128)(2,1)S(1)} collective-permute-done((bf16[64,1024]{1,0:T(8,128)(2,1)S(1)}, bf16[64,1024]{1,0:T(8,128)(2,1)S(1)}, u32[]{:S(2)}, u32[]{:S(2)}) %collective-permute-start.7) | collective-permute-done | bytes 131104 | tf_op jit(solution)/shard_map/ppermute | solution.py:30
  24.7 1.1 %collective-permute-start.9 = (bf16[64,1024]{1,0:T(8,128)(2,1)S(1)}, bf16[64,1024]{1,0:T(8,128)(2,1)S(1)}, u32[]{:S(2)}, u32[]{:S(2)}) collective-permute-start(bf16[64,1024]{1,0:T(8,128)(2,1)S(1)} %shard_map.58), channel_id=1, source_target_pairs={{0,8},{1,2},{2,1},{3,4},{4,3},{5,6},{6,5},{7,15},{8,0},{9,10},{10,... | collective-permute-start | bytes 393224 | tf_op jit(solution)/shard_map/ppermute | solution.py:30
  25.9 2.9 %shard_map.57 = (f32[64,1024]{1,0:T(8,128)S(1)}, f32[1,64,1024]{2,1,0:T(8,128)S(1)}, f32[64,1024]{1,0:T(8,128)S(1)}, bf16[1,64,1024]{2,1,0:T(8,128)(2,1)S(1)}, b...) custom-call(f32[8,1024]{1,0:T(8,128)S(1)} %get-tuple-element.73.rows_ref, ...), custom_call_target="tpu_custom_call" | custom-call | flops 671088640 | bytes 14057472 | tf_op jit(solution)/shard_map/pallas_call | solution.py:454
  28.8 0.1 collective-permute-start.10
  28.9 0.5 collective-permute-start.11
  29.4 0.4 collective-permute-done.9.outer_b_ref.arrived_ref
  29.8 1.1 %collective-permute-start.12 = (bf16[64,1024]{1,0:T(8,128)(2,1)S(1)}, bf16[64,1024]{1,0:T(8,128)(2,1)S(1)}, u32[]{:S(2)}, u32[]{:S(2)}) collective-permute-start(bf16[64,1024]{1,0:T(8,128)(2,1)S(1)} %shard_map.60), channel_id=1, source_target_pairs={{0,8},{1,2},{2,1},{3,4},{4,3},{5,6},{6,5},{7,15},{8,0},{9,10},{10,... | collective-permute-start | bytes 393224 | tf_op jit(solution)/shard_map/ppermute | solution.py:30
  30.9 0.0 collective-permute-done.11.refs_1_
  30.9 0.0 collective-permute-done.10.arrived_ref
  30.9 2.4 %shard_map.59 = (f32[64,1024]{1,0:T(8,128)S(1)}, f32[1,64,1024]{2,1,0:T(8,128)S(1)}, f32[64,1024]{1,0:T(8,128)S(1)}, bf16[1,64,1024]{2,1,0:T(8,128)(2,1)S(1)}, b...) custom-call(f32[8,1024]{1,0:T(8,128)S(1)} %get-tuple-element.73.rows_ref, ...), custom_call_target="tpu_custom_call" | custom-call | flops 671088640 | bytes 14090240 | tf_op jit(solution)/shard_map/pallas_call | solution.py:454
  33.4 0.3 collective-permute-start.13
  33.7 1.6 %collective-permute-start.14 = (f32[64,64]{1,0:T(8,128)S(1)}, f32[64,64]{1,0:T(8,128)S(1)}, u32[]{:S(2)}, u32[]{:S(2)}) collective-permute-start(f32[64,64]{1,0:T(8,128)S(1)} %get-tuple-element.117.refs_0_), channel_id=1, source_target_pairs={{0,3},{1,2},{2,1},{3,0},{4,7},{5,6},{6,5},{7,4},{8,11},{9,10},{10,... | collective-permute-start | bytes 49160 | tf_op jit(solution)/shard_map/ppermute | solution.py:49
  35.3 0.0 collective-permute-done.12.outer_b_ref.arrived_ref
  35.3 0.9 %collective-permute-start.15 = (bf16[64,1024]{1,0:T(8,128)(2,1)S(1)}, bf16[64,1024]{1,0:T(8,128)(2,1)S(1)}, u32[]{:S(2)}, u32[]{:S(2)}) collective-permute-start(bf16[64,1024]{1,0:T(8,128)(2,1)S(1)} %shard_map.62), channel_id=1, source_target_pairs={{0,8},{1,2},{2,1},{3,4},{4,3},{5,6},{6,5},{7,15},{8,0},{9,10},{10,... | collective-permute-start | bytes 393224 | tf_op jit(solution)/shard_map/ppermute | solution.py:30
  36.2 0.8 %collective-permute-done.14.refs_1_ = f32[64,64]{1,0:T(8,128)S(1)} collective-permute-done((f32[64,64]{1,0:T(8,128)S(1)}, f32[64,64]{1,0:T(8,128)S(1)}, u32[]{:S(2)}, u32[]{:S(2)}) %collective-permute-start.14) | collective-permute-done | bytes 16416 | tf_op jit(solution)/shard_map/ppermute | solution.py:49
  37.1 0.0 collective-permute-done.13.arrived_ref
  37.1 2.6 %shard_map.61 = (f32[64,1024]{1,0:T(8,128)S(1)}, f32[1,64,1024]{2,1,0:T(8,128)S(1)}, f32[64,1024]{1,0:T(8,128)S(1)}, bf16[1,64,1024]{2,1,0:T(8,128)(2,1)S(1)}, b...) custom-call(f32[8,1024]{1,0:T(8,128)S(1)} %get-tuple-element.73.rows_ref, ...), custom_call_target="tpu_custom_call" | custom-call | flops 671088640 | bytes 14090240 | tf_op jit(solution)/shard_map/pallas_call | solution.py:454
  39.7 0.3 collective-permute-start.16
  40.0 0.3 collective-permute-done.15.outer_b_ref.arrived_ref
  40.4 0.9 %collective-permute-start.17 = (bf16[64,1024]{1,0:T(8,128)(2,1)S(1)}, bf16[64,1024]{1,0:T(8,128)(2,1)S(1)}, u32[]{:S(2)}, u32[]{:S(2)}) collective-permute-start(bf16[64,1024]{1,0:T(8,128)(2,1)S(1)} %shard_map.64), channel_id=1, source_target_pairs={{0,8},{1,2},{2,1},{3,4},{4,3},{5,6},{6,5},{7,15},{8,0},{9,10},{10,... | collective-permute-start | bytes 393224 | tf_op jit(solution)/shard_map/ppermute | solution.py:30
  41.3 3.1 %collective-permute-start.18 = (f32[64,64]{1,0:T(8,128)S(1)}, f32[64,64]{1,0:T(8,128)S(1)}, u32[]{:S(2)}, u32[]{:S(2)}) collective-permute-start(f32[64,64]{1,0:T(8,128)S(1)} %get-tuple-element.126.refs_0_), channel_id=1, source_target_pairs={{0,5},{1,4},{2,7},{3,6},{4,1},{5,0},{6,3},{7,2},{8,13},{9,12},{10,... | collective-permute-start | bytes 49160 | tf_op jit(solution)/shard_map/ppermute | solution.py:49
  44.4 0.0 collective-permute-done.16.arrived_ref
  44.4 2.5 %shard_map.63 = (f32[64,1024]{1,0:T(8,128)S(1)}, f32[1,64,1024]{2,1,0:T(8,128)S(1)}, f32[64,1024]{1,0:T(8,128)}) custom-call(f32[8,1024]{1,0:T(8,128)S(1)} %get-tuple-element.73.rows_ref, f32[64,1024]{1,0:T(8,128)S(1)} %get-tuple-element.118.outer_a_ref.base_ref, bf16[64,1024]{1,0:T(8,128)(2,1)S(1)} %collective-permute-done.15.outer_b_ref.arrived_ref, ...), custom_call_target="tpu_custom_call" | custom-call | flops 671088640 | bytes 14057472 | tf_op jit(solution)/shard_map/pallas_call | solution.py:454
  46.9 0.4 shard_map.65
  47.4 0.5 shard_map.66
  47.9 1.7 %collective-permute-start.19 = (bf16[2,16,1024]{2,1,0:T(8,128)(2,1)S(1)}, bf16[2,16,1024]{2,1,0:T(8,128)(2,1)S(1)}, u32[]{:S(2)}, u32[]{:S(2)}) collective-permute-start(bf16[2,16,1024]{2,1,0:T(8,128)(2,1)S(1)} %get-tuple-element.133), channel_id=1, source_target_pairs={{0,24},{8,0},{16,8},{24,16},{1,25},{9,1},{17,9},{25,17},{2,26},{10... | collective-permute-start | bytes 196616 | tf_op jit(solution)/shard_map/ppermute | solution.py:39
  49.6 3.1 %collective-permute-done.19.above_ref = bf16[2,16,1024]{2,1,0:T(8,128)(2,1)S(1)} collective-permute-done((bf16[2,16,1024]{2,1,0:T(8,128)(2,1)S(1)}, bf16[2,16,1024]{2,1,0:T(8,128)(2,1)S(1)}, u32[]{:S(2)}, u32[]{:S(2)}) %collective-permute-start.19) | collective-permute-done | bytes 65568 | tf_op jit(solution)/shard_map/ppermute | solution.py:39
  52.7 0.3 shard_map.67
  53.0 0.2 collective-permute-start.20
  53.2 1.1 %collective-permute-done.20 = f32[64,96]{1,0:T(8,128)S(1)} collective-permute-done((f32[64,96]{1,0:T(8,128)S(1)}, f32[64,96]{1,0:T(8,128)S(1)}, u32[]{:S(2)}, u32[]{:S(2)}) %collective-permute-start.20) | collective-permute-done | bytes 24608 | tf_op jit(solution)/shard_map/ppermute | solution.py:49
  54.3 2.1 %collective-permute-start.23 = (f32[64,96]{1,0:T(8,128)S(1)}, f32[64,96]{1,0:T(8,128)S(1)}, u32[]{:S(2)}, u32[]{:S(2)}) collective-permute-start(f32[64,96]{1,0:T(8,128)S(1)} %add.3.refs_0_), channel_id=1, source_target_pairs={{0,7},{1,6},{2,5},{3,4},{4,3},{5,2},{6,1},{7,0},{8,15},{9,14},{10,... | collective-permute-start | bytes 73736 | tf_op jit(solution)/shard_map/ppermute | solution.py:49
  56.3 0.0 collective-permute-start.22
  56.3 1.8 %collective-permute-start.21 = (f32[64,96]{1,0:T(8,128)S(1)}, f32[64,96]{1,0:T(8,128)S(1)}, u32[]{:S(2)}, u32[]{:S(2)}) collective-permute-start(f32[64,96]{1,0:T(8,128)S(1)} %add.3.refs_0_), channel_id=1, source_target_pairs={{0,3},{1,2},{2,1},{3,0},{4,7},{5,6},{6,5},{7,4},{8,11},{9,10},{10,... | collective-permute-start | bytes 73736 | tf_op jit(solution)/shard_map/ppermute | solution.py:49
  58.1 2.3 %shard_map.68 = (f32[64,64]{1,0:T(8,128)S(1)}, f32[2,64,1024]{2,1,0:T(8,128)S(1)}) custom-call(f32[64,64]{1,0:T(8,128)S(1)} %get-tuple-element.126.refs_0_, f32[64,64]{1,0:T(8,128)S(1)} %collective-permute-done.18.refs_1_, f32[64,1024]{1,0:T(8,128)S(1)} %get-tuple-element.134.refs_2_, f32[1,64,1024]{2,1,0:T(8,128)S(1)} %get-tuple-element.135.refs_3_), custom_call_target="tpu_custom_call" | custom-call | flops 134217728 | bytes 557056 | tf_op jit(solution)/shard_map/pallas_call | solution.py:454
  60.4 0.0 collective-permute-done.23.refs_3_
  60.4 0.4 collective-permute-done.22.refs_2_
  60.9 2.9 %shard_map.69 = (f32[64,64]{1,0:T(8,128)S(1)}, f32[16,16]{1,0:T(8,128)S(1)}, bf16[2,16,1024]{2,1,0:T(8,128)(2,1)S(1)}) custom-call(f32[64,96]{1,0:T(8,128)S(1)} %add.3.refs_0_, f32[64,96]{1,0:T(8,128)S(1)} %collective-permute-done.21.refs_1_, f32[64,96]{1,0:T(8,128)S(1)} %collective-permute-done.22.refs_2_, f32[64,96]{1,0:T(8,128)S(1)} %collective-permute-done.23.refs_3_, ...), custom_call_target="tpu_custom_call" | custom-call | flops 134217728 | bytes 638976 | tf_op jit(solution)/shard_map/pallas_call | solution.py:454
  63.7 1.6 %collective-permute-start.24 = (bf16[2,16,1024]{2,1,0:T(8,128)(2,1)S(1)}, bf16[2,16,1024]{2,1,0:T(8,128)(2,1)S(1)}, u32[]{:S(2)}, u32[]{:S(2)}) collective-permute-start(bf16[2,16,1024]{2,1,0:T(8,128)(2,1)S(1)} %get-tuple-element.140), channel_id=1, source_target_pairs={{0,8},{8,16},{16,24},{24,0},{1,9},{9,17},{17,25},{25,1},{2,10},{10... | collective-permute-start | bytes 196616 | tf_op jit(solution)/shard_map/ppermute | solution.py:39
  65.4 0.7 %shard_map.70.all_ref = f32[2,64,1024]{2,1,0:T(8,128)S(1)} custom-call(f32[64,64]{1,0:T(8,128)S(1)} %get-tuple-element.138.inverse_ref, f32[16,16]{1,0:T(8,128)S(1)} %get-tuple-element.139.weights_ref, f32[2,64,1024]{2,1,0:T(8,128)S(1)} %get-tuple-element.137.refs_5_.first_ref, bf16[2,16,1024]{2,1,0:T(8,128)(2,1)S(1)} %collective-permute-done.19.above_ref), custom_call_target="tpu_custom_call" | custom-call | flops 134217728 | bytes 607232 | tf_op jit(solution)/shard_map/pallas_call | solution.py:454
  66.1 2.8 %collective-permute-done.24.below_ref = bf16[2,16,1024]{2,1,0:T(8,128)(2,1)S(1)} collective-permute-done((bf16[2,16,1024]{2,1,0:T(8,128)(2,1)S(1)}, bf16[2,16,1024]{2,1,0:T(8,128)(2,1)S(1)}, u32[]{:S(2)}, u32[]{:S(2)}) %collective-permute-start.24) | collective-permute-done | bytes 65568 | tf_op jit(solution)/shard_map/ppermute | solution.py:39
  68.9 0.9 %shard_map.71 = f32[64,2,1024]{2,1,0:T(2,128)} custom-call(f32[2,64,1024]{2,1,0:T(8,128)S(1)} %shard_map.70.all_ref, bf16[2,16,1024]{2,1,0:T(8,128)(2,1)S(1)} %collective-permute-done.24.below_ref), custom_call_target="tpu_custom_call" | custom-call | flops 134217728 | bytes 589824 | tf_op jit(solution)/shard_map/pallas_call | solution.py:454
  (15 shorter events, 0.3 us)
Async XLA Ops:
  2.4 4.5 %copy-start = (bf16[2,1024,1024]{2,1,0:T(8,128)(2,1)S(1)}, bf16[2,1024,1024]{2,1,0:T(8,128)(2,1)}, u32[]{:S(2)}) copy-start(bf16[2,1024,1024]{2,1,0:T(8,128)(2,1)} %diag_ref.15) | copy-start | bytes 12582916
  2.5 4.5 %collective-permute-start = (bf16[64,1024]{1,0:T(8,128)(2,1)S(1)}, bf16[64,1024]{1,0:T(8,128)(2,1)S(1)}, u32[]{:S(2)}, u32[]{:S(2)}) collective-permute-start(bf16[64,1024]{1,0:T(8,128)(2,1)S(1)} %get-tuple-element.77), channel_id=1, source_target_pairs={{0,1},{1,0},{2,3},{3,2},{4,5},{5,4},{6,7},{7,6},{8,9},{9,8},{10,11... | collective-permute-start | bytes 393224 | tf_op jit(solution)/shard_map/ppermute | solution.py:30
  3.0 6.4 %collective-permute-start.1 = (bf16[64,1024]{1,0:T(8,128)(2,1)S(1)}, bf16[64,1024]{1,0:T(8,128)(2,1)S(1)}, u32[]{:S(2)}, u32[]{:S(2)}) collective-permute-start(bf16[64,1024]{1,0:T(8,128)(2,1)S(1)} %get-tuple-element.84), channel_id=1, source_target_pairs={{0,8},{1,2},{2,1},{3,4},{4,3},{5,6},{6,5},{7,15},{8,0},{9,10},{10,... | collective-permute-start | bytes 393224 | tf_op jit(solution)/shard_map/ppermute | solution.py:30
  9.3 1.4 %collective-permute-start.2 = (bf16[64,1024]{1,0:T(8,128)(2,1)S(1)}, bf16[64,1024]{1,0:T(8,128)(2,1)S(1)}, u32[]{:S(2)}, u32[]{:S(2)}) collective-permute-start(bf16[64,1024]{1,0:T(8,128)(2,1)S(1)} %get-tuple-element.86), channel_id=1, source_target_pairs={{0,1},{1,0},{2,3},{3,2},{4,5},{5,4},{6,7},{7,6},{8,9},{9,8},{10,11... | collective-permute-start | bytes 393224 | tf_op jit(solution)/shard_map/ppermute | solution.py:30
  9.5 5.0 %collective-permute-start.3 = (bf16[64,1024]{1,0:T(8,128)(2,1)S(1)}, bf16[64,1024]{1,0:T(8,128)(2,1)S(1)}, u32[]{:S(2)}, u32[]{:S(2)}) collective-permute-start(bf16[64,1024]{1,0:T(8,128)(2,1)S(1)} %shard_map.50), channel_id=1, source_target_pairs={{0,8},{1,2},{2,1},{3,4},{4,3},{5,6},{6,5},{7,15},{8,0},{9,10},{10,... | collective-permute-start | bytes 393224 | tf_op jit(solution)/shard_map/ppermute | solution.py:30
  13.1 2.6 %collective-permute-start.4 = (bf16[64,1024]{1,0:T(8,128)(2,1)S(1)}, bf16[64,1024]{1,0:T(8,128)(2,1)S(1)}, u32[]{:S(2)}, u32[]{:S(2)}) collective-permute-start(bf16[64,1024]{1,0:T(8,128)(2,1)S(1)} %get-tuple-element.90), channel_id=1, source_target_pairs={{0,1},{1,0},{2,3},{3,2},{4,5},{5,4},{6,7},{7,6},{8,9},{9,8},{10,11... | collective-permute-start | bytes 393224 | tf_op jit(solution)/shard_map/ppermute | solution.py:30
  14.6 5.0 %collective-permute-start.5 = (bf16[64,1024]{1,0:T(8,128)(2,1)S(1)}, bf16[64,1024]{1,0:T(8,128)(2,1)S(1)}, u32[]{:S(2)}, u32[]{:S(2)}) collective-permute-start(bf16[64,1024]{1,0:T(8,128)(2,1)S(1)} %shard_map.53), channel_id=1, source_target_pairs={{0,8},{1,2},{2,1},{3,4},{4,3},{5,6},{6,5},{7,15},{8,0},{9,10},{10,... | collective-permute-start | bytes 393224 | tf_op jit(solution)/shard_map/ppermute | solution.py:30
  18.1 2.7 %collective-permute-start.6 = (bf16[64,1024]{1,0:T(8,128)(2,1)S(1)}, bf16[64,1024]{1,0:T(8,128)(2,1)S(1)}, u32[]{:S(2)}, u32[]{:S(2)}) collective-permute-start(bf16[64,1024]{1,0:T(8,128)(2,1)S(1)} %get-tuple-element.95), channel_id=1, source_target_pairs={{0,1},{1,0},{2,3},{3,2},{4,5},{5,4},{6,7},{7,6},{8,9},{9,8},{10,11... | collective-permute-start | bytes 393224 | tf_op jit(solution)/shard_map/ppermute | solution.py:30
  19.6 5.0 %collective-permute-start.7 = (bf16[64,1024]{1,0:T(8,128)(2,1)S(1)}, bf16[64,1024]{1,0:T(8,128)(2,1)S(1)}, u32[]{:S(2)}, u32[]{:S(2)}) collective-permute-start(bf16[64,1024]{1,0:T(8,128)(2,1)S(1)} %shard_map.56), channel_id=1, source_target_pairs={{0,8},{1,2},{2,1},{3,4},{4,3},{5,6},{6,5},{7,15},{8,0},{9,10},{10,... | collective-permute-start | bytes 393224 | tf_op jit(solution)/shard_map/ppermute | solution.py:30
  23.2 2.7 %collective-permute-start.8 = (bf16[64,1024]{1,0:T(8,128)(2,1)S(1)}, bf16[64,1024]{1,0:T(8,128)(2,1)S(1)}, u32[]{:S(2)}, u32[]{:S(2)}) collective-permute-start(bf16[64,1024]{1,0:T(8,128)(2,1)S(1)} %get-tuple-element.101), channel_id=1, source_target_pairs={{0,1},{1,0},{2,3},{3,2},{4,5},{5,4},{6,7},{7,6},{8,9},{9,8},{10,11... | collective-permute-start | bytes 393224 | tf_op jit(solution)/shard_map/ppermute | solution.py:30
  24.7 5.0 %collective-permute-start.9 = (bf16[64,1024]{1,0:T(8,128)(2,1)S(1)}, bf16[64,1024]{1,0:T(8,128)(2,1)S(1)}, u32[]{:S(2)}, u32[]{:S(2)}) collective-permute-start(bf16[64,1024]{1,0:T(8,128)(2,1)S(1)} %shard_map.58), channel_id=1, source_target_pairs={{0,8},{1,2},{2,1},{3,4},{4,3},{5,6},{6,5},{7,15},{8,0},{9,10},{10,... | collective-permute-start | bytes 393224 | tf_op jit(solution)/shard_map/ppermute | solution.py:30
  28.8 2.1 %collective-permute-start.10 = (bf16[64,1024]{1,0:T(8,128)(2,1)S(1)}, bf16[64,1024]{1,0:T(8,128)(2,1)S(1)}, u32[]{:S(2)}, u32[]{:S(2)}) collective-permute-start(bf16[64,1024]{1,0:T(8,128)(2,1)S(1)} %get-tuple-element.107), channel_id=1, source_target_pairs={{0,1},{1,0},{2,3},{3,2},{4,5},{5,4},{6,7},{7,6},{8,9},{9,8},{10,11... | collective-permute-start | bytes 393224 | tf_op jit(solution)/shard_map/ppermute | solution.py:30
  28.9 2.1 %collective-permute-start.11 = (f32[64,64]{1,0:T(8,128)S(1)}, f32[64,64]{1,0:T(8,128)S(1)}, u32[]{:S(2)}, u32[]{:S(2)}) collective-permute-start(f32[64,64]{1,0:T(8,128)S(1)} %get-tuple-element.110.refs_0_), channel_id=1, source_target_pairs={{0,1},{1,0},{2,3},{3,2},{4,5},{5,4},{6,7},{7,6},{8,9},{9,8},{10,11... | collective-permute-start | bytes 49160 | tf_op jit(solution)/shard_map/ppermute | solution.py:49
  29.8 5.5 %collective-permute-start.12 = (bf16[64,1024]{1,0:T(8,128)(2,1)S(1)}, bf16[64,1024]{1,0:T(8,128)(2,1)S(1)}, u32[]{:S(2)}, u32[]{:S(2)}) collective-permute-start(bf16[64,1024]{1,0:T(8,128)(2,1)S(1)} %shard_map.60), channel_id=1, source_target_pairs={{0,8},{1,2},{2,1},{3,4},{4,3},{5,6},{6,5},{7,15},{8,0},{9,10},{10,... | collective-permute-start | bytes 393224 | tf_op jit(solution)/shard_map/ppermute | solution.py:30
  33.4 3.7 %collective-permute-start.13 = (bf16[64,1024]{1,0:T(8,128)(2,1)S(1)}, bf16[64,1024]{1,0:T(8,128)(2,1)S(1)}, u32[]{:S(2)}, u32[]{:S(2)}) collective-permute-start(bf16[64,1024]{1,0:T(8,128)(2,1)S(1)} %get-tuple-element.114), channel_id=1, source_target_pairs={{0,1},{1,0},{2,3},{3,2},{4,5},{5,4},{6,7},{7,6},{8,9},{9,8},{10,11... | collective-permute-start | bytes 393224 | tf_op jit(solution)/shard_map/ppermute | solution.py:30
  33.7 3.3 %collective-permute-start.14 = (f32[64,64]{1,0:T(8,128)S(1)}, f32[64,64]{1,0:T(8,128)S(1)}, u32[]{:S(2)}, u32[]{:S(2)}) collective-permute-start(f32[64,64]{1,0:T(8,128)S(1)} %get-tuple-element.117.refs_0_), channel_id=1, source_target_pairs={{0,3},{1,2},{2,1},{3,0},{4,7},{5,6},{6,5},{7,4},{8,11},{9,10},{10,... | collective-permute-start | bytes 49160 | tf_op jit(solution)/shard_map/ppermute | solution.py:49
  35.3 5.0 %collective-permute-start.15 = (bf16[64,1024]{1,0:T(8,128)(2,1)S(1)}, bf16[64,1024]{1,0:T(8,128)(2,1)S(1)}, u32[]{:S(2)}, u32[]{:S(2)}) collective-permute-start(bf16[64,1024]{1,0:T(8,128)(2,1)S(1)} %shard_map.62), channel_id=1, source_target_pairs={{0,8},{1,2},{2,1},{3,4},{4,3},{5,6},{6,5},{7,15},{8,0},{9,10},{10,... | collective-permute-start | bytes 393224 | tf_op jit(solution)/shard_map/ppermute | solution.py:30
  39.7 4.7 %collective-permute-start.16 = (bf16[64,1024]{1,0:T(8,128)(2,1)S(1)}, bf16[64,1024]{1,0:T(8,128)(2,1)S(1)}, u32[]{:S(2)}, u32[]{:S(2)}) collective-permute-start(bf16[64,1024]{1,0:T(8,128)(2,1)S(1)} %get-tuple-element.121), channel_id=1, source_target_pairs={{0,1},{1,0},{2,3},{3,2},{4,5},{5,4},{6,7},{7,6},{8,9},{9,8},{10,11... | collective-permute-start | bytes 393224 | tf_op jit(solution)/shard_map/ppermute | solution.py:30
  40.4 7.0 %collective-permute-start.17 = (bf16[64,1024]{1,0:T(8,128)(2,1)S(1)}, bf16[64,1024]{1,0:T(8,128)(2,1)S(1)}, u32[]{:S(2)}, u32[]{:S(2)}) collective-permute-start(bf16[64,1024]{1,0:T(8,128)(2,1)S(1)} %shard_map.64), channel_id=1, source_target_pairs={{0,8},{1,2},{2,1},{3,4},{4,3},{5,6},{6,5},{7,15},{8,0},{9,10},{10,... | collective-permute-start | bytes 393224 | tf_op jit(solution)/shard_map/ppermute | solution.py:30
  41.3 5.6 %collective-permute-start.18 = (f32[64,64]{1,0:T(8,128)S(1)}, f32[64,64]{1,0:T(8,128)S(1)}, u32[]{:S(2)}, u32[]{:S(2)}) collective-permute-start(f32[64,64]{1,0:T(8,128)S(1)} %get-tuple-element.126.refs_0_), channel_id=1, source_target_pairs={{0,5},{1,4},{2,7},{3,6},{4,1},{5,0},{6,3},{7,2},{8,13},{9,12},{10,... | collective-permute-start | bytes 49160 | tf_op jit(solution)/shard_map/ppermute | solution.py:49
  47.9 4.8 %collective-permute-start.19 = (bf16[2,16,1024]{2,1,0:T(8,128)(2,1)S(1)}, bf16[2,16,1024]{2,1,0:T(8,128)(2,1)S(1)}, u32[]{:S(2)}, u32[]{:S(2)}) collective-permute-start(bf16[2,16,1024]{2,1,0:T(8,128)(2,1)S(1)} %get-tuple-element.133), channel_id=1, source_target_pairs={{0,24},{8,0},{16,8},{24,16},{1,25},{9,1},{17,9},{25,17},{2,26},{10... | collective-permute-start | bytes 196616 | tf_op jit(solution)/shard_map/ppermute | solution.py:39
  53.0 1.3 %collective-permute-start.20 = (f32[64,96]{1,0:T(8,128)S(1)}, f32[64,96]{1,0:T(8,128)S(1)}, u32[]{:S(2)}, u32[]{:S(2)}) collective-permute-start(f32[64,96]{1,0:T(8,128)S(1)} %shard_map.67), channel_id=1, source_target_pairs={{0,1},{1,0},{2,3},{3,2},{4,5},{5,4},{6,7},{7,6},{8,9},{9,8},{10,11... | collective-permute-start | bytes 73736 | tf_op jit(solution)/shard_map/ppermute | solution.py:49
  54.3 6.2 %collective-permute-start.23 = (f32[64,96]{1,0:T(8,128)S(1)}, f32[64,96]{1,0:T(8,128)S(1)}, u32[]{:S(2)}, u32[]{:S(2)}) collective-permute-start(f32[64,96]{1,0:T(8,128)S(1)} %add.3.refs_0_), channel_id=1, source_target_pairs={{0,7},{1,6},{2,5},{3,4},{4,3},{5,2},{6,1},{7,0},{8,15},{9,14},{10,... | collective-permute-start | bytes 73736 | tf_op jit(solution)/shard_map/ppermute | solution.py:49
  56.3 4.5 %collective-permute-start.22 = (f32[64,96]{1,0:T(8,128)S(1)}, f32[64,96]{1,0:T(8,128)S(1)}, u32[]{:S(2)}, u32[]{:S(2)}) collective-permute-start(f32[64,96]{1,0:T(8,128)S(1)} %add.3.refs_0_), channel_id=1, source_target_pairs={{0,5},{1,4},{2,7},{3,6},{4,1},{5,0},{6,3},{7,2},{8,13},{9,12},{10,... | collective-permute-start | bytes 73736 | tf_op jit(solution)/shard_map/ppermute | solution.py:49
  56.3 4.5 %collective-permute-start.21 = (f32[64,96]{1,0:T(8,128)S(1)}, f32[64,96]{1,0:T(8,128)S(1)}, u32[]{:S(2)}, u32[]{:S(2)}) collective-permute-start(f32[64,96]{1,0:T(8,128)S(1)} %add.3.refs_0_), channel_id=1, source_target_pairs={{0,3},{1,2},{2,1},{3,0},{4,7},{5,6},{6,5},{7,4},{8,11},{9,10},{10,... | collective-permute-start | bytes 73736 | tf_op jit(solution)/shard_map/ppermute | solution.py:49
  63.7 5.2 %collective-permute-start.24 = (bf16[2,16,1024]{2,1,0:T(8,128)(2,1)S(1)}, bf16[2,16,1024]{2,1,0:T(8,128)(2,1)S(1)}, u32[]{:S(2)}, u32[]{:S(2)}) collective-permute-start(bf16[2,16,1024]{2,1,0:T(8,128)(2,1)S(1)} %get-tuple-element.140), channel_id=1, source_target_pairs={{0,8},{8,16},{16,24},{24,0},{1,9},{9,17},{17,25},{25,1},{2,10},{10... | collective-permute-start | bytes 196616 | tf_op jit(solution)/shard_map/ppermute | solution.py:39

commit v4 on v3

--- a/solution.py
+++ b/solution.py
@@ -337,55 +337,44 @@
     return lax.rsqrt(jnp.sum(gram * identity(gram.shape[0]), axis=1, keepdims=True))
 
 
+def outer_kernel(count, rows_ref, base_ref, arrived_ref, last_t_ref, next_ref):
+    def store(block):
+        next_ref[...] = block
+
+    add_arrived(count, rows_ref[2:3], base_ref, arrived_ref, last_t_ref, store)
+
+
 def scale_kernel(parts, length, *refs):
-    grams, (rest_ref, next_ref, next16_ref, gram_ref, scales_ref) = refs[:parts], refs[parts:]
+    grams, (outer_ref, rest_ref, all_ref, all16_ref, low_ref, gram_ref) = refs[:parts], refs[parts:]
     scales = row_scales(sum(ref[...] for ref in grams) * (1.0 / length))
-    scales_ref[...] = jnp.broadcast_to(scales, scales_ref.shape)
-    gram_ref[...] = jnp.zeros(gram_ref.shape, F32)
-    for i in range(rest_ref.shape[0]):
-        block = rest_ref[i] * scales
-        next_ref[i] = block
-        next16_ref[i] = block.astype(BF16)
-        gram_ref[...] += product_t(block, block, HIGHEST)
-
-
-def last_kernel(
-    count, rows_ref, base_ref, arrived_ref, last_t_ref, scales_ref, rest16_ref, rest_gram_ref,
-    next_ref, next16_ref, low_ref, gram_ref,
-):
-    def store(block):
-        next_ref[...] = block * scales_ref[:, :1]
-
-    add_arrived(count, rows_ref[2:3], base_ref, arrived_ref, last_t_ref, store)
-    next16_ref[...] = next_ref[...].astype(BF16)
     edge = low_ref.shape[1]
-    low_ref[0] = next16_ref[:edge]
-    for i in range(low_ref.shape[0] - 1):
-        low_ref[i + 1] = rest16_ref[i, :edge]
-    gram_ref[...] = rest_gram_ref[...] + product_t(next_ref[...], next_ref[...], HIGHEST)
+    total = 0.0
+    for i in range(all_ref.shape[0]):
+        block = (rest_ref[i - 1] if i else outer_ref[...]) * scales
+        all_ref[i] = block
+        rounded = block.astype(BF16)
+        all16_ref[i] = rounded
+        low_ref[i] = rounded[:edge]
+        total = total + product_t(block, block, HIGHEST)
+    gram_ref[...] = total
 
 
 def first_factor_kernel(parts, length, *refs):
-    grams, (outer_ref, rest_ref, inverse_ref, all_ref) = refs[:parts], refs[parts:]
+    grams, (scaled_ref, inverse_ref, all_ref) = refs[:parts], refs[parts:]
     gram = sum(ref[...] for ref in grams) * (1.0 / length)
     scales = row_scales(gram)
     across = jnp.sum(identity(gram.shape[0]) * scales, axis=0, keepdims=True)
     inverse_ref[...] = inverse_factors(gram * scales * across)[0]
-    all_ref[0] = exact(inverse_ref[...], outer_ref[...])
-    for i in range(rest_ref.shape[0]):
-        all_ref[i + 1] = exact(inverse_ref[...], rest_ref[i])
-
-
-def cross_kernel(gram_ref, outer16_ref, rest16_ref, above_ref, out_ref):
-    size, edge = outer16_ref.shape[0], above_ref.shape[1]
-    rest = range(rest16_ref.shape[0])
+    for i in range(all_ref.shape[0]):
+        all_ref[i] = exact(inverse_ref[...], scaled_ref[i])
+
+
+def cross_kernel(gram_ref, all16_ref, above_ref, out_ref):
+    size, edge = gram_ref.shape[0], above_ref.shape[1]
+    places = range(above_ref.shape[0])
     out_ref[:, :size] = gram_ref[...]
-    out_ref[:, size : size + edge] = product_t(outer16_ref[...], above_ref[0]) + sum(
-        product_t(rest16_ref[i], above_ref[i + 1]) for i in rest
-    )
-    out_ref[:edge, size + edge :] = sum(
-        product_t(above_ref[l], above_ref[l]) for l in range(above_ref.shape[0])
-    )
+    out_ref[:, size : size + edge] = sum(product_t(all16_ref[i], above_ref[i]) for i in places)
+    out_ref[:edge, size + edge :] = sum(product_t(above_ref[i], above_ref[i]) for i in places)
     out_ref[edge:, size + edge :] = jnp.zeros((size - edge, edge), F32)
 
 
@@ -404,32 +393,49 @@
     correlation = product_t(exact(high, cross), above, HIGHEST)
     up = exact(correlation.T, high)
     for i in range(all_ref.shape[0]):
-        up_ref[i] = exact(up, all_ref[i]).astype(BF16)
+        up_ref[i] = jnp.dot(up.astype(BF16), all_ref[i].astype(BF16), preferred_element_type=F32).astype(BF16)
     weights_ref[...] = exact(correlation, above)
 
 
-def vectors_kernel(inverse_ref, weights_ref, first_ref, above_ref, all_ref):
-    layers, size, _ = all_ref.shape
-    edge = above_ref.shape[1]
+def by_layer(layers, store):
+    for parity in (0, 1):
+
+        @pl.when(position("layer") % 2 == parity)
+        def _():
+            for place, layer in enumerate(range(layers)[:: -1 if parity else 1]):
+                store(layer, place)
+
+
+def vectors_kernel(inverse_ref, weights_ref, first_ref, above_ref, low_ref, out_ref, block_ref, sem):
+    layers, size, _ = first_ref.shape
+    edge = low_ref.shape[1]
+    blocks = []
     for i in range(layers):
         block = exact(inverse_ref[...], first_ref[i])
-        all_ref[i] = block
-        all_ref[i, size - edge :] = block[size - edge :] - exact(
-            weights_ref[...], above_ref[i].astype(F32)
-        )
-
-
-def final_kernel(all_ref, below_ref, out_ref):
-    layers, size, _ = all_ref.shape
-    edge = below_ref.shape[1]
+        high = block[size - edge :] - exact(weights_ref[...], above_ref[i].astype(F32))
+        low_ref[i] = block[:edge]
+        blocks.append(jnp.concatenate([block[edge : size - edge], high], 0))
+
+    def store(layer, place):
+        block_ref[:, layer, :] = blocks[place]
+
+    by_layer(layers, store)
+    copy = pltpu.make_async_copy(block_ref, out_ref.at[pl.ds(edge, size - edge)], sem)
+    copy.start()
+    copy.wait()
+
+
+def final_kernel(low_ref, below_ref, _, out_ref, block_ref, sem):
+    layers, edge, _ = low_ref.shape
     has_below = (position("cuts") > 0).astype(F32)
-    for parity in (0, 1):
-
-        @pl.when(position("layer") % 2 == parity)
-        def _():
-            for i, l in enumerate(range(layers)[:: -1 if parity else 1]):
-                out_ref[:edge, l, :] = all_ref[i, :edge] - below_ref[i].astype(F32) * has_below
-                out_ref[edge:, l, :] = all_ref[i, edge:]
+
+    def store(layer, place):
+        block_ref[:, layer, :] = low_ref[place] - below_ref[place].astype(F32) * has_below
+
+    by_layer(layers, store)
+    copy = pltpu.make_async_copy(block_ref, out_ref.at[pl.ds(0, edge)], sem)
+    copy.start()
+    copy.wait()
 
 
 def per_device(vectors, diag_blocks, couplings, bounds):
@@ -449,13 +455,17 @@
     edges = array(BF16, layers, EDGE, width)
     one = 2 * count_vec * width * width
 
-    def call(kernel, outs, *operands, far=(), scratch_shapes=(), flops=one, aliases=()):
+    def call(kernel, outs, *operands, far=(), far_out=(), scratch_shapes=(), flops=one, aliases=()):
         moved = sum(x.size * x.dtype.itemsize for x in operands)
         return pl.pallas_call(
             kernel,
             out_shape=outs,
             in_specs=[HBM if i in far else VMEM for i in range(len(operands))],
-            out_specs=jax.tree.map(lambda _: VMEM, outs),
+            out_specs=(
+                tuple(HBM if i in far_out else VMEM for i in range(len(outs)))
+                if isinstance(outs, tuple)
+                else VMEM
+            ),
             scratch_shapes=list(scratch_shapes),
             input_output_aliases=dict(aliases),
             compiler_params=pltpu.CompilerParams(vmem_limit_bytes=32 * 2**20),
@@ -497,7 +507,7 @@
             rest, outer_now, rest_before,
             *((total, swapped(total, reaches.pop(0))) if adds else ()),
             scratch_shapes=[pltpu.VMEM((count_vec, width), F32)],
-            flops=(3 * layers - 1) * one,
+            flops=int(2 * (3 * layers - 1) * one),
         )
         if step:
             outer_now = extra.pop(0)
@@ -524,22 +534,20 @@
     totals = [total]
     for reach in reaches:
         totals = [sum(totals), swapped(sum(totals), reach)]
-    rest, rest_r, rest_gram, scales = call(
+    outer = call(functools.partial(outer_kernel, count), outer32, rows, base, outer_in, last_t)
+    field32 = array(F32, layers, count_vec, width)
+    field16 = array(BF16, layers, count_vec, width)
+    scaled, scaled_r, low, gram = call(
         functools.partial(scale_kernel, len(totals), length_all),
-        (rest32, rest16, square, array(F32, count_vec, 128)), *totals, rest_next,
-    )
-    outer, outer_r, low, gram = call(
-        functools.partial(last_kernel, count), (outer32, outer16, edges, square),
-        rows, base, outer_in, last_t, scales, rest_r, rest_gram,
+        (field32, field16, edges, square), *totals, outer, rest_next,
     )
     above = rotated(low, -1)
-    field32 = array(F32, layers, count_vec, width)
     cross = call(
-        cross_kernel, array(F32, count_vec, count_vec + 2 * EDGE), gram, outer_r, rest_r, above
+        cross_kernel, array(F32, count_vec, count_vec + 2 * EDGE), gram, scaled_r, above
     )
     first, first_all = call(
         functools.partial(first_factor_kernel, len(totals), length_all),
-        (square, field32), *totals, outer, rest,
+        (square, field32), *totals, scaled,
     )
     grams = partial_sums(cross)
     inverse, weights, up = call(
@@ -547,8 +555,18 @@
         (square, array(F32, EDGE, EDGE), edges), *grams, first, first_all,
     )
     below = rotated(up, 1)
-    vectors_all = call(vectors_kernel, field32, inverse, weights, first_all, above)
-    result = call(final_kernel, array(F32, count_vec, layers, width), vectors_all, below)
+    whole = array(F32, count_vec, layers, width)
+    low, result = call(
+        vectors_kernel, (array(F32, layers, EDGE, width), whole),
+        inverse, weights, first_all, above, far_out=(1,),
+        scratch_shapes=[
+            pltpu.VMEM((count_vec - EDGE, layers, width), F32), pltpu.SemaphoreType.DMA,
+        ],
+    )
+    (result,) = call(
+        final_kernel, (whole,), low, below, result, far=(2,), far_out=(0,), aliases={2: 0},
+        scratch_shapes=[pltpu.VMEM((EDGE, layers, width), F32), pltpu.SemaphoreType.DMA],
+    )
     return result[None]
 
 

time: 70 us -> 69.6 us (level)
  waiting for transfers between devices: 12.7 us -> 11.9 us
    ppermute x2, waiting for transfers between devices: 5.92 us -> 4.94 us  [rotated(): lax.ppermute(block, 'cuts', [(i, (i + distance) % size) for i in range(si...]
  transfers between devices with their start and end apart: 25 -> 25, of which waited for: 11 -> 11; matrix products, arithmetic and copies ran while one was open for 0% -> 0% of each run, Pallas kernels for 36% -> 37%
where the time goes in v4:
time: 69.6 us; the launch traced here: 69.5 us
  Pallas kernels  32.4 us (47%)
  starting transfers between devices  24.7 us (35%)
  waiting for transfers between devices  11.9 us (17%)
    pallas_call x26, Pallas kernels, call(): pl.pallas_call(kernel, out_shape=outs, in_specs=[HBM if i in far else VME...  32.4 us
    ppermute x16, starting transfers between devices, exchanged(): return lax.ppermute(block, ('cuts', 'layer'), route)  12.1 us
    ppermute x7, starting transfers between devices, swapped(): lax.ppermute(block, 'layer', [(i, i ^ far) for i in range(lax.axis_size('...  9.06 us
    ppermute x2, waiting for transfers between devices, rotated(): lax.ppermute(block, 'cuts', [(i, (i + distance) % size) for i in range(si...  4.94 us
    ppermute x16, waiting for transfers between devices, exchanged(): return lax.ppermute(block, ('cuts', 'layer'), route)  4.45 us
    ppermute x2, starting transfers between devices, rotated(): lax.ppermute(block, 'cuts', [(i, (i + distance) % size) for i in range(si...  3.5 us
    ppermute x7, waiting for transfers between devices, swapped(): lax.ppermute(block, 'layer', [(i, i ^ far) for i in range(lax.axis_size('...  2.5 us
  transfers between devices with their start and end apart: 25, of which 11 were waited for; matrix products, arithmetic and copies ran while one was open for 0% of the time, Pallas kernels for 37%

profile of v4, /device:TPU:0, one launch (start us, length us, event | category | flops | bytes accessed | tf_op | source)
XLA Modules:
  0.0 69.5 jit_solution(15615047439914238777)
XLA Ops:
  0.0 2.4 %shard_map.46 = (f32[64,1024]{1,0:T(8,128)S(1)}, f32[1,64,1024]{2,1,0:T(8,128)S(1)}, bf16[64,1024]{1,0:T(8,128)(2,1)S(1)}, bf16[1,64,1024]{2,1,0:T(8,128)(2,1)S(...) custom-call(s32[1,2]{1,0:T(1,128)} %far_bounds_ref.1, ...), custom_call_target="tpu_custom_call" | custom-call | flops 134217728 | bytes 4718600 | tf_op jit(solution)/shard_map/pallas_call | solution.py:460
  2.4 0.0 copy-start
  2.5 0.5 collective-permute-start
  3.0 2.6 %collective-permute-start.1 = (bf16[64,1024]{1,0:T(8,128)(2,1)S(1)}, bf16[64,1024]{1,0:T(8,128)(2,1)S(1)}, u32[]{:S(2)}, u32[]{:S(2)}) collective-permute-start(bf16[64,1024]{1,0:T(8,128)(2,1)S(1)} %get-tuple-element.82), channel_id=1, source_target_pairs={{0,8},{1,2},{2,1},{3,4},{4,3},{5,6},{6,5},{7,15},{8,0},{9,10},{10,... | collective-permute-start | bytes 393224 | tf_op jit(solution)/shard_map/ppermute | solution.py:30
  5.5 1.4 %shard_map.47 = (bf16[1024,1024]{1,0:T(8,128)(2,1)S(1)}, bf16[2,1,1024,1024]{3,2,1,0:T(8,128)(2,1)S(1)}) custom-call(bf16[1024,1024]{1,0:T(8,128)(2,1)S(1)} %get-tuple-element.76.last_ref, bf16[2,1,1024,1024]{3,2,1,0:T(8,128)(2,1)S(1)} %get-tuple-element.77.mids_in_ref), custom_call_target="tpu_custom_call", output_to_operand_aliasing={{1}: (1, {})} | custom-call | flops 134217728 | bytes 6291456 | tf_op jit(solution)/shard_map/pallas_call | solution.py:460
  6.9 0.0 collective-permute-done.arrived_ref
  7.0 2.4 %shard_map.48 = (f32[64,1024]{1,0:T(8,128)S(1)}, f32[1,64,1024]{2,1,0:T(8,128)S(1)}, bf16[1,64,1024]{2,1,0:T(8,128)(2,1)S(1)}, bf16[64,1024]{1,0:T(8,128)(2,1)S(1)}) custom-call(f32[8,1024]{1,0:T(8,128)S(1)} %get-tuple-element.71.rows_ref, f32[64,1024]{1,0:T(8,128)S(1)} %get-tuple-element.72.outer_a_ref.outer_before_ref, ...), custom_call_target="tpu_custom_call" | custom-call | flops 1342177280 | bytes 14057472 | tf_op jit(solution)/shard_map/pallas_call | solution.py:460
  9.3 0.1 collective-permute-start.2
  9.4 0.1 shard_map.50
  9.5 1.1 %collective-permute-start.3 = (bf16[64,1024]{1,0:T(8,128)(2,1)S(1)}, bf16[64,1024]{1,0:T(8,128)(2,1)S(1)}, u32[]{:S(2)}, u32[]{:S(2)}) collective-permute-start(bf16[64,1024]{1,0:T(8,128)(2,1)S(1)} %shard_map.50), channel_id=1, source_target_pairs={{0,8},{1,2},{2,1},{3,4},{4,3},{5,6},{6,5},{7,15},{8,0},{9,10},{10,... | collective-permute-start | bytes 393224 | tf_op jit(solution)/shard_map/ppermute | solution.py:30
  10.6 0.1 collective-permute-done.2.arrived_ref
  10.7 2.4 %shard_map.49 = (f32[64,1024]{1,0:T(8,128)S(1)}, f32[1,64,1024]{2,1,0:T(8,128)S(1)}, f32[64,1024]{1,0:T(8,128)S(1)}, bf16[1,64,1024]{2,1,0:T(8,128)(2,1)S(1)}, bf16[64,1024]{1,0:T(8,128)(2,1)S(1)}) custom-call(f32[8,1024]{1,0:T(8,128)S(1)} %get-tuple-element.71.rows_ref, f32[64,1024]{1,0:T(8,128)S(1)} %get-tuple-element.81.outer_a_ref.base_ref, ...), custom_call_target="tpu_custom_call" | custom-call | flops 1342177280 | bytes 14057472 | tf_op jit(solution)/shard_map/pallas_call | solution.py:460
  13.1 0.1 collective-permute-start.4
  13.2 1.3 %collective-permute-done.3.outer_b_ref.arrived_ref = bf16[64,1024]{1,0:T(8,128)(2,1)S(1)} collective-permute-done((bf16[64,1024]{1,0:T(8,128)(2,1)S(1)}, bf16[64,1024]{1,0:T(8,128)(2,1)S(1)}, u32[]{:S(2)}, u32[]{:S(2)}) %collective-permute-start.3) | collective-permute-done | bytes 131104 | tf_op jit(solution)/shard_map/ppermute | solution.py:30
  14.6 1.1 %collective-permute-start.5 = (bf16[64,1024]{1,0:T(8,128)(2,1)S(1)}, bf16[64,1024]{1,0:T(8,128)(2,1)S(1)}, u32[]{:S(2)}, u32[]{:S(2)}) collective-permute-start(bf16[64,1024]{1,0:T(8,128)(2,1)S(1)} %shard_map.53), channel_id=1, source_target_pairs={{0,8},{1,2},{2,1},{3,4},{4,3},{5,6},{6,5},{7,15},{8,0},{9,10},{10,... | collective-permute-start | bytes 393224 | tf_op jit(solution)/shard_map/ppermute | solution.py:30
  15.7 0.0 collective-permute-done.4.arrived_ref
  15.7 2.4 %shard_map.51 = (f32[64,1024]{1,0:T(8,128)S(1)}, f32[1,64,1024]{2,1,0:T(8,128)S(1)}, f32[64,1024]{1,0:T(8,128)S(1)}, bf16[1,64,1024]{2,1,0:T(8,128)(2,1)S(1)}, b...) custom-call(f32[8,1024]{1,0:T(8,128)S(1)} %get-tuple-element.71.rows_ref, ...), custom_call_target="tpu_custom_call" | custom-call | flops 1342177280 | bytes 14057472 | tf_op jit(solution)/shard_map/pallas_call | solution.py:460
  18.1 0.4 collective-permute-start.6
  18.5 1.1 %collective-permute-done.5.outer_b_ref.arrived_ref = bf16[64,1024]{1,0:T(8,128)(2,1)S(1)} collective-permute-done((bf16[64,1024]{1,0:T(8,128)(2,1)S(1)}, bf16[64,1024]{1,0:T(8,128)(2,1)S(1)}, u32[]{:S(2)}, u32[]{:S(2)}) %collective-permute-start.5) | collective-permute-done | bytes 131104 | tf_op jit(solution)/shard_map/ppermute | solution.py:30
  19.6 1.1 %collective-permute-start.7 = (bf16[64,1024]{1,0:T(8,128)(2,1)S(1)}, bf16[64,1024]{1,0:T(8,128)(2,1)S(1)}, u32[]{:S(2)}, u32[]{:S(2)}) collective-permute-start(bf16[64,1024]{1,0:T(8,128)(2,1)S(1)} %shard_map.56), channel_id=1, source_target_pairs={{0,8},{1,2},{2,1},{3,4},{4,3},{5,6},{6,5},{7,15},{8,0},{9,10},{10,... | collective-permute-start | bytes 393224 | tf_op jit(solution)/shard_map/ppermute | solution.py:30
  20.8 0.0 collective-permute-done.6.arrived_ref
  20.8 2.4 %shard_map.54 = (f32[64,1024]{1,0:T(8,128)S(1)}, f32[1,64,1024]{2,1,0:T(8,128)S(1)}, f32[64,1024]{1,0:T(8,128)S(1)}, bf16[1,64,1024]{2,1,0:T(8,128)(2,1)S(1)}, b...) custom-call(f32[8,1024]{1,0:T(8,128)S(1)} %get-tuple-element.71.rows_ref, ...), custom_call_target="tpu_custom_call" | custom-call | flops 1342177280 | bytes 14057472 | tf_op jit(solution)/shard_map/pallas_call | solution.py:460
  23.2 0.2 collective-permute-start.8
  23.4 1.2 %collective-permute-done.7.outer_b_ref.arrived_ref = bf16[64,1024]{1,0:T(8,128)(2,1)S(1)} collective-permute-done((bf16[64,1024]{1,0:T(8,128)(2,1)S(1)}, bf16[64,1024]{1,0:T(8,128)(2,1)S(1)}, u32[]{:S(2)}, u32[]{:S(2)}) %collective-permute-start.7) | collective-permute-done | bytes 131104 | tf_op jit(solution)/shard_map/ppermute | solution.py:30
  24.7 1.1 %collective-permute-start.9 = (bf16[64,1024]{1,0:T(8,128)(2,1)S(1)}, bf16[64,1024]{1,0:T(8,128)(2,1)S(1)}, u32[]{:S(2)}, u32[]{:S(2)}) collective-permute-start(bf16[64,1024]{1,0:T(8,128)(2,1)S(1)} %shard_map.58), channel_id=1, source_target_pairs={{0,8},{1,2},{2,1},{3,4},{4,3},{5,6},{6,5},{7,15},{8,0},{9,10},{10,... | collective-permute-start | bytes 393224 | tf_op jit(solution)/shard_map/ppermute | solution.py:30
  25.9 0.0 collective-permute-done.8.arrived_ref
  25.9 2.9 %shard_map.57 = (f32[64,1024]{1,0:T(8,128)S(1)}, f32[1,64,1024]{2,1,0:T(8,128)S(1)}, f32[64,1024]{1,0:T(8,128)S(1)}, bf16[1,64,1024]{2,1,0:T(8,128)(2,1)S(1)}, b...) custom-call(f32[8,1024]{1,0:T(8,128)S(1)} %get-tuple-element.71.rows_ref, ...), custom_call_target="tpu_custom_call" | custom-call | flops 1342177280 | bytes 14057472 | tf_op jit(solution)/shard_map/pallas_call | solution.py:460
  28.8 0.1 collective-permute-start.10
  28.9 0.5 collective-permute-start.11
  29.4 0.4 collective-permute-done.9.outer_b_ref.arrived_ref
  29.8 1.1 %collective-permute-start.12 = (bf16[64,1024]{1,0:T(8,128)(2,1)S(1)}, bf16[64,1024]{1,0:T(8,128)(2,1)S(1)}, u32[]{:S(2)}, u32[]{:S(2)}) collective-permute-start(bf16[64,1024]{1,0:T(8,128)(2,1)S(1)} %shard_map.60), channel_id=1, source_target_pairs={{0,8},{1,2},{2,1},{3,4},{4,3},{5,6},{6,5},{7,15},{8,0},{9,10},{10,... | collective-permute-start | bytes 393224 | tf_op jit(solution)/shard_map/ppermute | solution.py:30
  30.9 0.0 collective-permute-done.10.arrived_ref
  30.9 2.4 %shard_map.59 = (f32[64,1024]{1,0:T(8,128)S(1)}, f32[1,64,1024]{2,1,0:T(8,128)S(1)}, f32[64,1024]{1,0:T(8,128)S(1)}, bf16[1,64,1024]{2,1,0:T(8,128)(2,1)S(1)}, b...) custom-call(f32[8,1024]{1,0:T(8,128)S(1)} %get-tuple-element.71.rows_ref, ...), custom_call_target="tpu_custom_call" | custom-call | flops 1342177280 | bytes 14090240 | tf_op jit(solution)/shard_map/pallas_call | solution.py:460
  33.4 0.3 collective-permute-start.13
  33.7 1.6 %collective-permute-start.14 = (f32[64,64]{1,0:T(8,128)S(1)}, f32[64,64]{1,0:T(8,128)S(1)}, u32[]{:S(2)}, u32[]{:S(2)}) collective-permute-start(f32[64,64]{1,0:T(8,128)S(1)} %get-tuple-element.115.refs_0_), channel_id=1, source_target_pairs={{0,3},{1,2},{2,1},{3,0},{4,7},{5,6},{6,5},{7,4},{8,11},{9,10},{10,... | collective-permute-start | bytes 49160 | tf_op jit(solution)/shard_map/ppermute | solution.py:49
  35.3 0.0 collective-permute-done.12.outer_b_ref.arrived_ref
  35.3 0.9 %collective-permute-start.16 = (bf16[64,1024]{1,0:T(8,128)(2,1)S(1)}, bf16[64,1024]{1,0:T(8,128)(2,1)S(1)}, u32[]{:S(2)}, u32[]{:S(2)}) collective-permute-start(bf16[64,1024]{1,0:T(8,128)(2,1)S(1)} %shard_map.62), channel_id=1, source_target_pairs={{0,8},{1,2},{2,1},{3,4},{4,3},{5,6},{6,5},{7,15},{8,0},{9,10},{10,... | collective-permute-start | bytes 393224 | tf_op jit(solution)/shard_map/ppermute | solution.py:30
  36.2 0.8 %collective-permute-done.14.refs_1_ = f32[64,64]{1,0:T(8,128)S(1)} collective-permute-done((f32[64,64]{1,0:T(8,128)S(1)}, f32[64,64]{1,0:T(8,128)S(1)}, u32[]{:S(2)}, u32[]{:S(2)}) %collective-permute-start.14) | collective-permute-done | bytes 16416 | tf_op jit(solution)/shard_map/ppermute | solution.py:49
  37.1 0.0 collective-permute-done.13.arrived_ref
  37.1 2.6 %shard_map.61 = (f32[64,1024]{1,0:T(8,128)S(1)}, f32[1,64,1024]{2,1,0:T(8,128)S(1)}, f32[64,1024]{1,0:T(8,128)S(1)}, bf16[1,64,1024]{2,1,0:T(8,128)(2,1)S(1)}, b...) custom-call(f32[8,1024]{1,0:T(8,128)S(1)} %get-tuple-element.71.rows_ref, ...), custom_call_target="tpu_custom_call" | custom-call | flops 1342177280 | bytes 14090240 | tf_op jit(solution)/shard_map/pallas_call | solution.py:460
  39.7 0.3 collective-permute-start.17
  40.0 0.3 collective-permute-done.16.outer_b_ref.arrived_ref
  40.4 0.9 %collective-permute-start.18 = (bf16[64,1024]{1,0:T(8,128)(2,1)S(1)}, bf16[64,1024]{1,0:T(8,128)(2,1)S(1)}, u32[]{:S(2)}, u32[]{:S(2)}) collective-permute-start(bf16[64,1024]{1,0:T(8,128)(2,1)S(1)} %shard_map.64), channel_id=1, source_target_pairs={{0,8},{1,2},{2,1},{3,4},{4,3},{5,6},{6,5},{7,15},{8,0},{9,10},{10,... | collective-permute-start | bytes 393224 | tf_op jit(solution)/shard_map/ppermute | solution.py:30
  41.3 3.1 %collective-permute-start.15 = (f32[64,64]{1,0:T(8,128)S(1)}, f32[64,64]{1,0:T(8,128)S(1)}, u32[]{:S(2)}, u32[]{:S(2)}) collective-permute-start(f32[64,64]{1,0:T(8,128)S(1)} %get-tuple-element.116.refs_0_), channel_id=1, source_target_pairs={{0,5},{1,4},{2,7},{3,6},{4,1},{5,0},{6,3},{7,2},{8,13},{9,12},{10,... | collective-permute-start | bytes 49160 | tf_op jit(solution)/shard_map/ppermute | solution.py:49
  44.4 0.0 collective-permute-done.17.arrived_ref
  44.4 2.5 %shard_map.63 = (f32[64,1024]{1,0:T(8,128)S(1)}, f32[1,64,1024]{2,1,0:T(8,128)S(1)}, f32[64,1024]{1,0:T(8,128)}) custom-call(f32[8,1024]{1,0:T(8,128)S(1)} %get-tuple-element.71.rows_ref, f32[64,1024]{1,0:T(8,128)S(1)} %get-tuple-element.117.outer_a_ref.base_ref, bf16[64,1024]{1,0:T(8,128)(2,1)S(1)} %collective-permute-done.16.outer_b_ref.arrived_ref, ...), custom_call_target="tpu_custom_call" | custom-call | flops 1342177280 | bytes 14057472 | tf_op jit(solution)/shard_map/pallas_call | solution.py:460
  46.9 0.0 collective-permute-done.18.arrived_ref
  46.9 0.0 collective-permute-done.15.refs_1_
  47.0 0.7 shard_map.66
  47.6 1.7 %collective-permute-start.19 = (bf16[2,16,1024]{2,1,0:T(8,128)(2,1)S(1)}, bf16[2,16,1024]{2,1,0:T(8,128)(2,1)S(1)}, u32[]{:S(2)}, u32[]{:S(2)}) collective-permute-start(bf16[2,16,1024]{2,1,0:T(8,128)(2,1)S(1)} %get-tuple-element.128), channel_id=1, source_target_pairs={{0,24},{8,0},{16,8},{24,16},{1,25},{9,1},{17,9},{25,17},{2,26},{10... | collective-permute-start | bytes 196616 | tf_op jit(solution)/shard_map/ppermute | solution.py:39
  49.4 3.1 %collective-permute-done.19.above_ref = bf16[2,16,1024]{2,1,0:T(8,128)(2,1)S(1)} collective-permute-done((bf16[2,16,1024]{2,1,0:T(8,128)(2,1)S(1)}, bf16[2,16,1024]{2,1,0:T(8,128)(2,1)S(1)}, u32[]{:S(2)}, u32[]{:S(2)}) %collective-permute-start.19) | collective-permute-done | bytes 65568 | tf_op jit(solution)/shard_map/ppermute | solution.py:39
  52.5 0.3 shard_map.67
  52.8 0.1 collective-permute-start.20
  52.8 1.2 %collective-permute-done.20 = f32[64,96]{1,0:T(8,128)S(1)} collective-permute-done((f32[64,96]{1,0:T(8,128)S(1)}, f32[64,96]{1,0:T(8,128)S(1)}, u32[]{:S(2)}, u32[]{:S(2)}) %collective-permute-start.20) | collective-permute-done | bytes 24608 | tf_op jit(solution)/shard_map/ppermute | solution.py:49
  54.0 2.0 %collective-permute-start.23 = (f32[64,96]{1,0:T(8,128)S(1)}, f32[64,96]{1,0:T(8,128)S(1)}, u32[]{:S(2)}, u32[]{:S(2)}) collective-permute-start(f32[64,96]{1,0:T(8,128)S(1)} %add.3.refs_0_), channel_id=1, source_target_pairs={{0,7},{1,6},{2,5},{3,4},{4,3},{5,2},{6,1},{7,0},{8,15},{9,14},{10,... | collective-permute-start | bytes 73736 | tf_op jit(solution)/shard_map/ppermute | solution.py:49
  56.1 0.1 collective-permute-start.22
  56.1 1.8 %collective-permute-start.21 = (f32[64,96]{1,0:T(8,128)S(1)}, f32[64,96]{1,0:T(8,128)S(1)}, u32[]{:S(2)}, u32[]{:S(2)}) collective-permute-start(f32[64,96]{1,0:T(8,128)S(1)} %add.3.refs_0_), channel_id=1, source_target_pairs={{0,3},{1,2},{2,1},{3,0},{4,7},{5,6},{6,5},{7,4},{8,11},{9,10},{10,... | collective-permute-start | bytes 73736 | tf_op jit(solution)/shard_map/ppermute | solution.py:49
  57.9 2.3 %shard_map.68 = (f32[64,64]{1,0:T(8,128)S(1)}, f32[2,64,1024]{2,1,0:T(8,128)S(1)}) custom-call(f32[64,64]{1,0:T(8,128)S(1)} %get-tuple-element.116.refs_0_, f32[64,64]{1,0:T(8,128)S(1)} %collective-permute-done.15.refs_1_, f32[2,64,1024]{2,1,0:T(8,128)S(1)} %get-tuple-element.129.refs_2_), custom_call_target="tpu_custom_call" | custom-call | flops 134217728 | bytes 557056 | tf_op jit(solution)/shard_map/pallas_call | solution.py:460
  60.2 0.5 collective-permute-done.22.refs_2_
  60.7 2.7 %shard_map.69 = (f32[64,64]{1,0:T(8,128)S(1)}, f32[16,16]{1,0:T(8,128)S(1)}, bf16[2,16,1024]{2,1,0:T(8,128)(2,1)S(1)}) custom-call(f32[64,96]{1,0:T(8,128)S(1)} %add.3.refs_0_, f32[64,96]{1,0:T(8,128)S(1)} %collective-permute-done.21.refs_1_, f32[64,96]{1,0:T(8,128)S(1)} %collective-permute-done.22.refs_2_, f32[64,96]{1,0:T(8,128)S(1)} %collective-permute-done.23.refs_3_, ...), custom_call_target="tpu_custom_call" | custom-call | flops 134217728 | bytes 638976 | tf_op jit(solution)/shard_map/pallas_call | solution.py:460
  63.4 1.8 %collective-permute-start.24 = (bf16[2,16,1024]{2,1,0:T(8,128)(2,1)S(1)}, bf16[2,16,1024]{2,1,0:T(8,128)(2,1)S(1)}, u32[]{:S(2)}, u32[]{:S(2)}) collective-permute-start(bf16[2,16,1024]{2,1,0:T(8,128)(2,1)S(1)} %get-tuple-element.135), channel_id=1, source_target_pairs={{0,8},{8,16},{16,24},{24,0},{1,9},{9,17},{17,25},{25,1},{2,10},{10... | collective-permute-start | bytes 196616 | tf_op jit(solution)/shard_map/ppermute | solution.py:39
  65.2 1.6 %shard_map.70 = (f32[2,16,1024]{2,1,0:T(8,128)S(1)}, f32[64,2,1024]{2,1,0:T(2,128)}) custom-call(f32[64,64]{1,0:T(8,128)S(1)} %get-tuple-element.132.inverse_ref, f32[16,16]{1,0:T(8,128)S(1)} %get-tuple-element.133.weights_ref, f32[2,64,1024]{2,1,0:T(8,128)S(1)} %get-tuple-element.131.refs_5_.first_ref, ...), custom_call_target="tpu_custom_call" | custom-call | flops 134217728 | bytes 607232 | tf_op jit(solution)/shard_map/pallas_call | solution.py:460
  66.7 1.8 %collective-permute-done.24.below_ref = bf16[2,16,1024]{2,1,0:T(8,128)(2,1)S(1)} collective-permute-done((bf16[2,16,1024]{2,1,0:T(8,128)(2,1)S(1)}, bf16[2,16,1024]{2,1,0:T(8,128)(2,1)S(1)}, u32[]{:S(2)}, u32[]{:S(2)}) %collective-permute-start.24) | collective-permute-done | bytes 65568 | tf_op jit(solution)/shard_map/ppermute | solution.py:39
  68.6 0.7 %shard_map.71 = f32[64,2,1024]{2,1,0:T(2,128)} custom-call(f32[2,16,1024]{2,1,0:T(8,128)S(1)} %get-tuple-element.134.low_ref, bf16[2,16,1024]{2,1,0:T(8,128)(2,1)S(1)} %collective-permute-done.24.below_ref, f32[64,2,1024]{2,1,0:T(2,128)} %get-tuple-element.136._), custom_call_target="tpu_custom_call", output_to_operand_aliasing={{}: (2, {})} | custom-call | flops 134217728 | bytes 720896 | tf_op jit(solution)/shard_map/pallas_call | solution.py:460
  (15 shorter events, 0.3 us)
Async XLA Ops:
  2.4 4.5 %copy-start = (bf16[2,1024,1024]{2,1,0:T(8,128)(2,1)S(1)}, bf16[2,1024,1024]{2,1,0:T(8,128)(2,1)}, u32[]{:S(2)}) copy-start(bf16[2,1024,1024]{2,1,0:T(8,128)(2,1)} %diag_ref.15) | copy-start | bytes 12582916
  2.5 4.5 %collective-permute-start = (bf16[64,1024]{1,0:T(8,128)(2,1)S(1)}, bf16[64,1024]{1,0:T(8,128)(2,1)S(1)}, u32[]{:S(2)}, u32[]{:S(2)}) collective-permute-start(bf16[64,1024]{1,0:T(8,128)(2,1)S(1)} %get-tuple-element.75), channel_id=1, source_target_pairs={{0,1},{1,0},{2,3},{3,2},{4,5},{5,4},{6,7},{7,6},{8,9},{9,8},{10,11... | collective-permute-start | bytes 393224 | tf_op jit(solution)/shard_map/ppermute | solution.py:30
  3.0 6.4 %collective-permute-start.1 = (bf16[64,1024]{1,0:T(8,128)(2,1)S(1)}, bf16[64,1024]{1,0:T(8,128)(2,1)S(1)}, u32[]{:S(2)}, u32[]{:S(2)}) collective-permute-start(bf16[64,1024]{1,0:T(8,128)(2,1)S(1)} %get-tuple-element.82), channel_id=1, source_target_pairs={{0,8},{1,2},{2,1},{3,4},{4,3},{5,6},{6,5},{7,15},{8,0},{9,10},{10,... | collective-permute-start | bytes 393224 | tf_op jit(solution)/shard_map/ppermute | solution.py:30
  9.3 1.4 %collective-permute-start.2 = (bf16[64,1024]{1,0:T(8,128)(2,1)S(1)}, bf16[64,1024]{1,0:T(8,128)(2,1)S(1)}, u32[]{:S(2)}, u32[]{:S(2)}) collective-permute-start(bf16[64,1024]{1,0:T(8,128)(2,1)S(1)} %get-tuple-element.84), channel_id=1, source_target_pairs={{0,1},{1,0},{2,3},{3,2},{4,5},{5,4},{6,7},{7,6},{8,9},{9,8},{10,11... | collective-permute-start | bytes 393224 | tf_op jit(solution)/shard_map/ppermute | solution.py:30
  9.5 5.0 %collective-permute-start.3 = (bf16[64,1024]{1,0:T(8,128)(2,1)S(1)}, bf16[64,1024]{1,0:T(8,128)(2,1)S(1)}, u32[]{:S(2)}, u32[]{:S(2)}) collective-permute-start(bf16[64,1024]{1,0:T(8,128)(2,1)S(1)} %shard_map.50), channel_id=1, source_target_pairs={{0,8},{1,2},{2,1},{3,4},{4,3},{5,6},{6,5},{7,15},{8,0},{9,10},{10,... | collective-permute-start | bytes 393224 | tf_op jit(solution)/shard_map/ppermute | solution.py:30
  13.1 2.6 %collective-permute-start.4 = (bf16[64,1024]{1,0:T(8,128)(2,1)S(1)}, bf16[64,1024]{1,0:T(8,128)(2,1)S(1)}, u32[]{:S(2)}, u32[]{:S(2)}) collective-permute-start(bf16[64,1024]{1,0:T(8,128)(2,1)S(1)} %get-tuple-element.88), channel_id=1, source_target_pairs={{0,1},{1,0},{2,3},{3,2},{4,5},{5,4},{6,7},{7,6},{8,9},{9,8},{10,11... | collective-permute-start | bytes 393224 | tf_op jit(solution)/shard_map/ppermute | solution.py:30
  14.6 5.0 %collective-permute-start.5 = (bf16[64,1024]{1,0:T(8,128)(2,1)S(1)}, bf16[64,1024]{1,0:T(8,128)(2,1)S(1)}, u32[]{:S(2)}, u32[]{:S(2)}) collective-permute-start(bf16[64,1024]{1,0:T(8,128)(2,1)S(1)} %shard_map.53), channel_id=1, source_target_pairs={{0,8},{1,2},{2,1},{3,4},{4,3},{5,6},{6,5},{7,15},{8,0},{9,10},{10,... | collective-permute-start | bytes 393224 | tf_op jit(solution)/shard_map/ppermute | solution.py:30
  18.1 2.7 %collective-permute-start.6 = (bf16[64,1024]{1,0:T(8,128)(2,1)S(1)}, bf16[64,1024]{1,0:T(8,128)(2,1)S(1)}, u32[]{:S(2)}, u32[]{:S(2)}) collective-permute-start(bf16[64,1024]{1,0:T(8,128)(2,1)S(1)} %get-tuple-element.93), channel_id=1, source_target_pairs={{0,1},{1,0},{2,3},{3,2},{4,5},{5,4},{6,7},{7,6},{8,9},{9,8},{10,11... | collective-permute-start | bytes 393224 | tf_op jit(solution)/shard_map/ppermute | solution.py:30
  19.6 5.0 %collective-permute-start.7 = (bf16[64,1024]{1,0:T(8,128)(2,1)S(1)}, bf16[64,1024]{1,0:T(8,128)(2,1)S(1)}, u32[]{:S(2)}, u32[]{:S(2)}) collective-permute-start(bf16[64,1024]{1,0:T(8,128)(2,1)S(1)} %shard_map.56), channel_id=1, source_target_pairs={{0,8},{1,2},{2,1},{3,4},{4,3},{5,6},{6,5},{7,15},{8,0},{9,10},{10,... | collective-permute-start | bytes 393224 | tf_op jit(solution)/shard_map/ppermute | solution.py:30
  23.2 2.7 %collective-permute-start.8 = (bf16[64,1024]{1,0:T(8,128)(2,1)S(1)}, bf16[64,1024]{1,0:T(8,128)(2,1)S(1)}, u32[]{:S(2)}, u32[]{:S(2)}) collective-permute-start(bf16[64,1024]{1,0:T(8,128)(2,1)S(1)} %get-tuple-element.99), channel_id=1, source_target_pairs={{0,1},{1,0},{2,3},{3,2},{4,5},{5,4},{6,7},{7,6},{8,9},{9,8},{10,11... | collective-permute-start | bytes 393224 | tf_op jit(solution)/shard_map/ppermute | solution.py:30
  24.7 5.0 %collective-permute-start.9 = (bf16[64,1024]{1,0:T(8,128)(2,1)S(1)}, bf16[64,1024]{1,0:T(8,128)(2,1)S(1)}, u32[]{:S(2)}, u32[]{:S(2)}) collective-permute-start(bf16[64,1024]{1,0:T(8,128)(2,1)S(1)} %shard_map.58), channel_id=1, source_target_pairs={{0,8},{1,2},{2,1},{3,4},{4,3},{5,6},{6,5},{7,15},{8,0},{9,10},{10,... | collective-permute-start | bytes 393224 | tf_op jit(solution)/shard_map/ppermute | solution.py:30
  28.8 2.1 %collective-permute-start.10 = (bf16[64,1024]{1,0:T(8,128)(2,1)S(1)}, bf16[64,1024]{1,0:T(8,128)(2,1)S(1)}, u32[]{:S(2)}, u32[]{:S(2)}) collective-permute-start(bf16[64,1024]{1,0:T(8,128)(2,1)S(1)} %get-tuple-element.105), channel_id=1, source_target_pairs={{0,1},{1,0},{2,3},{3,2},{4,5},{5,4},{6,7},{7,6},{8,9},{9,8},{10,11... | collective-permute-start | bytes 393224 | tf_op jit(solution)/shard_map/ppermute | solution.py:30
  28.9 2.1 %collective-permute-start.11 = (f32[64,64]{1,0:T(8,128)S(1)}, f32[64,64]{1,0:T(8,128)S(1)}, u32[]{:S(2)}, u32[]{:S(2)}) collective-permute-start(f32[64,64]{1,0:T(8,128)S(1)} %get-tuple-element.108.refs_0_), channel_id=1, source_target_pairs={{0,1},{1,0},{2,3},{3,2},{4,5},{5,4},{6,7},{7,6},{8,9},{9,8},{10,11... | collective-permute-start | bytes 49160 | tf_op jit(solution)/shard_map/ppermute | solution.py:49
  29.8 5.5 %collective-permute-start.12 = (bf16[64,1024]{1,0:T(8,128)(2,1)S(1)}, bf16[64,1024]{1,0:T(8,128)(2,1)S(1)}, u32[]{:S(2)}, u32[]{:S(2)}) collective-permute-start(bf16[64,1024]{1,0:T(8,128)(2,1)S(1)} %shard_map.60), channel_id=1, source_target_pairs={{0,8},{1,2},{2,1},{3,4},{4,3},{5,6},{6,5},{7,15},{8,0},{9,10},{10,... | collective-permute-start | bytes 393224 | tf_op jit(solution)/shard_map/ppermute | solution.py:30
  33.4 3.7 %collective-permute-start.13 = (bf16[64,1024]{1,0:T(8,128)(2,1)S(1)}, bf16[64,1024]{1,0:T(8,128)(2,1)S(1)}, u32[]{:S(2)}, u32[]{:S(2)}) collective-permute-start(bf16[64,1024]{1,0:T(8,128)(2,1)S(1)} %get-tuple-element.112), channel_id=1, source_target_pairs={{0,1},{1,0},{2,3},{3,2},{4,5},{5,4},{6,7},{7,6},{8,9},{9,8},{10,11... | collective-permute-start | bytes 393224 | tf_op jit(solution)/shard_map/ppermute | solution.py:30
  33.7 3.3 %collective-permute-start.14 = (f32[64,64]{1,0:T(8,128)S(1)}, f32[64,64]{1,0:T(8,128)S(1)}, u32[]{:S(2)}, u32[]{:S(2)}) collective-permute-start(f32[64,64]{1,0:T(8,128)S(1)} %get-tuple-element.115.refs_0_), channel_id=1, source_target_pairs={{0,3},{1,2},{2,1},{3,0},{4,7},{5,6},{6,5},{7,4},{8,11},{9,10},{10,... | collective-permute-start | bytes 49160 | tf_op jit(solution)/shard_map/ppermute | solution.py:49
  35.3 5.0 %collective-permute-start.16 = (bf16[64,1024]{1,0:T(8,128)(2,1)S(1)}, bf16[64,1024]{1,0:T(8,128)(2,1)S(1)}, u32[]{:S(2)}, u32[]{:S(2)}) collective-permute-start(bf16[64,1024]{1,0:T(8,128)(2,1)S(1)} %shard_map.62), channel_id=1, source_target_pairs={{0,8},{1,2},{2,1},{3,4},{4,3},{5,6},{6,5},{7,15},{8,0},{9,10},{10,... | collective-permute-start | bytes 393224 | tf_op jit(solution)/shard_map/ppermute | solution.py:30
  39.7 4.7 %collective-permute-start.17 = (bf16[64,1024]{1,0:T(8,128)(2,1)S(1)}, bf16[64,1024]{1,0:T(8,128)(2,1)S(1)}, u32[]{:S(2)}, u32[]{:S(2)}) collective-permute-start(bf16[64,1024]{1,0:T(8,128)(2,1)S(1)} %get-tuple-element.120), channel_id=1, source_target_pairs={{0,1},{1,0},{2,3},{3,2},{4,5},{5,4},{6,7},{7,6},{8,9},{9,8},{10,11... | collective-permute-start | bytes 393224 | tf_op jit(solution)/shard_map/ppermute | solution.py:30
  40.4 6.5 %collective-permute-start.18 = (bf16[64,1024]{1,0:T(8,128)(2,1)S(1)}, bf16[64,1024]{1,0:T(8,128)(2,1)S(1)}, u32[]{:S(2)}, u32[]{:S(2)}) collective-permute-start(bf16[64,1024]{1,0:T(8,128)(2,1)S(1)} %shard_map.64), channel_id=1, source_target_pairs={{0,8},{1,2},{2,1},{3,4},{4,3},{5,6},{6,5},{7,15},{8,0},{9,10},{10,... | collective-permute-start | bytes 393224 | tf_op jit(solution)/shard_map/ppermute | solution.py:30
  41.3 5.6 %collective-permute-start.15 = (f32[64,64]{1,0:T(8,128)S(1)}, f32[64,64]{1,0:T(8,128)S(1)}, u32[]{:S(2)}, u32[]{:S(2)}) collective-permute-start(f32[64,64]{1,0:T(8,128)S(1)} %get-tuple-element.116.refs_0_), channel_id=1, source_target_pairs={{0,5},{1,4},{2,7},{3,6},{4,1},{5,0},{6,3},{7,2},{8,13},{9,12},{10,... | collective-permute-start | bytes 49160 | tf_op jit(solution)/shard_map/ppermute | solution.py:49
  47.6 4.8 %collective-permute-start.19 = (bf16[2,16,1024]{2,1,0:T(8,128)(2,1)S(1)}, bf16[2,16,1024]{2,1,0:T(8,128)(2,1)S(1)}, u32[]{:S(2)}, u32[]{:S(2)}) collective-permute-start(bf16[2,16,1024]{2,1,0:T(8,128)(2,1)S(1)} %get-tuple-element.128), channel_id=1, source_target_pairs={{0,24},{8,0},{16,8},{24,16},{1,25},{9,1},{17,9},{25,17},{2,26},{10... | collective-permute-start | bytes 196616 | tf_op jit(solution)/shard_map/ppermute | solution.py:39
  52.8 1.3 %collective-permute-start.20 = (f32[64,96]{1,0:T(8,128)S(1)}, f32[64,96]{1,0:T(8,128)S(1)}, u32[]{:S(2)}, u32[]{:S(2)}) collective-permute-start(f32[64,96]{1,0:T(8,128)S(1)} %shard_map.67), channel_id=1, source_target_pairs={{0,1},{1,0},{2,3},{3,2},{4,5},{5,4},{6,7},{7,6},{8,9},{9,8},{10,11... | collective-permute-start | bytes 73736 | tf_op jit(solution)/shard_map/ppermute | solution.py:49
  54.0 6.2 %collective-permute-start.23 = (f32[64,96]{1,0:T(8,128)S(1)}, f32[64,96]{1,0:T(8,128)S(1)}, u32[]{:S(2)}, u32[]{:S(2)}) collective-permute-start(f32[64,96]{1,0:T(8,128)S(1)} %add.3.refs_0_), channel_id=1, source_target_pairs={{0,7},{1,6},{2,5},{3,4},{4,3},{5,2},{6,1},{7,0},{8,15},{9,14},{10,... | collective-permute-start | bytes 73736 | tf_op jit(solution)/shard_map/ppermute | solution.py:49
  56.1 4.6 %collective-permute-start.22 = (f32[64,96]{1,0:T(8,128)S(1)}, f32[64,96]{1,0:T(8,128)S(1)}, u32[]{:S(2)}, u32[]{:S(2)}) collective-permute-start(f32[64,96]{1,0:T(8,128)S(1)} %add.3.refs_0_), channel_id=1, source_target_pairs={{0,5},{1,4},{2,7},{3,6},{4,1},{5,0},{6,3},{7,2},{8,13},{9,12},{10,... | collective-permute-start | bytes 73736 | tf_op jit(solution)/shard_map/ppermute | solution.py:49
  56.1 4.5 %collective-permute-start.21 = (f32[64,96]{1,0:T(8,128)S(1)}, f32[64,96]{1,0:T(8,128)S(1)}, u32[]{:S(2)}, u32[]{:S(2)}) collective-permute-start(f32[64,96]{1,0:T(8,128)S(1)} %add.3.refs_0_), channel_id=1, source_target_pairs={{0,3},{1,2},{2,1},{3,0},{4,7},{5,6},{6,5},{7,4},{8,11},{9,10},{10,... | collective-permute-start | bytes 73736 | tf_op jit(solution)/shard_map/ppermute | solution.py:49
  63.4 5.2 %collective-permute-start.24 = (bf16[2,16,1024]{2,1,0:T(8,128)(2,1)S(1)}, bf16[2,16,1024]{2,1,0:T(8,128)(2,1)S(1)}, u32[]{:S(2)}, u32[]{:S(2)}) collective-permute-start(bf16[2,16,1024]{2,1,0:T(8,128)(2,1)S(1)} %get-tuple-element.135), channel_id=1, source_target_pairs={{0,8},{8,16},{16,24},{24,0},{1,9},{9,17},{17,25},{25,1},{2,10},{10... | collective-permute-start | bytes 196616 | tf_op jit(solution)/shard_map/ppermute | solution.py:39

commit v5 on v4

--- a/solution.py
+++ b/solution.py
@@ -57,7 +57,8 @@
     while size // reach > 4:
         block = block + swapped(block, reach)
         reach *= 2
-    return [block] + [swapped(block, step) for step in range(reach, size, reach)]
+    steps = sorted(range(reach, size, reach), key=lambda step: (step == size - reach, -step))
+    return [block] + [swapped(block, step) for step in steps]
 
 
 def product(block, matrix):

time: 69.6 us -> 69.5 us (level)
  no operation moved by 1% of the time
where the time goes in v5:
time: 69.5 us; the launch traced here: 69.3 us
  Pallas kernels  32.4 us (47%)
  starting transfers between devices  24.7 us (36%)
  waiting for transfers between devices  11.7 us (17%)
    pallas_call x26, Pallas kernels, call(): pl.pallas_call(kernel, out_shape=outs, in_specs=[HBM if i in far else VME...  32.4 us
    ppermute x16, starting transfers between devices, exchanged(): return lax.ppermute(block, ('cuts', 'layer'), route)  12.1 us
    ppermute x7, starting transfers between devices, swapped(): lax.ppermute(block, 'layer', [(i, i ^ far) for i in range(lax.axis_size('...  9.06 us
    ppermute x2, waiting for transfers between devices, rotated(): lax.ppermute(block, 'cuts', [(i, (i + distance) % size) for i in range(si...  5.05 us
    ppermute x16, waiting for transfers between devices, exchanged(): return lax.ppermute(block, ('cuts', 'layer'), route)  4.45 us
    ppermute x2, starting transfers between devices, rotated(): lax.ppermute(block, 'cuts', [(i, (i + distance) % size) for i in range(si...  3.52 us
    ppermute x7, waiting for transfers between devices, swapped(): lax.ppermute(block, 'layer', [(i, i ^ far) for i in range(lax.axis_size('...  2.21 us
  transfers between devices with their start and end apart: 25, of which 11 were waited for; matrix products, arithmetic and copies ran while one was open for 0% of the time, Pallas kernels for 37%

profile of v5, /device:TPU:0, one launch (start us, length us, event | category | flops | bytes accessed | tf_op | source)
XLA Modules:
  0.0 69.3 jit_solution(14338932512583714061)
XLA Ops:
  0.0 2.4 %shard_map.46 = (f32[64,1024]{1,0:T(8,128)S(1)}, f32[1,64,1024]{2,1,0:T(8,128)S(1)}, bf16[64,1024]{1,0:T(8,128)(2,1)S(1)}, bf16[1,64,1024]{2,1,0:T(8,128)(2,1)S(...) custom-call(s32[1,2]{1,0:T(1,128)} %far_bounds_ref.1, ...), custom_call_target="tpu_custom_call" | custom-call | flops 134217728 | bytes 4718600 | tf_op jit(solution)/shard_map/pallas_call | solution.py:461
  2.4 0.0 copy-start
  2.5 0.5 collective-permute-start
  3.0 2.6 %collective-permute-start.1 = (bf16[64,1024]{1,0:T(8,128)(2,1)S(1)}, bf16[64,1024]{1,0:T(8,128)(2,1)S(1)}, u32[]{:S(2)}, u32[]{:S(2)}) collective-permute-start(bf16[64,1024]{1,0:T(8,128)(2,1)S(1)} %get-tuple-element.82), channel_id=1, source_target_pairs={{0,8},{1,2},{2,1},{3,4},{4,3},{5,6},{6,5},{7,15},{8,0},{9,10},{10,... | collective-permute-start | bytes 393224 | tf_op jit(solution)/shard_map/ppermute | solution.py:30
  5.5 1.4 %shard_map.47 = (bf16[1024,1024]{1,0:T(8,128)(2,1)S(1)}, bf16[2,1,1024,1024]{3,2,1,0:T(8,128)(2,1)S(1)}) custom-call(bf16[1024,1024]{1,0:T(8,128)(2,1)S(1)} %get-tuple-element.76.last_ref, bf16[2,1,1024,1024]{3,2,1,0:T(8,128)(2,1)S(1)} %get-tuple-element.77.mids_in_ref), custom_call_target="tpu_custom_call", output_to_operand_aliasing={{1}: (1, {})} | custom-call | flops 134217728 | bytes 6291456 | tf_op jit(solution)/shard_map/pallas_call | solution.py:461
  6.9 0.0 collective-permute-done.arrived_ref
  7.0 2.4 %shard_map.48 = (f32[64,1024]{1,0:T(8,128)S(1)}, f32[1,64,1024]{2,1,0:T(8,128)S(1)}, bf16[1,64,1024]{2,1,0:T(8,128)(2,1)S(1)}, bf16[64,1024]{1,0:T(8,128)(2,1)S(1)}) custom-call(f32[8,1024]{1,0:T(8,128)S(1)} %get-tuple-element.71.rows_ref, f32[64,1024]{1,0:T(8,128)S(1)} %get-tuple-element.72.outer_a_ref.outer_before_ref, ...), custom_call_target="tpu_custom_call" | custom-call | flops 1342177280 | bytes 14057472 | tf_op jit(solution)/shard_map/pallas_call | solution.py:461
  9.3 0.1 collective-permute-start.2
  9.4 0.0 collective-permute-done.1.outer_b_ref.arrived_ref
  9.4 0.1 shard_map.50
  9.5 1.1 %collective-permute-start.3 = (bf16[64,1024]{1,0:T(8,128)(2,1)S(1)}, bf16[64,1024]{1,0:T(8,128)(2,1)S(1)}, u32[]{:S(2)}, u32[]{:S(2)}) collective-permute-start(bf16[64,1024]{1,0:T(8,128)(2,1)S(1)} %shard_map.50), channel_id=1, source_target_pairs={{0,8},{1,2},{2,1},{3,4},{4,3},{5,6},{6,5},{7,15},{8,0},{9,10},{10,... | collective-permute-start | bytes 393224 | tf_op jit(solution)/shard_map/ppermute | solution.py:30
  10.6 0.1 collective-permute-done.2.arrived_ref
  10.7 2.4 %shard_map.49 = (f32[64,1024]{1,0:T(8,128)S(1)}, f32[1,64,1024]{2,1,0:T(8,128)S(1)}, f32[64,1024]{1,0:T(8,128)S(1)}, bf16[1,64,1024]{2,1,0:T(8,128)(2,1)S(1)}, bf16[64,1024]{1,0:T(8,128)(2,1)S(1)}) custom-call(f32[8,1024]{1,0:T(8,128)S(1)} %get-tuple-element.71.rows_ref, f32[64,1024]{1,0:T(8,128)S(1)} %get-tuple-element.81.outer_a_ref.base_ref, ...), custom_call_target="tpu_custom_call" | custom-call | flops 1342177280 | bytes 14057472 | tf_op jit(solution)/shard_map/pallas_call | solution.py:461
  13.1 0.1 collective-permute-start.4
  13.2 1.3 %collective-permute-done.3.outer_b_ref.arrived_ref = bf16[64,1024]{1,0:T(8,128)(2,1)S(1)} collective-permute-done((bf16[64,1024]{1,0:T(8,128)(2,1)S(1)}, bf16[64,1024]{1,0:T(8,128)(2,1)S(1)}, u32[]{:S(2)}, u32[]{:S(2)}) %collective-permute-start.3) | collective-permute-done | bytes 131104 | tf_op jit(solution)/shard_map/ppermute | solution.py:30
  14.6 1.1 %collective-permute-start.5 = (bf16[64,1024]{1,0:T(8,128)(2,1)S(1)}, bf16[64,1024]{1,0:T(8,128)(2,1)S(1)}, u32[]{:S(2)}, u32[]{:S(2)}) collective-permute-start(bf16[64,1024]{1,0:T(8,128)(2,1)S(1)} %shard_map.53), channel_id=1, source_target_pairs={{0,8},{1,2},{2,1},{3,4},{4,3},{5,6},{6,5},{7,15},{8,0},{9,10},{10,... | collective-permute-start | bytes 393224 | tf_op jit(solution)/shard_map/ppermute | solution.py:30
  15.7 0.0 collective-permute-done.4.arrived_ref
  15.7 2.4 %shard_map.51 = (f32[64,1024]{1,0:T(8,128)S(1)}, f32[1,64,1024]{2,1,0:T(8,128)S(1)}, f32[64,1024]{1,0:T(8,128)S(1)}, bf16[1,64,1024]{2,1,0:T(8,128)(2,1)S(1)}, b...) custom-call(f32[8,1024]{1,0:T(8,128)S(1)} %get-tuple-element.71.rows_ref, ...), custom_call_target="tpu_custom_call" | custom-call | flops 1342177280 | bytes 14057472 | tf_op jit(solution)/shard_map/pallas_call | solution.py:461
  18.1 0.4 collective-permute-start.6
  18.5 1.1 %collective-permute-done.5.outer_b_ref.arrived_ref = bf16[64,1024]{1,0:T(8,128)(2,1)S(1)} collective-permute-done((bf16[64,1024]{1,0:T(8,128)(2,1)S(1)}, bf16[64,1024]{1,0:T(8,128)(2,1)S(1)}, u32[]{:S(2)}, u32[]{:S(2)}) %collective-permute-start.5) | collective-permute-done | bytes 131104 | tf_op jit(solution)/shard_map/ppermute | solution.py:30
  19.6 1.1 %collective-permute-start.7 = (bf16[64,1024]{1,0:T(8,128)(2,1)S(1)}, bf16[64,1024]{1,0:T(8,128)(2,1)S(1)}, u32[]{:S(2)}, u32[]{:S(2)}) collective-permute-start(bf16[64,1024]{1,0:T(8,128)(2,1)S(1)} %shard_map.56), channel_id=1, source_target_pairs={{0,8},{1,2},{2,1},{3,4},{4,3},{5,6},{6,5},{7,15},{8,0},{9,10},{10,... | collective-permute-start | bytes 393224 | tf_op jit(solution)/shard_map/ppermute | solution.py:30
  20.8 2.4 %shard_map.54 = (f32[64,1024]{1,0:T(8,128)S(1)}, f32[1,64,1024]{2,1,0:T(8,128)S(1)}, f32[64,1024]{1,0:T(8,128)S(1)}, bf16[1,64,1024]{2,1,0:T(8,128)(2,1)S(1)}, b...) custom-call(f32[8,1024]{1,0:T(8,128)S(1)} %get-tuple-element.71.rows_ref, ...), custom_call_target="tpu_custom_call" | custom-call | flops 1342177280 | bytes 14057472 | tf_op jit(solution)/shard_map/pallas_call | solution.py:461
  23.2 0.2 collective-permute-start.8
  23.4 1.2 %collective-permute-done.7.outer_b_ref.arrived_ref = bf16[64,1024]{1,0:T(8,128)(2,1)S(1)} collective-permute-done((bf16[64,1024]{1,0:T(8,128)(2,1)S(1)}, bf16[64,1024]{1,0:T(8,128)(2,1)S(1)}, u32[]{:S(2)}, u32[]{:S(2)}) %collective-permute-start.7) | collective-permute-done | bytes 131104 | tf_op jit(solution)/shard_map/ppermute | solution.py:30
  24.7 1.1 %collective-permute-start.9 = (bf16[64,1024]{1,0:T(8,128)(2,1)S(1)}, bf16[64,1024]{1,0:T(8,128)(2,1)S(1)}, u32[]{:S(2)}, u32[]{:S(2)}) collective-permute-start(bf16[64,1024]{1,0:T(8,128)(2,1)S(1)} %shard_map.58), channel_id=1, source_target_pairs={{0,8},{1,2},{2,1},{3,4},{4,3},{5,6},{6,5},{7,15},{8,0},{9,10},{10,... | collective-permute-start | bytes 393224 | tf_op jit(solution)/shard_map/ppermute | solution.py:30
  25.9 0.0 collective-permute-done.8.arrived_ref
  25.9 2.9 %shard_map.57 = (f32[64,1024]{1,0:T(8,128)S(1)}, f32[1,64,1024]{2,1,0:T(8,128)S(1)}, f32[64,1024]{1,0:T(8,128)S(1)}, bf16[1,64,1024]{2,1,0:T(8,128)(2,1)S(1)}, b...) custom-call(f32[8,1024]{1,0:T(8,128)S(1)} %get-tuple-element.71.rows_ref, ...), custom_call_target="tpu_custom_call" | custom-call | flops 1342177280 | bytes 14057472 | tf_op jit(solution)/shard_map/pallas_call | solution.py:461
  28.8 0.1 collective-permute-start.10
  28.9 0.5 collective-permute-start.11
  29.4 0.4 collective-permute-done.9.outer_b_ref.arrived_ref
  29.8 1.1 %collective-permute-start.12 = (bf16[64,1024]{1,0:T(8,128)(2,1)S(1)}, bf16[64,1024]{1,0:T(8,128)(2,1)S(1)}, u32[]{:S(2)}, u32[]{:S(2)}) collective-permute-start(bf16[64,1024]{1,0:T(8,128)(2,1)S(1)} %shard_map.60), channel_id=1, source_target_pairs={{0,8},{1,2},{2,1},{3,4},{4,3},{5,6},{6,5},{7,15},{8,0},{9,10},{10,... | collective-permute-start | bytes 393224 | tf_op jit(solution)/shard_map/ppermute | solution.py:30
  30.9 0.0 collective-permute-done.11.refs_1_
  30.9 0.0 collective-permute-done.10.arrived_ref
  30.9 2.4 %shard_map.59 = (f32[64,1024]{1,0:T(8,128)S(1)}, f32[1,64,1024]{2,1,0:T(8,128)S(1)}, f32[64,1024]{1,0:T(8,128)S(1)}, bf16[1,64,1024]{2,1,0:T(8,128)(2,1)S(1)}, b...) custom-call(f32[8,1024]{1,0:T(8,128)S(1)} %get-tuple-element.71.rows_ref, ...), custom_call_target="tpu_custom_call" | custom-call | flops 1342177280 | bytes 14090240 | tf_op jit(solution)/shard_map/pallas_call | solution.py:461
  33.4 0.3 collective-permute-start.13
  33.7 1.6 %collective-permute-start.14 = (f32[64,64]{1,0:T(8,128)S(1)}, f32[64,64]{1,0:T(8,128)S(1)}, u32[]{:S(2)}, u32[]{:S(2)}) collective-permute-start(f32[64,64]{1,0:T(8,128)S(1)} %get-tuple-element.115.refs_0_), channel_id=1, source_target_pairs={{0,3},{1,2},{2,1},{3,0},{4,7},{5,6},{6,5},{7,4},{8,11},{9,10},{10,... | collective-permute-start | bytes 49160 | tf_op jit(solution)/shard_map/ppermute | solution.py:49
  35.3 0.0 collective-permute-done.12.outer_b_ref.arrived_ref
  35.3 0.9 %collective-permute-start.16 = (bf16[64,1024]{1,0:T(8,128)(2,1)S(1)}, bf16[64,1024]{1,0:T(8,128)(2,1)S(1)}, u32[]{:S(2)}, u32[]{:S(2)}) collective-permute-start(bf16[64,1024]{1,0:T(8,128)(2,1)S(1)} %shard_map.62), channel_id=1, source_target_pairs={{0,8},{1,2},{2,1},{3,4},{4,3},{5,6},{6,5},{7,15},{8,0},{9,10},{10,... | collective-permute-start | bytes 393224 | tf_op jit(solution)/shard_map/ppermute | solution.py:30
  36.2 0.8 %collective-permute-done.14.refs_1_ = f32[64,64]{1,0:T(8,128)S(1)} collective-permute-done((f32[64,64]{1,0:T(8,128)S(1)}, f32[64,64]{1,0:T(8,128)S(1)}, u32[]{:S(2)}, u32[]{:S(2)}) %collective-permute-start.14) | collective-permute-done | bytes 16416 | tf_op jit(solution)/shard_map/ppermute | solution.py:49
  37.1 2.6 %shard_map.61 = (f32[64,1024]{1,0:T(8,128)S(1)}, f32[1,64,1024]{2,1,0:T(8,128)S(1)}, f32[64,1024]{1,0:T(8,128)S(1)}, bf16[1,64,1024]{2,1,0:T(8,128)(2,1)S(1)}, b...) custom-call(f32[8,1024]{1,0:T(8,128)S(1)} %get-tuple-element.71.rows_ref, ...), custom_call_target="tpu_custom_call" | custom-call | flops 1342177280 | bytes 14090240 | tf_op jit(solution)/shard_map/pallas_call | solution.py:461
  39.7 0.3 collective-permute-start.17
  40.0 0.3 collective-permute-done.16.outer_b_ref.arrived_ref
  40.4 0.9 %collective-permute-start.18 = (bf16[64,1024]{1,0:T(8,128)(2,1)S(1)}, bf16[64,1024]{1,0:T(8,128)(2,1)S(1)}, u32[]{:S(2)}, u32[]{:S(2)}) collective-permute-start(bf16[64,1024]{1,0:T(8,128)(2,1)S(1)} %shard_map.64), channel_id=1, source_target_pairs={{0,8},{1,2},{2,1},{3,4},{4,3},{5,6},{6,5},{7,15},{8,0},{9,10},{10,... | collective-permute-start | bytes 393224 | tf_op jit(solution)/shard_map/ppermute | solution.py:30
  41.3 3.1 %collective-permute-start.15 = (f32[64,64]{1,0:T(8,128)S(1)}, f32[64,64]{1,0:T(8,128)S(1)}, u32[]{:S(2)}, u32[]{:S(2)}) collective-permute-start(f32[64,64]{1,0:T(8,128)S(1)} %get-tuple-element.116.refs_0_), channel_id=1, source_target_pairs={{0,5},{1,4},{2,7},{3,6},{4,1},{5,0},{6,3},{7,2},{8,13},{9,12},{10,... | collective-permute-start | bytes 49160 | tf_op jit(solution)/shard_map/ppermute | solution.py:49
  44.4 2.5 %shard_map.63 = (f32[64,1024]{1,0:T(8,128)S(1)}, f32[1,64,1024]{2,1,0:T(8,128)S(1)}, f32[64,1024]{1,0:T(8,128)}) custom-call(f32[8,1024]{1,0:T(8,128)S(1)} %get-tuple-element.71.rows_ref, f32[64,1024]{1,0:T(8,128)S(1)} %get-tuple-element.117.outer_a_ref.base_ref, bf16[64,1024]{1,0:T(8,128)(2,1)S(1)} %collective-permute-done.16.outer_b_ref.arrived_ref, ...), custom_call_target="tpu_custom_call" | custom-call | flops 1342177280 | bytes 14057472 | tf_op jit(solution)/shard_map/pallas_call | solution.py:461
  46.9 0.0 collective-permute-done.18.arrived_ref
  47.0 0.7 shard_map.66
  47.6 1.7 %collective-permute-start.19 = (bf16[2,16,1024]{2,1,0:T(8,128)(2,1)S(1)}, bf16[2,16,1024]{2,1,0:T(8,128)(2,1)S(1)}, u32[]{:S(2)}, u32[]{:S(2)}) collective-permute-start(bf16[2,16,1024]{2,1,0:T(8,128)(2,1)S(1)} %get-tuple-element.128), channel_id=1, source_target_pairs={{0,24},{8,0},{16,8},{24,16},{1,25},{9,1},{17,9},{25,17},{2,26},{10... | collective-permute-start | bytes 196616 | tf_op jit(solution)/shard_map/ppermute | solution.py:39
  49.4 3.1 %collective-permute-done.19.above_ref = bf16[2,16,1024]{2,1,0:T(8,128)(2,1)S(1)} collective-permute-done((bf16[2,16,1024]{2,1,0:T(8,128)(2,1)S(1)}, bf16[2,16,1024]{2,1,0:T(8,128)(2,1)S(1)}, u32[]{:S(2)}, u32[]{:S(2)}) %collective-permute-start.19) | collective-permute-done | bytes 65568 | tf_op jit(solution)/shard_map/ppermute | solution.py:39
  52.5 0.3 shard_map.67
  52.8 0.1 collective-permute-start.20
  52.8 1.2 %collective-permute-done.20 = f32[64,96]{1,0:T(8,128)S(1)} collective-permute-done((f32[64,96]{1,0:T(8,128)S(1)}, f32[64,96]{1,0:T(8,128)S(1)}, u32[]{:S(2)}, u32[]{:S(2)}) %collective-permute-start.20) | collective-permute-done | bytes 24608 | tf_op jit(solution)/shard_map/ppermute | solution.py:49
  54.0 2.0 %collective-permute-start.23 = (f32[64,96]{1,0:T(8,128)S(1)}, f32[64,96]{1,0:T(8,128)S(1)}, u32[]{:S(2)}, u32[]{:S(2)}) collective-permute-start(f32[64,96]{1,0:T(8,128)S(1)} %add.3.refs_0_), channel_id=1, source_target_pairs={{0,7},{1,6},{2,5},{3,4},{4,3},{5,2},{6,1},{7,0},{8,15},{9,14},{10,... | collective-permute-start | bytes 73736 | tf_op jit(solution)/shard_map/ppermute | solution.py:49
  56.1 0.0 collective-permute-start.22
  56.1 1.8 %collective-permute-start.21 = (f32[64,96]{1,0:T(8,128)S(1)}, f32[64,96]{1,0:T(8,128)S(1)}, u32[]{:S(2)}, u32[]{:S(2)}) collective-permute-start(f32[64,96]{1,0:T(8,128)S(1)} %add.3.refs_0_), channel_id=1, source_target_pairs={{0,5},{1,4},{2,7},{3,6},{4,1},{5,0},{6,3},{7,2},{8,13},{9,12},{10,... | collective-permute-start | bytes 73736 | tf_op jit(solution)/shard_map/ppermute | solution.py:49
  57.9 2.3 %shard_map.68 = (f32[64,64]{1,0:T(8,128)S(1)}, f32[2,64,1024]{2,1,0:T(8,128)S(1)}) custom-call(f32[64,64]{1,0:T(8,128)S(1)} %get-tuple-element.116.refs_0_, f32[64,64]{1,0:T(8,128)S(1)} %collective-permute-done.15.refs_1_, f32[2,64,1024]{2,1,0:T(8,128)S(1)} %get-tuple-element.129.refs_2_), custom_call_target="tpu_custom_call" | custom-call | flops 134217728 | bytes 557056 | tf_op jit(solution)/shard_map/pallas_call | solution.py:461
  60.2 0.0 collective-permute-done.23.refs_3_
  60.2 0.2 collective-permute-done.22.refs_2_
  60.4 0.0 collective-permute-done.21.refs_1_
  60.4 2.7 %shard_map.69 = (f32[64,64]{1,0:T(8,128)S(1)}, f32[16,16]{1,0:T(8,128)S(1)}, bf16[2,16,1024]{2,1,0:T(8,128)(2,1)S(1)}) custom-call(f32[64,96]{1,0:T(8,128)S(1)} %add.3.refs_0_, f32[64,96]{1,0:T(8,128)S(1)} %collective-permute-done.21.refs_1_, f32[64,96]{1,0:T(8,128)S(1)} %collective-permute-done.22.refs_2_, f32[64,96]{1,0:T(8,128)S(1)} %collective-permute-done.23.refs_3_, ...), custom_call_target="tpu_custom_call" | custom-call | flops 134217728 | bytes 638976 | tf_op jit(solution)/shard_map/pallas_call | solution.py:461
  63.1 1.8 %collective-permute-start.24 = (bf16[2,16,1024]{2,1,0:T(8,128)(2,1)S(1)}, bf16[2,16,1024]{2,1,0:T(8,128)(2,1)S(1)}, u32[]{:S(2)}, u32[]{:S(2)}) collective-permute-start(bf16[2,16,1024]{2,1,0:T(8,128)(2,1)S(1)} %get-tuple-element.135), channel_id=1, source_target_pairs={{0,8},{8,16},{16,24},{24,0},{1,9},{9,17},{17,25},{25,1},{2,10},{10... | collective-permute-start | bytes 196616 | tf_op jit(solution)/shard_map/ppermute | solution.py:39
  64.9 1.6 %shard_map.70 = (f32[2,16,1024]{2,1,0:T(8,128)S(1)}, f32[64,2,1024]{2,1,0:T(2,128)}) custom-call(f32[64,64]{1,0:T(8,128)S(1)} %get-tuple-element.132.inverse_ref, f32[16,16]{1,0:T(8,128)S(1)} %get-tuple-element.133.weights_ref, f32[2,64,1024]{2,1,0:T(8,128)S(1)} %get-tuple-element.131.refs_5_.first_ref, ...), custom_call_target="tpu_custom_call" | custom-call | flops 134217728 | bytes 607232 | tf_op jit(solution)/shard_map/pallas_call | solution.py:461
  66.5 2.0 %collective-permute-done.24.below_ref = bf16[2,16,1024]{2,1,0:T(8,128)(2,1)S(1)} collective-permute-done((bf16[2,16,1024]{2,1,0:T(8,128)(2,1)S(1)}, bf16[2,16,1024]{2,1,0:T(8,128)(2,1)S(1)}, u32[]{:S(2)}, u32[]{:S(2)}) %collective-permute-start.24) | collective-permute-done | bytes 65568 | tf_op jit(solution)/shard_map/ppermute | solution.py:39
  68.4 0.7 %shard_map.71 = f32[64,2,1024]{2,1,0:T(2,128)} custom-call(f32[2,16,1024]{2,1,0:T(8,128)S(1)} %get-tuple-element.134.low_ref, bf16[2,16,1024]{2,1,0:T(8,128)(2,1)S(1)} %collective-permute-done.24.below_ref, f32[64,2,1024]{2,1,0:T(2,128)} %get-tuple-element.136._), custom_call_target="tpu_custom_call", output_to_operand_aliasing={{}: (2, {})} | custom-call | flops 134217728 | bytes 720896 | tf_op jit(solution)/shard_map/pallas_call | solution.py:461
  (15 shorter events, 0.3 us)
Async XLA Ops:
  2.4 4.5 %copy-start = (bf16[2,1024,1024]{2,1,0:T(8,128)(2,1)S(1)}, bf16[2,1024,1024]{2,1,0:T(8,128)(2,1)}, u32[]{:S(2)}) copy-start(bf16[2,1024,1024]{2,1,0:T(8,128)(2,1)} %diag_ref.15) | copy-start | bytes 12582916
  2.5 4.5 %collective-permute-start = (bf16[64,1024]{1,0:T(8,128)(2,1)S(1)}, bf16[64,1024]{1,0:T(8,128)(2,1)S(1)}, u32[]{:S(2)}, u32[]{:S(2)}) collective-permute-start(bf16[64,1024]{1,0:T(8,128)(2,1)S(1)} %get-tuple-element.75), channel_id=1, source_target_pairs={{0,1},{1,0},{2,3},{3,2},{4,5},{5,4},{6,7},{7,6},{8,9},{9,8},{10,11... | collective-permute-start | bytes 393224 | tf_op jit(solution)/shard_map/ppermute | solution.py:30
  3.0 6.4 %collective-permute-start.1 = (bf16[64,1024]{1,0:T(8,128)(2,1)S(1)}, bf16[64,1024]{1,0:T(8,128)(2,1)S(1)}, u32[]{:S(2)}, u32[]{:S(2)}) collective-permute-start(bf16[64,1024]{1,0:T(8,128)(2,1)S(1)} %get-tuple-element.82), channel_id=1, source_target_pairs={{0,8},{1,2},{2,1},{3,4},{4,3},{5,6},{6,5},{7,15},{8,0},{9,10},{10,... | collective-permute-start | bytes 393224 | tf_op jit(solution)/shard_map/ppermute | solution.py:30
  9.3 1.4 %collective-permute-start.2 = (bf16[64,1024]{1,0:T(8,128)(2,1)S(1)}, bf16[64,1024]{1,0:T(8,128)(2,1)S(1)}, u32[]{:S(2)}, u32[]{:S(2)}) collective-permute-start(bf16[64,1024]{1,0:T(8,128)(2,1)S(1)} %get-tuple-element.84), channel_id=1, source_target_pairs={{0,1},{1,0},{2,3},{3,2},{4,5},{5,4},{6,7},{7,6},{8,9},{9,8},{10,11... | collective-permute-start | bytes 393224 | tf_op jit(solution)/shard_map/ppermute | solution.py:30
  9.5 5.0 %collective-permute-start.3 = (bf16[64,1024]{1,0:T(8,128)(2,1)S(1)}, bf16[64,1024]{1,0:T(8,128)(2,1)S(1)}, u32[]{:S(2)}, u32[]{:S(2)}) collective-permute-start(bf16[64,1024]{1,0:T(8,128)(2,1)S(1)} %shard_map.50), channel_id=1, source_target_pairs={{0,8},{1,2},{2,1},{3,4},{4,3},{5,6},{6,5},{7,15},{8,0},{9,10},{10,... | collective-permute-start | bytes 393224 | tf_op jit(solution)/shard_map/ppermute | solution.py:30
  13.1 2.6 %collective-permute-start.4 = (bf16[64,1024]{1,0:T(8,128)(2,1)S(1)}, bf16[64,1024]{1,0:T(8,128)(2,1)S(1)}, u32[]{:S(2)}, u32[]{:S(2)}) collective-permute-start(bf16[64,1024]{1,0:T(8,128)(2,1)S(1)} %get-tuple-element.88), channel_id=1, source_target_pairs={{0,1},{1,0},{2,3},{3,2},{4,5},{5,4},{6,7},{7,6},{8,9},{9,8},{10,11... | collective-permute-start | bytes 393224 | tf_op jit(solution)/shard_map/ppermute | solution.py:30
  14.6 5.0 %collective-permute-start.5 = (bf16[64,1024]{1,0:T(8,128)(2,1)S(1)}, bf16[64,1024]{1,0:T(8,128)(2,1)S(1)}, u32[]{:S(2)}, u32[]{:S(2)}) collective-permute-start(bf16[64,1024]{1,0:T(8,128)(2,1)S(1)} %shard_map.53), channel_id=1, source_target_pairs={{0,8},{1,2},{2,1},{3,4},{4,3},{5,6},{6,5},{7,15},{8,0},{9,10},{10,... | collective-permute-start | bytes 393224 | tf_op jit(solution)/shard_map/ppermute | solution.py:30
  18.1 2.7 %collective-permute-start.6 = (bf16[64,1024]{1,0:T(8,128)(2,1)S(1)}, bf16[64,1024]{1,0:T(8,128)(2,1)S(1)}, u32[]{:S(2)}, u32[]{:S(2)}) collective-permute-start(bf16[64,1024]{1,0:T(8,128)(2,1)S(1)} %get-tuple-element.93), channel_id=1, source_target_pairs={{0,1},{1,0},{2,3},{3,2},{4,5},{5,4},{6,7},{7,6},{8,9},{9,8},{10,11... | collective-permute-start | bytes 393224 | tf_op jit(solution)/shard_map/ppermute | solution.py:30
  19.6 5.0 %collective-permute-start.7 = (bf16[64,1024]{1,0:T(8,128)(2,1)S(1)}, bf16[64,1024]{1,0:T(8,128)(2,1)S(1)}, u32[]{:S(2)}, u32[]{:S(2)}) collective-permute-start(bf16[64,1024]{1,0:T(8,128)(2,1)S(1)} %shard_map.56), channel_id=1, source_target_pairs={{0,8},{1,2},{2,1},{3,4},{4,3},{5,6},{6,5},{7,15},{8,0},{9,10},{10,... | collective-permute-start | bytes 393224 | tf_op jit(solution)/shard_map/ppermute | solution.py:30
  23.2 2.7 %collective-permute-start.8 = (bf16[64,1024]{1,0:T(8,128)(2,1)S(1)}, bf16[64,1024]{1,0:T(8,128)(2,1)S(1)}, u32[]{:S(2)}, u32[]{:S(2)}) collective-permute-start(bf16[64,1024]{1,0:T(8,128)(2,1)S(1)} %get-tuple-element.99), channel_id=1, source_target_pairs={{0,1},{1,0},{2,3},{3,2},{4,5},{5,4},{6,7},{7,6},{8,9},{9,8},{10,11... | collective-permute-start | bytes 393224 | tf_op jit(solution)/shard_map/ppermute | solution.py:30
  24.7 5.0 %collective-permute-start.9 = (bf16[64,1024]{1,0:T(8,128)(2,1)S(1)}, bf16[64,1024]{1,0:T(8,128)(2,1)S(1)}, u32[]{:S(2)}, u32[]{:S(2)}) collective-permute-start(bf16[64,1024]{1,0:T(8,128)(2,1)S(1)} %shard_map.58), channel_id=1, source_target_pairs={{0,8},{1,2},{2,1},{3,4},{4,3},{5,6},{6,5},{7,15},{8,0},{9,10},{10,... | collective-permute-start | bytes 393224 | tf_op jit(solution)/shard_map/ppermute | solution.py:30
  28.8 2.1 %collective-permute-start.10 = (bf16[64,1024]{1,0:T(8,128)(2,1)S(1)}, bf16[64,1024]{1,0:T(8,128)(2,1)S(1)}, u32[]{:S(2)}, u32[]{:S(2)}) collective-permute-start(bf16[64,1024]{1,0:T(8,128)(2,1)S(1)} %get-tuple-element.105), channel_id=1, source_target_pairs={{0,1},{1,0},{2,3},{3,2},{4,5},{5,4},{6,7},{7,6},{8,9},{9,8},{10,11... | collective-permute-start | bytes 393224 | tf_op jit(solution)/shard_map/ppermute | solution.py:30
  28.9 2.1 %collective-permute-start.11 = (f32[64,64]{1,0:T(8,128)S(1)}, f32[64,64]{1,0:T(8,128)S(1)}, u32[]{:S(2)}, u32[]{:S(2)}) collective-permute-start(f32[64,64]{1,0:T(8,128)S(1)} %get-tuple-element.108.refs_0_), channel_id=1, source_target_pairs={{0,1},{1,0},{2,3},{3,2},{4,5},{5,4},{6,7},{7,6},{8,9},{9,8},{10,11... | collective-permute-start | bytes 49160 | tf_op jit(solution)/shard_map/ppermute | solution.py:49
  29.8 5.5 %collective-permute-start.12 = (bf16[64,1024]{1,0:T(8,128)(2,1)S(1)}, bf16[64,1024]{1,0:T(8,128)(2,1)S(1)}, u32[]{:S(2)}, u32[]{:S(2)}) collective-permute-start(bf16[64,1024]{1,0:T(8,128)(2,1)S(1)} %shard_map.60), channel_id=1, source_target_pairs={{0,8},{1,2},{2,1},{3,4},{4,3},{5,6},{6,5},{7,15},{8,0},{9,10},{10,... | collective-permute-start | bytes 393224 | tf_op jit(solution)/shard_map/ppermute | solution.py:30
  33.4 3.7 %collective-permute-start.13 = (bf16[64,1024]{1,0:T(8,128)(2,1)S(1)}, bf16[64,1024]{1,0:T(8,128)(2,1)S(1)}, u32[]{:S(2)}, u32[]{:S(2)}) collective-permute-start(bf16[64,1024]{1,0:T(8,128)(2,1)S(1)} %get-tuple-element.112), channel_id=1, source_target_pairs={{0,1},{1,0},{2,3},{3,2},{4,5},{5,4},{6,7},{7,6},{8,9},{9,8},{10,11... | collective-permute-start | bytes 393224 | tf_op jit(solution)/shard_map/ppermute | solution.py:30
  33.7 3.3 %collective-permute-start.14 = (f32[64,64]{1,0:T(8,128)S(1)}, f32[64,64]{1,0:T(8,128)S(1)}, u32[]{:S(2)}, u32[]{:S(2)}) collective-permute-start(f32[64,64]{1,0:T(8,128)S(1)} %get-tuple-element.115.refs_0_), channel_id=1, source_target_pairs={{0,3},{1,2},{2,1},{3,0},{4,7},{5,6},{6,5},{7,4},{8,11},{9,10},{10,... | collective-permute-start | bytes 49160 | tf_op jit(solution)/shard_map/ppermute | solution.py:49
  35.3 5.0 %collective-permute-start.16 = (bf16[64,1024]{1,0:T(8,128)(2,1)S(1)}, bf16[64,1024]{1,0:T(8,128)(2,1)S(1)}, u32[]{:S(2)}, u32[]{:S(2)}) collective-permute-start(bf16[64,1024]{1,0:T(8,128)(2,1)S(1)} %shard_map.62), channel_id=1, source_target_pairs={{0,8},{1,2},{2,1},{3,4},{4,3},{5,6},{6,5},{7,15},{8,0},{9,10},{10,... | collective-permute-start | bytes 393224 | tf_op jit(solution)/shard_map/ppermute | solution.py:30
  39.7 4.7 %collective-permute-start.17 = (bf16[64,1024]{1,0:T(8,128)(2,1)S(1)}, bf16[64,1024]{1,0:T(8,128)(2,1)S(1)}, u32[]{:S(2)}, u32[]{:S(2)}) collective-permute-start(bf16[64,1024]{1,0:T(8,128)(2,1)S(1)} %get-tuple-element.120), channel_id=1, source_target_pairs={{0,1},{1,0},{2,3},{3,2},{4,5},{5,4},{6,7},{7,6},{8,9},{9,8},{10,11... | collective-permute-start | bytes 393224 | tf_op jit(solution)/shard_map/ppermute | solution.py:30
  40.4 6.5 %collective-permute-start.18 = (bf16[64,1024]{1,0:T(8,128)(2,1)S(1)}, bf16[64,1024]{1,0:T(8,128)(2,1)S(1)}, u32[]{:S(2)}, u32[]{:S(2)}) collective-permute-start(bf16[64,1024]{1,0:T(8,128)(2,1)S(1)} %shard_map.64), channel_id=1, source_target_pairs={{0,8},{1,2},{2,1},{3,4},{4,3},{5,6},{6,5},{7,15},{8,0},{9,10},{10,... | collective-permute-start | bytes 393224 | tf_op jit(solution)/shard_map/ppermute | solution.py:30
  41.3 5.6 %collective-permute-start.15 = (f32[64,64]{1,0:T(8,128)S(1)}, f32[64,64]{1,0:T(8,128)S(1)}, u32[]{:S(2)}, u32[]{:S(2)}) collective-permute-start(f32[64,64]{1,0:T(8,128)S(1)} %get-tuple-element.116.refs_0_), channel_id=1, source_target_pairs={{0,5},{1,4},{2,7},{3,6},{4,1},{5,0},{6,3},{7,2},{8,13},{9,12},{10,... | collective-permute-start | bytes 49160 | tf_op jit(solution)/shard_map/ppermute | solution.py:49
  47.6 4.8 %collective-permute-start.19 = (bf16[2,16,1024]{2,1,0:T(8,128)(2,1)S(1)}, bf16[2,16,1024]{2,1,0:T(8,128)(2,1)S(1)}, u32[]{:S(2)}, u32[]{:S(2)}) collective-permute-start(bf16[2,16,1024]{2,1,0:T(8,128)(2,1)S(1)} %get-tuple-element.128), channel_id=1, source_target_pairs={{0,24},{8,0},{16,8},{24,16},{1,25},{9,1},{17,9},{25,17},{2,26},{10... | collective-permute-start | bytes 196616 | tf_op jit(solution)/shard_map/ppermute | solution.py:39
  52.8 1.3 %collective-permute-start.20 = (f32[64,96]{1,0:T(8,128)S(1)}, f32[64,96]{1,0:T(8,128)S(1)}, u32[]{:S(2)}, u32[]{:S(2)}) collective-permute-start(f32[64,96]{1,0:T(8,128)S(1)} %shard_map.67), channel_id=1, source_target_pairs={{0,1},{1,0},{2,3},{3,2},{4,5},{5,4},{6,7},{7,6},{8,9},{9,8},{10,11... | collective-permute-start | bytes 73736 | tf_op jit(solution)/shard_map/ppermute | solution.py:49
  54.0 6.2 %collective-permute-start.23 = (f32[64,96]{1,0:T(8,128)S(1)}, f32[64,96]{1,0:T(8,128)S(1)}, u32[]{:S(2)}, u32[]{:S(2)}) collective-permute-start(f32[64,96]{1,0:T(8,128)S(1)} %add.3.refs_0_), channel_id=1, source_target_pairs={{0,7},{1,6},{2,5},{3,4},{4,3},{5,2},{6,1},{7,0},{8,15},{9,14},{10,... | collective-permute-start | bytes 73736 | tf_op jit(solution)/shard_map/ppermute | solution.py:49
  56.1 4.3 %collective-permute-start.22 = (f32[64,96]{1,0:T(8,128)S(1)}, f32[64,96]{1,0:T(8,128)S(1)}, u32[]{:S(2)}, u32[]{:S(2)}) collective-permute-start(f32[64,96]{1,0:T(8,128)S(1)} %add.3.refs_0_), channel_id=1, source_target_pairs={{0,3},{1,2},{2,1},{3,0},{4,7},{5,6},{6,5},{7,4},{8,11},{9,10},{10,... | collective-permute-start | bytes 73736 | tf_op jit(solution)/shard_map/ppermute | solution.py:49
  56.1 4.3 %collective-permute-start.21 = (f32[64,96]{1,0:T(8,128)S(1)}, f32[64,96]{1,0:T(8,128)S(1)}, u32[]{:S(2)}, u32[]{:S(2)}) collective-permute-start(f32[64,96]{1,0:T(8,128)S(1)} %add.3.refs_0_), channel_id=1, source_target_pairs={{0,5},{1,4},{2,7},{3,6},{4,1},{5,0},{6,3},{7,2},{8,13},{9,12},{10,... | collective-permute-start | bytes 73736 | tf_op jit(solution)/shard_map/ppermute | solution.py:49
  63.1 5.3 %collective-permute-start.24 = (bf16[2,16,1024]{2,1,0:T(8,128)(2,1)S(1)}, bf16[2,16,1024]{2,1,0:T(8,128)(2,1)S(1)}, u32[]{:S(2)}, u32[]{:S(2)}) collective-permute-start(bf16[2,16,1024]{2,1,0:T(8,128)(2,1)S(1)} %get-tuple-element.135), channel_id=1, source_target_pairs={{0,8},{8,16},{16,24},{24,0},{1,9},{9,17},{17,25},{25,1},{2,10},{10... | collective-permute-start | bytes 196616 | tf_op jit(solution)/shard_map/ppermute | solution.py:39
